TPU v7x, 512 devices: a whole 4x4x16 slice. The times are simulated.
512 devices in a mesh: tok: 64 (over y, z_lo, core), slab: 8 (over z_hi, x).
Axes of the slice: x: 4, y: 4, z: 16 (z_hi: 2, z_lo: 8; z = z_hi * 8 + z_lo), core: 2. Of those that a mesh axis runs over, the one named last changes fastest.
Arguments:
- activations: bfloat16 [32768, 32, 256], P('tok', 'slab'), may hold values from -40 to 40, as said below
- block_map: int32 [8, 16, 2], P('slab'), may hold values from -1 to 31, as said below
Outputs:
- hessian_blocks: float32 [8, 4096, 256], P('slab', 'tok')
Inputs may be any that keep to these rules, and one draw needn't show every extreme that they name: `block_map`: each slot holds either (i, j) with 0 <= i <= j < 32 and j among slab s's blocks s * 4 to s * 4 + 3, or (-1, -1) for an empty slot; empty slots come after the live ones; no block appears twice; the last slab has all 16 slots live. `activations`: values of order one.
All inputs are finite; a program needn't handle non-finite values.
Results may differ from a plain program's by a relative error of at most 0.0003.
Values may be sent and summed in bfloat16 or wider, within the bound.
No kernel may reach another device: no remote copies, remote signals or barrier semaphores. Data moves between devices by JAX's collectives and lax.ppermute only.
A program may use at most 64 MiB of HBM per device.

v0:
```python
import jax
import jax.numpy as jnp
from jax import lax
from jax.sharding import PartitionSpec as P


def body(activations, block_map):
    tok_rows, local_blocks, width = activations.shape
    slab_id = lax.axis_index("slab")
    slots = block_map[0]
    live = slots[:, 0] >= 0
    local_col = slots[:, 1] - slab_id * local_blocks
    col_pick = (local_col[:, None] == jnp.arange(local_blocks, dtype=jnp.int32)[None, :]) & live[
        :, None
    ]
    right_side = jnp.einsum(
        "tcb,kc->tkb",
        activations,
        col_pick.astype(jnp.bfloat16),
        preferred_element_type=jnp.bfloat16,
    )
    piece = lax.all_gather(activations, "slab", axis=1, tiled=True)
    count = piece.shape[1]
    row_pick = (slots[:, 0][:, None] == jnp.arange(count, dtype=jnp.int32)[None, :]) & live[:, None]
    chosen = jnp.einsum(
        "tcb,kc->tkb", piece, row_pick.astype(jnp.bfloat16), preferred_element_type=jnp.bfloat16
    )
    total_tokens = tok_rows * lax.axis_size("tok")
    scale = 2.0 / total_tokens
    slot_count = slots.shape[0]
    terms = jnp.einsum("tkb,tkc->kbc", chosen, right_side, preferred_element_type=jnp.float32)
    terms = terms.reshape(slot_count * width, width)
    summed = lax.psum_scatter(terms, "tok", scatter_dimension=0, tiled=True)
    return (summed * scale)[None, :, :]


def solution(mesh):
    return jax.shard_map(
        body,
        mesh=mesh,
        in_specs=(P("tok", "slab", None), P("slab", None, None)),
        out_specs=P("slab", "tok", None),
        check_vma=False,
    )
```

profile of v0, /device:TPU:6, one launch (start us, length us, event | category | flops | bytes accessed | tf_op | source)
XLA Modules:
  0.0 784.9 jit_solution(14966938430581989593)
XLA Ops:
  6.5 0.0 all-gather.2.cloned.1.call-start
  6.5 2.4 copy.3
  8.9 0.0 all-gather.2.cloned.1.call-update
  9.0 0.0 reduce-scatter.2.cloned.1.call-start
  9.0 0.7 compare_bitcast_fusion
  9.7 0.8 subtract_bitcast_fusion
  10.5 4.5 fusion.11
  14.9 286.1 %all-gather.2.cloned.1.call-done = bf16[512,32,256]{2,0,1:T(8,128)(2,1)} async-done(((bf16[512,4,256]{2,0,1:T(8,128)(2,1)}), bf16[512,32,256]{2,0,1:T(8,128)(2,1)}) %all-gather.2.cloned.1.call-update) | async-done | bytes 8388624 | tf_op jit(solution)/shard_map/all_gather | solution.py:22
  301.1 10.0 %fusion = bf16[16,512,256]{2,0,1:T(8,128)(2,1)} fusion(bf16[512,32,256]{2,0,1:T(8,128)(2,1)} %all-gather.2.cloned.1.call-done, s32[16]{0:T(128)S(1)} %get-tuple-element.6, pred[16]{0:T(512)(128)(4,1)S(1)} %compare_bitcast_fusion), kind=kOutput, calls=%fused_computation | convolution fusion | flops 134218752 | bytes 12582992 | tf_op jit(solution)/shard_map/tcb,kc->tkb/dot_general | solution.py:25
  311.1 7.5 copy.5
  318.6 7.2 fusion.2
  325.8 0.0 reduce-scatter.2.cloned.1.call-update
  325.8 450.8 %reduce-scatter.2.cloned.1.call-done = f32[64,256]{1,0:T(8,128)} async-done(((f32[4096,256]{1,0:T(8,128)}), f32[64,256]{1,0:T(8,128)}) %reduce-scatter.2.cloned.1.call-update) | async-done | bytes 65552 | tf_op jit(solution)/shard_map/reduce_scatter | solution.py:33
  776.6 1.5 multiply_bitcast_fusion
Async XLA Ops:
  6.5 294.5 %all-gather.2.cloned.1.call-start = ((), (), s32[]{:S(2)}) async-start(), calls=%async_computation.1 | async-start | bytes 9437184 | tf_op jit(solution)/shard_map/all_gather | solution.py:22
  9.0 767.7 %reduce-scatter.2.cloned.1.call-start = ((), (), s32[]{:S(2)}) async-start(), calls=%async_computation.2 | async-start | bytes 4259840 | tf_op jit(solution)/shard_map/reduce_scatter | solution.py:33
Sparse Core Ops, SparseCore 0:
  10.6 290.4 all-gather.1
  325.9 450.6 reduce-scatter.1
where the time goes:
time: 785 us
  waiting for transfers between devices  737 us (94%)
  matrix products  21.6 us (3%)
  between operations  13.4 us (2%)
  local copies, waits for them, and re-layouts  9.93 us (1%)
    reduce_scatter x1, waiting for transfers between devices, body(): summed = lax.psum_scatter(terms, 'tok', scatter_dimension=0, tiled=True)  451 us
    all_gather x1, waiting for transfers between devices, body(): piece = lax.all_gather(activations, 'slab', axis=1, tiled=True)  286 us
  transfers between devices with their start and end apart: 2, of which 2 were waited for; matrix products, arithmetic and copies ran while one was open for 1% of the time, Pallas kernels for 0%

commit v1 on v0

v1 whole, which is shorter than its diff:
```python
import jax
import jax.numpy as jnp
from jax import lax
from jax.experimental import pallas as pl
from jax.experimental.pallas import tpu as pltpu
from jax.sharding import Mesh, PartitionSpec as P

NY, NZ, NC, NH, NX = 4, 8, 2, 2, 4
WAVES = 2


def shift_x(v, d, upper_only=False):
    halves = (1,) if upper_only else (0, 1)
    pairs = [(h * NX + i, h * NX + (i - d) % NX) for h in halves for i in range(NX)]
    return lax.ppermute(v, ("zh", "x"), pairs)


def products_kernel(meta, *refs):
    n = 4 + 4 * WAVES
    sources, (keep, send, rows, row_sems, own, own_sem) = refs[:n], refs[n:]
    slots = rows.shape[0]
    y, zl, core = meta[0], meta[1], meta[2]
    own_copy = pltpu.make_async_copy(sources[0], own, own_sem)
    own_copy.start()

    def fetch(k, _):
        for b in range(n):

            @pl.when(meta[8 + k] == b)
            def _():
                pltpu.make_async_copy(
                    sources[b].at[meta[24 + k]], rows.at[k], row_sems.at[k]
                ).start()

        return 0

    lax.fori_loop(0, slots, fetch, 0)
    own_copy.wait()

    def one(k, _):
        pltpu.make_async_copy(sources[0].at[0], rows.at[k], row_sems.at[k]).wait()
        product = lax.dot_general(
            rows[k],
            own[meta[40 + k]],
            (((0,), (0,)), ((), ())),
            preferred_element_type=jnp.float32,
        )
        product = jnp.where(meta[56 + k] > 0, product, 0.0)
        group = lax.rem(k // 4 - y + NY, NY)
        for half in range(2):
            e = (lax.rem(k, 4) * 2 + half) ^ zl
            place = ((e & 1) << 2) | (e & 2) | (e >> 2)
            at = pl.ds(pl.multiple_of((group * 8 + place) * 64, 64), 64)
            first = product[half * 128 : half * 128 + 64]
            second = product[half * 128 + 64 : half * 128 + 128]
            keep[at, :] = jnp.where(core == 0, first, second)
            send[at, :] = jnp.where(core == 0, second, first)
        return 0

    lax.fori_loop(0, slots, one, 0)


def products(meta, sources, slots, tokens, width):
    half = slots * width // 2
    return pl.pallas_call(
        products_kernel,
        out_shape=[jax.ShapeDtypeStruct((half, width), jnp.float32)] * 2,
        in_specs=[pl.BlockSpec(memory_space=pltpu.SMEM)]
        + [pl.BlockSpec(memory_space=pl.ANY)] * len(sources),
        out_specs=[pl.BlockSpec(memory_space=pltpu.VMEM)] * 2,
        scratch_shapes=[
            pltpu.VMEM((slots, tokens, width), jnp.bfloat16),
            pltpu.SemaphoreType.DMA((slots,)),
            pltpu.VMEM((4, tokens, width), jnp.bfloat16),
            pltpu.SemaphoreType.DMA,
        ],
        compiler_params=pltpu.CompilerParams(vmem_limit_bytes=24 << 20),
        cost_estimate=pl.CostEstimate(
            flops=2 * slots * tokens * width * width,
            bytes_accessed=12 << 20,
            transcendentals=0,
        ),
    )(meta, *sources)


def body(activations, block_map):
    tokens, blocks, width = activations.shape
    y, zl, core = (lax.axis_index(a) for a in ("y", "zl", "core"))
    zh, x = lax.axis_index("zh"), lax.axis_index("x")
    slots = block_map[0]
    count = slots.shape[0]
    row, col = slots[:, 0], slots[:, 1]
    live = row >= 0
    slab, place = jnp.maximum(row, 0) // blocks, jnp.maximum(row, 0) % blocks
    step = (slab - x) % NX
    same = slab // NX == zh
    per = blocks // WAVES
    buffer = jnp.where(live, jnp.where(same, step, 4 + place // per * 4 + step), 0)
    inside = jnp.where(live, jnp.where(same, place, place % per), 0)
    local = jnp.where(live, col - (zh * NX + x) * blocks, 0)
    where = jnp.stack([y, zl, core, zh, x, zh, zh, zh]).astype(jnp.int32)
    meta = jnp.concatenate([where, buffer, inside, local, live.astype(jnp.int32)])

    own = jnp.transpose(activations, (1, 0, 2))
    waves = []
    for w in range(WAVES):
        waves.append(lax.ppermute(own[w * per : w * per + per], "zh", [(0, 1)]))
    sources = [own] + [shift_x(own, d) for d in (1, 2, 3)]
    for low in waves:
        sources += [low] + [shift_x(low, d, True) for d in (1, 2, 3)]

    keep, send = products(meta, sources, count, tokens, width)
    total = keep + lax.ppermute(send, "core", [(0, 1), (1, 0)])
    part = total.shape[0] // NY
    mine = total[:part]
    for d in (1, 2, 3):
        mine = mine + lax.ppermute(
            total[d * part : d * part + part], "y", [(i, (i + d) % NY) for i in range(NY)]
        )
    for bit in (1, 2, 4):
        half = mine.shape[0] // 2
        mine = mine[:half] + lax.ppermute(mine[half:], "zl", [(i, i ^ bit) for i in range(NZ)])
    scale = 2.0 / (tokens * NY * NZ * NC)
    return (mine * scale)[None]


def solution(mesh):
    grid = Mesh(mesh.devices.reshape(NY, NZ, NC, NH, NX), ("y", "zl", "core", "zh", "x"))
    tok, slab = ("y", "zl", "core"), ("zh", "x")
    return jax.shard_map(
        body,
        mesh=grid,
        in_specs=(P(tok, slab, None), P(slab, None, None)),
        out_specs=P(slab, tok, None),
        check_vma=False,
    )
```

time: 785 us -> 272 us (0.35)
  the two profiles are of different devices: /device:TPU:6 before, /device:TPU:490 now
where the time goes in v1:
time: 272 us; the launch traced here: 271 us
  starting transfers between devices  136 us (50%)
  waiting for transfers between devices  116 us (43%)
  local copies, waits for them, and re-layouts  10.9 us (4%)
  Pallas kernels  6.79 us (2%)
    ppermute x3, starting transfers between devices, body(): lax.ppermute(mine[half:], 'zl', [(i, i ^ bit) for i in range(NZ)])  77.1 us
    ppermute x9, waiting for transfers between devices, shift_x(): return lax.ppermute(v, ('zh', 'x'), pairs)  47.7 us
    ppermute x9, starting transfers between devices, shift_x(): return lax.ppermute(v, ('zh', 'x'), pairs)  44.7 us
    ppermute x2, waiting for transfers between devices, body(): waves.append(lax.ppermute(own[w * per:w * per + per], 'zh', [(0, 1)]))  23.1 us
    ppermute x3, waiting for transfers between devices, body(): lax.ppermute(total[d * part:d * part + part], 'y', [(i, (i + d) % NY) for...  21 us
    ppermute x3, waiting for transfers between devices, body(): lax.ppermute(mine[half:], 'zl', [(i, i ^ bit) for i in range(NZ)])  19.7 us
    unnamed x23, local copies, waits for them, and re-layouts  10.6 us
    ppermute x3, starting transfers between devices, body(): lax.ppermute(total[d * part:d * part + part], 'y', [(i, (i + d) % NY) for...  10 us
  transfers between devices with their start and end apart: 18, of which 11 were waited for; matrix products, arithmetic and copies ran while one was open for 0% of the time, Pallas kernels for 0%

profile of v1, /device:TPU:490, one launch (start us, length us, event | category | flops | bytes accessed | tf_op | source)
XLA Modules:
  0.0 271.0 jit_solution(12186234620576954148)
XLA Ops:
  0.0 0.0 copy-start.10
  0.0 1.4 copy.5
  1.4 0.1 fusion.7
  1.5 1.3 collective-permute-start.7
  2.8 1.3 collective-permute-start.3
  4.1 23.1 %collective-permute-done.7.refs_8_ = bf16[2,512,256]{2,1,0:T(8,128)(2,1)S(1)} collective-permute-done((bf16[2,512,256]{2,1,0:T(8,128)(2,1)S(1)}, bf16[2,512,256]{2,1,0:T(8,128)(2,1)S(1)}, u32[]{:S(2)}, u32[]{:S(2)}) %collective-permute-start.7) | collective-permute-done | bytes 524320 | tf_op jit(solution)/shard_map/ppermute | solution.py:107
  27.2 3.4 %collective-permute-start.10 = (bf16[2,512,256]{2,1,0:T(8,128)(2,1)S(1)}, bf16[2,512,256]{2,1,0:T(8,128)(2,1)S(1)}, u32[]{:S(2)}, u32[]{:S(2)}) collective-permute-start(bf16[2,512,256]{2,1,0:T(8,128)(2,1)S(1)} %collective-permute-done.7.refs_8_), channel_id=1, source_target_pairs={{4,5},{5,6},{6,7},{7,4},{12,13},{13,14},{14,15},{15,12},{20,21},{2... | collective-permute-start | bytes 1572872 | tf_op jit(solution)/shard_map/ppermute | solution.py:15
  30.6 3.0 %collective-permute-start.9 = (bf16[2,512,256]{2,1,0:T(8,128)(2,1)S(1)}, bf16[2,512,256]{2,1,0:T(8,128)(2,1)S(1)}, u32[]{:S(2)}, u32[]{:S(2)}) collective-permute-start(bf16[2,512,256]{2,1,0:T(8,128)(2,1)S(1)} %collective-permute-done.7.refs_8_), channel_id=1, source_target_pairs={{4,6},{5,7},{6,4},{7,5},{12,14},{13,15},{14,12},{15,13},{20,22},{2... | collective-permute-start | bytes 1572872 | tf_op jit(solution)/shard_map/ppermute | solution.py:15
  33.6 4.1 %collective-permute-start.8 = (bf16[2,512,256]{2,1,0:T(8,128)(2,1)S(1)}, bf16[2,512,256]{2,1,0:T(8,128)(2,1)S(1)}, u32[]{:S(2)}, u32[]{:S(2)}) collective-permute-start(bf16[2,512,256]{2,1,0:T(8,128)(2,1)S(1)} %collective-permute-done.7.refs_8_), channel_id=1, source_target_pairs={{4,7},{5,4},{6,5},{7,6},{12,15},{13,12},{14,13},{15,14},{20,23},{2... | collective-permute-start | bytes 1572872 | tf_op jit(solution)/shard_map/ppermute | solution.py:15
  37.7 0.0 copy-start
  37.7 0.8 copy-done
  38.5 0.0 collective-permute-done.3.refs_4_
  38.5 2.3 collective-permute-start.6
  40.8 3.1 %collective-permute-start.2 = (bf16[4,512,256]{2,1,0:T(8,128)(2,1)S(1)}, bf16[4,512,256]{2,1,0:T(8,128)(2,1)S(1)}, u32[]{:S(2)}, u32[]{:S(2)}) collective-permute-start(bf16[4,512,256]{2,1,0:T(8,128)(2,1)S(1)} %bitcast.47), channel_id=1, source_target_pairs={{0,1},{1,2},{2,3},{3,0},{4,5},{5,6},{6,7},{7,4},{8,9},{9,10},{10,1... | collective-permute-start | bytes 3145736 | tf_op jit(solution)/shard_map/ppermute | solution.py:15
  43.9 5.8 %collective-permute-done.10.refs_11_ = bf16[2,512,256]{2,1,0:T(8,128)(2,1)S(1)} collective-permute-done((bf16[2,512,256]{2,1,0:T(8,128)(2,1)S(1)}, bf16[2,512,256]{2,1,0:T(8,128)(2,1)S(1)}, u32[]{:S(2)}, u32[]{:S(2)}) %collective-permute-start.10) | collective-permute-done | bytes 524320 | tf_op jit(solution)/shard_map/ppermute | solution.py:15
  49.7 0.0 copy-start.2
  49.7 0.8 copy-done.2
  50.5 1.9 collective-permute-start.1
  52.4 0.0 collective-permute-done.9.refs_10_
  52.4 0.0 copy-start.4
  52.5 0.8 copy-done.4
  53.2 7.4 %collective-permute-start = (bf16[4,512,256]{2,1,0:T(8,128)(2,1)S(1)}, bf16[4,512,256]{2,1,0:T(8,128)(2,1)}, u32[]{:S(2)}, u32[]{:S(2)}) collective-permute-start(bf16[4,512,256]{2,1,0:T(8,128)(2,1)S(1)} %bitcast.49), channel_id=1, source_target_pairs={{0,3},{1,0},{2,1},{3,2},{4,7},{5,4},{6,5},{7,6},{8,11},{9,8},{10,9... | collective-permute-start | bytes 3145736 | tf_op jit(solution)/shard_map/ppermute | solution.py:15
  60.6 0.0 collective-permute-done.8.refs_9_
  60.7 0.0 copy-start.6
  60.7 0.8 copy-done.6
  61.5 17.6 %collective-permute-start.5 = (bf16[2,512,256]{2,1,0:T(8,128)(2,1)}, bf16[2,512,256]{2,1,0:T(8,128)(2,1)}, u32[]{:S(2)}, u32[]{:S(2)}) collective-permute-start(bf16[2,512,256]{2,1,0:T(8,128)(2,1)} %collective-permute-done.3.refs_4_), channel_id=1, source_target_pairs={{4,6},{5,7},{6,4},{7,5},{12,14},{13,15},{14,12},{15,13},{20,22},{2... | collective-permute-start | bytes 1572872 | tf_op jit(solution)/shard_map/ppermute | solution.py:15
  79.1 0.0 collective-permute-done.6.refs_7_
  79.1 0.0 copy-start.8
  79.1 0.8 copy-done.8
  79.9 1.9 collective-permute-start.4
  81.8 0.0 copy-done.10
  81.9 0.1 concatenate.3.meta
  82.0 34.5 %collective-permute-done.5.refs_6_ = bf16[2,512,256]{2,1,0:T(8,128)(2,1)} collective-permute-done((bf16[2,512,256]{2,1,0:T(8,128)(2,1)}, bf16[2,512,256]{2,1,0:T(8,128)(2,1)}, u32[]{:S(2)}, u32[]{:S(2)}) %collective-permute-start.5) | collective-permute-done | bytes 524320 | tf_op jit(solution)/shard_map/ppermute | solution.py:15
  116.4 7.4 %collective-permute-done.4.refs_5_ = bf16[2,512,256]{2,1,0:T(8,128)(2,1)} collective-permute-done((bf16[2,512,256]{2,1,0:T(8,128)(2,1)}, bf16[2,512,256]{2,1,0:T(8,128)(2,1)}, u32[]{:S(2)}, u32[]{:S(2)}) %collective-permute-start.4) | collective-permute-done | bytes 524320 | tf_op jit(solution)/shard_map/ppermute | solution.py:15
  123.8 0.0 collective-permute-done.2.refs_3_
  123.8 0.0 collective-permute-done.1.refs_2_
  123.8 0.0 collective-permute-done.refs_1_
  123.8 0.0 copy-start.1
  123.8 1.0 copy-done.1
  124.9 0.0 copy-start.3
  124.9 1.0 copy-done.3
  125.9 0.0 copy-start.5
  125.9 1.0 copy-done.5
  126.9 1.0 copy-done.7
  128.0 1.0 copy-done.9
  129.0 6.8 %shard_map.28 = (f32[2048,256]{1,0:T(8,128)S(1)}, f32[2048,256]{1,0:T(8,128)S(1)}) custom-call(s32[72]{0:T(128)S(1)} %concatenate.3.meta, bf16[4,512,256]{2,1,0:T(8,128)(2,1)S(1)} %bitcast.50, bf16[4,512,256]{2,1,0:T(8,128)(2,1)} %collective-permute-done.refs_1_, bf16[4,512,256]{2,1,0:T(8,128)(2,1)S(1)} %collective-permute-done.1.refs_2_, ...), custom_call_target="tpu_custom_call" | custom-call | flops 1073741824 | bytes 12582912 | tf_op jit(solution)/shard_map/pallas_call | solution.py:65
  135.8 1.9 collective-permute-start.11
  137.7 4.1 %collective-permute-done.11 = f32[2048,256]{1,0:T(8,128)S(1)} collective-permute-done((f32[2048,256]{1,0:T(8,128)S(1)}, f32[2048,256]{1,0:T(8,128)S(1)}, u32[]{:S(2)}, u32[]{:S(2)}) %collective-permute-start.11) | collective-permute-done | bytes 2097184 | tf_op jit(solution)/shard_map/ppermute | solution.py:113
  141.9 0.3 add.53
  142.1 0.1 fusion.6
  142.3 3.5 %collective-permute-start.12 = (f32[512,256]{1,0:T(8,128)S(1)}, f32[512,256]{1,0:T(8,128)S(1)}, u32[]{:S(2)}, u32[]{:S(2)}) collective-permute-start(f32[512,256]{1,0:T(8,128)S(1)} %get-tuple-element.11), channel_id=1, source_target_pairs={{0,128},{128,256},{256,384},{384,0},{1,129},{129,257},{257,385},{3... | collective-permute-start | bytes 1572872 | tf_op jit(solution)/shard_map/ppermute | solution.py:117
  145.7 2.4 collective-permute-start.14
  148.1 4.2 %collective-permute-start.13 = (f32[512,256]{1,0:T(8,128)S(1)}, f32[512,256]{1,0:T(8,128)S(1)}, u32[]{:S(2)}, u32[]{:S(2)}) collective-permute-start(f32[512,256]{1,0:T(8,128)S(1)} %get-tuple-element.13), channel_id=1, source_target_pairs={{0,256},{128,384},{256,0},{384,128},{1,257},{129,385},{257,1},{385... | collective-permute-start | bytes 1572872 | tf_op jit(solution)/shard_map/ppermute | solution.py:117
  152.3 6.6 %collective-permute-done.12 = f32[512,256]{1,0:T(8,128)S(1)} collective-permute-done((f32[512,256]{1,0:T(8,128)S(1)}, f32[512,256]{1,0:T(8,128)S(1)}, u32[]{:S(2)}, u32[]{:S(2)}) %collective-permute-start.12) | collective-permute-done | bytes 524320 | tf_op jit(solution)/shard_map/ppermute | solution.py:117
  158.9 2.8 %collective-permute-done.14 = f32[512,256]{1,0:T(8,128)S(1)} collective-permute-done((f32[512,256]{1,0:T(8,128)S(1)}, f32[512,256]{1,0:T(8,128)S(1)}, u32[]{:S(2)}, u32[]{:S(2)}) %collective-permute-start.14) | collective-permute-done | bytes 524320 | tf_op jit(solution)/shard_map/ppermute | solution.py:117
  161.7 11.6 %collective-permute-done.13 = f32[512,256]{1,0:T(8,128)S(1)} collective-permute-done((f32[512,256]{1,0:T(8,128)S(1)}, f32[512,256]{1,0:T(8,128)S(1)}, u32[]{:S(2)}, u32[]{:S(2)}) %collective-permute-start.13) | collective-permute-done | bytes 524320 | tf_op jit(solution)/shard_map/ppermute | solution.py:117
  173.3 0.2 fusion.1
  173.5 70.5 %collective-permute-start.15 = (f32[256,256]{1,0:T(8,128)S(1)}, f32[256,256]{1,0:T(8,128)S(1)}, u32[]{:S(2)}, u32[]{:S(2)}) collective-permute-start(f32[256,256]{1,0:T(8,128)S(1)} %slice.63), channel_id=1, source_target_pairs={{0,16},{16,0},{32,48},{48,32},{64,80},{80,64},{96,112},{112,96},{1... | collective-permute-start | bytes 786440 | tf_op jit(solution)/shard_map/ppermute | solution.py:122
  244.0 5.4 %collective-permute-done.15 = f32[256,256]{1,0:T(8,128)S(1)} collective-permute-done((f32[256,256]{1,0:T(8,128)S(1)}, f32[256,256]{1,0:T(8,128)S(1)}, u32[]{:S(2)}, u32[]{:S(2)}) %collective-permute-start.15) | collective-permute-done | bytes 262176 | tf_op jit(solution)/shard_map/ppermute | solution.py:122
  249.5 1.9 collective-permute-start.16
  251.4 7.4 %collective-permute-done.16 = f32[128,256]{1,0:T(8,128)S(1)} collective-permute-done((f32[128,256]{1,0:T(8,128)S(1)}, f32[128,256]{1,0:T(8,128)S(1)}, u32[]{:S(2)}, u32[]{:S(2)}) %collective-permute-start.16) | collective-permute-done | bytes 131104 | tf_op jit(solution)/shard_map/ppermute | solution.py:122
  258.8 4.7 %collective-permute-start.17 = (f32[64,256]{1,0:T(8,128)S(1)}, f32[64,256]{1,0:T(8,128)S(1)}, u32[]{:S(2)}, u32[]{:S(2)}) collective-permute-start(f32[64,256]{1,0:T(8,128)S(1)} %slice.67), channel_id=1, source_target_pairs={{0,64},{16,80},{32,96},{48,112},{64,0},{80,16},{96,32},{112,48},{1... | collective-permute-start | bytes 196616 | tf_op jit(solution)/shard_map/ppermute | solution.py:122
  263.5 6.8 %collective-permute-done.17 = f32[64,256]{1,0:T(8,128)S(1)} collective-permute-done((f32[64,256]{1,0:T(8,128)S(1)}, f32[64,256]{1,0:T(8,128)S(1)}, u32[]{:S(2)}, u32[]{:S(2)}) %collective-permute-start.17) | collective-permute-done | bytes 65568 | tf_op jit(solution)/shard_map/ppermute | solution.py:122
  270.4 0.6 fusion.3
  (10 shorter events, 0.1 us)
Async XLA Ops:
  0.0 81.8 %copy-start.10 = (s32[1,16,2]{1,2,0:T(2,128)S(1)}, s32[1,16,2]{1,2,0:T(2,128)}, u32[]{:S(2)}) copy-start(s32[1,16,2]{1,2,0:T(2,128)} %param.3) | copy-start | bytes 388
  1.5 25.7 %collective-permute-start.7 = (bf16[2,512,256]{2,1,0:T(8,128)(2,1)S(1)}, bf16[2,512,256]{2,1,0:T(8,128)(2,1)S(1)}, u32[]{:S(2)}, u32[]{:S(2)}) collective-permute-start(bf16[2,512,256]{2,1,0:T(8,128)(2,1)S(1)} %get-tuple-element.14), channel_id=1, source_target_pairs={{0,4},{1,5},{2,6},{3,7},{8,12},{9,13},{10,14},{11,15},{16,20},{17,... | collective-permute-start | bytes 1572872 | tf_op jit(solution)/shard_map/ppermute | solution.py:107
  2.8 35.7 %collective-permute-start.3 = (bf16[2,512,256]{2,1,0:T(8,128)(2,1)S(1)}, bf16[2,512,256]{2,1,0:T(8,128)(2,1)}, u32[]{:S(2)}, u32[]{:S(2)}) collective-permute-start(bf16[2,512,256]{2,1,0:T(8,128)(2,1)S(1)} %get-tuple-element.15), channel_id=1, source_target_pairs={{0,4},{1,5},{2,6},{3,7},{8,12},{9,13},{10,14},{11,15},{16,20},{17,... | collective-permute-start | bytes 1572872 | tf_op jit(solution)/shard_map/ppermute | solution.py:107
  27.2 22.5 %collective-permute-start.10 = (bf16[2,512,256]{2,1,0:T(8,128)(2,1)S(1)}, bf16[2,512,256]{2,1,0:T(8,128)(2,1)S(1)}, u32[]{:S(2)}, u32[]{:S(2)}) collective-permute-start(bf16[2,512,256]{2,1,0:T(8,128)(2,1)S(1)} %collective-permute-done.7.refs_8_), channel_id=1, source_target_pairs={{4,5},{5,6},{6,7},{7,4},{12,13},{13,14},{14,15},{15,12},{20,21},{2... | collective-permute-start | bytes 1572872 | tf_op jit(solution)/shard_map/ppermute | solution.py:15
  30.6 21.9 %collective-permute-start.9 = (bf16[2,512,256]{2,1,0:T(8,128)(2,1)S(1)}, bf16[2,512,256]{2,1,0:T(8,128)(2,1)S(1)}, u32[]{:S(2)}, u32[]{:S(2)}) collective-permute-start(bf16[2,512,256]{2,1,0:T(8,128)(2,1)S(1)} %collective-permute-done.7.refs_8_), channel_id=1, source_target_pairs={{4,6},{5,7},{6,4},{7,5},{12,14},{13,15},{14,12},{15,13},{20,22},{2... | collective-permute-start | bytes 1572872 | tf_op jit(solution)/shard_map/ppermute | solution.py:15
  33.6 27.0 %collective-permute-start.8 = (bf16[2,512,256]{2,1,0:T(8,128)(2,1)S(1)}, bf16[2,512,256]{2,1,0:T(8,128)(2,1)S(1)}, u32[]{:S(2)}, u32[]{:S(2)}) collective-permute-start(bf16[2,512,256]{2,1,0:T(8,128)(2,1)S(1)} %collective-permute-done.7.refs_8_), channel_id=1, source_target_pairs={{4,7},{5,4},{6,5},{7,6},{12,15},{13,12},{14,13},{15,14},{20,23},{2... | collective-permute-start | bytes 1572872 | tf_op jit(solution)/shard_map/ppermute | solution.py:15
  37.7 0.8 copy-start
  38.5 40.6 %collective-permute-start.6 = (bf16[2,512,256]{2,1,0:T(8,128)(2,1)}, bf16[2,512,256]{2,1,0:T(8,128)(2,1)S(1)}, u32[]{:S(2)}, u32[]{:S(2)}) collective-permute-start(bf16[2,512,256]{2,1,0:T(8,128)(2,1)} %collective-permute-done.3.refs_4_), channel_id=1, source_target_pairs={{4,5},{5,6},{6,7},{7,4},{12,13},{13,14},{14,15},{15,12},{20,21},{2... | collective-permute-start | bytes 1572872 | tf_op jit(solution)/shard_map/ppermute | solution.py:15
  40.8 83.0 %collective-permute-start.2 = (bf16[4,512,256]{2,1,0:T(8,128)(2,1)S(1)}, bf16[4,512,256]{2,1,0:T(8,128)(2,1)S(1)}, u32[]{:S(2)}, u32[]{:S(2)}) collective-permute-start(bf16[4,512,256]{2,1,0:T(8,128)(2,1)S(1)} %bitcast.47), channel_id=1, source_target_pairs={{0,1},{1,2},{2,3},{3,0},{4,5},{5,6},{6,7},{7,4},{8,9},{9,10},{10,1... | collective-permute-start | bytes 3145736 | tf_op jit(solution)/shard_map/ppermute | solution.py:15
  49.7 0.8 copy-start.2
  50.5 73.3 %collective-permute-start.1 = (bf16[4,512,256]{2,1,0:T(8,128)(2,1)S(1)}, bf16[4,512,256]{2,1,0:T(8,128)(2,1)S(1)}, u32[]{:S(2)}, u32[]{:S(2)}) collective-permute-start(bf16[4,512,256]{2,1,0:T(8,128)(2,1)S(1)} %bitcast.48), channel_id=1, source_target_pairs={{0,2},{1,3},{2,0},{3,1},{4,6},{5,7},{6,4},{7,5},{8,10},{9,11},{10,... | collective-permute-start | bytes 3145736 | tf_op jit(solution)/shard_map/ppermute | solution.py:15
  52.4 0.8 copy-start.4
  53.2 70.6 %collective-permute-start = (bf16[4,512,256]{2,1,0:T(8,128)(2,1)S(1)}, bf16[4,512,256]{2,1,0:T(8,128)(2,1)}, u32[]{:S(2)}, u32[]{:S(2)}) collective-permute-start(bf16[4,512,256]{2,1,0:T(8,128)(2,1)S(1)} %bitcast.49), channel_id=1, source_target_pairs={{0,3},{1,0},{2,1},{3,2},{4,7},{5,4},{6,5},{7,6},{8,11},{9,8},{10,9... | collective-permute-start | bytes 3145736 | tf_op jit(solution)/shard_map/ppermute | solution.py:15
  60.7 0.8 copy-start.6
  61.5 55.0 %collective-permute-start.5 = (bf16[2,512,256]{2,1,0:T(8,128)(2,1)}, bf16[2,512,256]{2,1,0:T(8,128)(2,1)}, u32[]{:S(2)}, u32[]{:S(2)}) collective-permute-start(bf16[2,512,256]{2,1,0:T(8,128)(2,1)} %collective-permute-done.3.refs_4_), channel_id=1, source_target_pairs={{4,6},{5,7},{6,4},{7,5},{12,14},{13,15},{14,12},{15,13},{20,22},{2... | collective-permute-start | bytes 1572872 | tf_op jit(solution)/shard_map/ppermute | solution.py:15
  79.1 0.8 copy-start.8
  79.9 43.9 %collective-permute-start.4 = (bf16[2,512,256]{2,1,0:T(8,128)(2,1)}, bf16[2,512,256]{2,1,0:T(8,128)(2,1)}, u32[]{:S(2)}, u32[]{:S(2)}) collective-permute-start(bf16[2,512,256]{2,1,0:T(8,128)(2,1)} %collective-permute-done.3.refs_4_), channel_id=1, source_target_pairs={{4,7},{5,4},{6,5},{7,6},{12,15},{13,12},{14,13},{15,14},{20,23},{2... | collective-permute-start | bytes 1572872 | tf_op jit(solution)/shard_map/ppermute | solution.py:15
  123.8 1.0 copy-start.1
  124.9 1.0 copy-start.3
  125.9 1.0 copy-start.5
  126.9 1.0 copy-start.7
  128.0 1.0 copy-start.9
  135.8 6.1 %collective-permute-start.11 = (f32[2048,256]{1,0:T(8,128)S(1)}, f32[2048,256]{1,0:T(8,128)S(1)}, u32[]{:S(2)}, u32[]{:S(2)}) collective-permute-start(f32[2048,256]{1,0:T(8,128)S(1)} %get-tuple-element.8), channel_id=1, source_target_pairs={{0,8},{8,0},{1,9},{9,1},{2,10},{10,2},{3,11},{11,3},{4,12},{12,4},... | collective-permute-start | bytes 6291464 | tf_op jit(solution)/shard_map/ppermute | solution.py:113
  142.3 16.7 %collective-permute-start.12 = (f32[512,256]{1,0:T(8,128)S(1)}, f32[512,256]{1,0:T(8,128)S(1)}, u32[]{:S(2)}, u32[]{:S(2)}) collective-permute-start(f32[512,256]{1,0:T(8,128)S(1)} %get-tuple-element.11), channel_id=1, source_target_pairs={{0,128},{128,256},{256,384},{384,0},{1,129},{129,257},{257,385},{3... | collective-permute-start | bytes 1572872 | tf_op jit(solution)/shard_map/ppermute | solution.py:117
  145.7 16.0 %collective-permute-start.14 = (f32[512,256]{1,0:T(8,128)S(1)}, f32[512,256]{1,0:T(8,128)S(1)}, u32[]{:S(2)}, u32[]{:S(2)}) collective-permute-start(f32[512,256]{1,0:T(8,128)S(1)} %get-tuple-element.12), channel_id=1, source_target_pairs={{0,384},{128,0},{256,128},{384,256},{1,385},{129,1},{257,129},{385... | collective-permute-start | bytes 1572872 | tf_op jit(solution)/shard_map/ppermute | solution.py:117
  148.1 25.2 %collective-permute-start.13 = (f32[512,256]{1,0:T(8,128)S(1)}, f32[512,256]{1,0:T(8,128)S(1)}, u32[]{:S(2)}, u32[]{:S(2)}) collective-permute-start(f32[512,256]{1,0:T(8,128)S(1)} %get-tuple-element.13), channel_id=1, source_target_pairs={{0,256},{128,384},{256,0},{384,128},{1,257},{129,385},{257,1},{385... | collective-permute-start | bytes 1572872 | tf_op jit(solution)/shard_map/ppermute | solution.py:117
  173.5 75.9 %collective-permute-start.15 = (f32[256,256]{1,0:T(8,128)S(1)}, f32[256,256]{1,0:T(8,128)S(1)}, u32[]{:S(2)}, u32[]{:S(2)}) collective-permute-start(f32[256,256]{1,0:T(8,128)S(1)} %slice.63), channel_id=1, source_target_pairs={{0,16},{16,0},{32,48},{48,32},{64,80},{80,64},{96,112},{112,96},{1... | collective-permute-start | bytes 786440 | tf_op jit(solution)/shard_map/ppermute | solution.py:122
  249.5 9.3 %collective-permute-start.16 = (f32[128,256]{1,0:T(8,128)S(1)}, f32[128,256]{1,0:T(8,128)S(1)}, u32[]{:S(2)}, u32[]{:S(2)}) collective-permute-start(f32[128,256]{1,0:T(8,128)S(1)} %slice.65), channel_id=1, source_target_pairs={{0,32},{16,48},{32,0},{48,16},{64,96},{80,112},{96,64},{112,80},{1... | collective-permute-start | bytes 393224 | tf_op jit(solution)/shard_map/ppermute | solution.py:122
  258.8 11.5 %collective-permute-start.17 = (f32[64,256]{1,0:T(8,128)S(1)}, f32[64,256]{1,0:T(8,128)S(1)}, u32[]{:S(2)}, u32[]{:S(2)}) collective-permute-start(f32[64,256]{1,0:T(8,128)S(1)} %slice.67), channel_id=1, source_target_pairs={{0,64},{16,80},{32,96},{48,112},{64,0},{80,16},{96,32},{112,48},{1... | collective-permute-start | bytes 196616 | tf_op jit(solution)/shard_map/ppermute | solution.py:122

commit v2 on v0

v2 whole, which is shorter than its diff:
```python
import functools

import jax
import jax.numpy as jnp
from jax import lax
from jax.experimental import pallas as pl
from jax.experimental.pallas import tpu as pltpu
from jax.sharding import Mesh, PartitionSpec as P

NY, NZ, NC, NH, NX = 4, 8, 2, 2, 4
SIZES = {"y": NY, "zl": NZ, "core": NC, "x": NX}
QUARTER = 64
VMEM = pl.BlockSpec(memory_space=pltpu.VMEM)
SMEM = pl.BlockSpec(memory_space=pltpu.SMEM)
ANY = pl.BlockSpec(memory_space=pl.ANY)


def swap(v, axis, e):
    return lax.ppermute(v, axis, [(i, i ^ e) for i in range(SIZES[axis])])


def quarter_picker(x, width):
    p = lax.broadcasted_iota(jnp.int32, (QUARTER, width), 0)
    f = lax.broadcasted_iota(jnp.int32, (QUARTER, width), 1)
    wanted = (p // 32) * 128 + ((p // 16) % 2) * 64 + x * 16 + p % 16
    return (f == wanted).astype(jnp.float32).astype(jnp.bfloat16)


def pick(picker, block):
    return lax.dot_general(
        picker, block, (((1,), (1,)), ((), ())), preferred_element_type=jnp.float32
    ).astype(jnp.bfloat16)


def quarters_kernel(meta, pairs, own, load, *outs):
    blocks, tokens, width = own.shape
    for d in range(NX):
        picker = quarter_picker(meta[0] ^ d, width)
        for b in range(blocks):
            outs[d][b] = pick(picker, own[b])
    for b in range(blocks):
        load[b * tokens : (b + 1) * tokens] = own[b]
    slots = pairs.shape[0]
    slot = lax.broadcasted_iota(jnp.int32, (slots, width), 0)
    lane = lax.broadcasted_iota(jnp.int32, (slots, width), 1)
    table = jnp.zeros((slots, width), jnp.int32)
    for k in range(slots):
        table = jnp.where(slot == k, jnp.where(lane == 0, pairs[k, 0], pairs[k, 1]), table)
    load[blocks * tokens :] = table.astype(jnp.float32).astype(jnp.bfloat16)


def quarters(x, pairs, own):
    blocks, tokens, width = own.shape
    rows = blocks * tokens + pairs.shape[0]
    return pl.pallas_call(
        quarters_kernel,
        out_shape=[jax.ShapeDtypeStruct((rows, width), jnp.bfloat16)]
        + [jax.ShapeDtypeStruct((blocks, QUARTER, tokens), jnp.bfloat16)] * NX,
        in_specs=[SMEM, SMEM, VMEM],
        out_specs=[VMEM] * (1 + NX),
        compiler_params=pltpu.CompilerParams(vmem_limit_bytes=16 << 20),
    )(x[None].astype(jnp.int32), pairs, own)


HEAD = 8


def put(meta, n, product, keep, send):
    y, zl, core, x = meta[0], meta[1], meta[2], meta[3]
    k = lax.rem(n, 16)
    group = (k // 4) ^ y
    for half in range(2):
        e = (lax.rem(k, 4) * 2 + half) ^ zl
        place = ((e & 1) << 2) | (e & 2) | (e >> 2)
        at = pl.ds(pl.multiple_of(((group * 8 + place) * NX + (n // 16 ^ x)) * 16, 16), 16)
        if product is None:
            keep[at, :] = jnp.zeros((16, keep.shape[1]), jnp.float32)
            send[at, :] = jnp.zeros((16, keep.shape[1]), jnp.float32)
        else:
            first = product[half * 32 : half * 32 + 16]
            second = product[half * 32 + 16 : half * 32 + 32]
            keep[at, :] = jnp.where(core == 0, first, second)
            send[at, :] = jnp.where(core == 0, second, first)


def early_kernel(slots, meta, source, keep, send, cols, rows, sems):
    tokens = cols.shape[1]
    per = cols.shape[0] // NX
    copies = [
        pltpu.make_async_copy(source.at[b // per, pl.ds(b % per * tokens, tokens)], cols.at[b], sems.at[b])
        for b in range(cols.shape[0])
    ]
    for copy in copies:
        copy.start()
    picker = quarter_picker(meta[3], cols.shape[2])
    for b, copy in enumerate(copies):
        copy.wait()
        rows[b] = pick(picker, cols[b])

    def one(n, _):
        @pl.when(meta[HEAD + n] == 0)
        def _():
            put(meta, n, None, keep, send)

        @pl.when(meta[HEAD + n] == 1)
        def _():
            product = jnp.dot(
                rows[meta[HEAD + slots + n]],
                cols[meta[HEAD + 2 * slots + n]],
                preferred_element_type=jnp.float32,
            )
            put(meta, n, product, keep, send)

        return 0

    lax.fori_loop(0, slots, one, 0)


def late_kernel(slots, meta, cols, *refs):
    sources, (_, _, keep, send, rows, sems) = refs[:NX], refs[NX:]
    per = sources[0].shape[0]
    copies = [
        pltpu.make_async_copy(sources[d], rows.at[pl.ds(d * per, per)], sems.at[d])
        for d in range(NX)
    ]
    for copy in copies:
        copy.start()
    for copy in copies:
        copy.wait()

    def one(n, _):
        @pl.when(meta[HEAD + n] == 2)
        def _():
            product = jnp.dot(
                rows[meta[HEAD + slots + n]],
                cols[meta[HEAD + 2 * slots + n]],
                preferred_element_type=jnp.float32,
            )
            put(meta, n, product, keep, send)

        return 0

    lax.fori_loop(0, slots, one, 0)


def early(meta, source, count, tokens, slots):
    width = source.shape[2]
    half = jax.ShapeDtypeStruct((slots * QUARTER // 2, width), jnp.float32)
    return pl.pallas_call(
        functools.partial(early_kernel, slots),
        out_shape=[half, half, jax.ShapeDtypeStruct((count, tokens, width), jnp.bfloat16)],
        in_specs=[SMEM, ANY],
        out_specs=[VMEM] * 3,
        scratch_shapes=[
            pltpu.VMEM((count, QUARTER, tokens), jnp.bfloat16),
            pltpu.SemaphoreType.DMA((count,)),
        ],
        compiler_params=pltpu.CompilerParams(vmem_limit_bytes=24 << 20),
    )(meta, source)


def late(meta, cols, sources, keep, send, slots):
    per, quarter, tokens = sources[0].shape
    half = jax.ShapeDtypeStruct(keep.shape, jnp.float32)
    return pl.pallas_call(
        functools.partial(late_kernel, slots),
        out_shape=[half, half],
        in_specs=[SMEM, VMEM] + [ANY] * NX + [VMEM] * 2,
        out_specs=[VMEM] * 2,
        scratch_shapes=[
            pltpu.VMEM((NX * per, quarter, tokens), jnp.bfloat16),
            pltpu.SemaphoreType.DMA((NX,)),
        ],
        input_output_aliases={2 + NX: 0, 3 + NX: 1},
        compiler_params=pltpu.CompilerParams(vmem_limit_bytes=24 << 20),
    )(meta, cols, *sources, keep, send)


def body(activations, block_map):
    tokens, blocks, width = activations.shape
    y, zl, core = (lax.axis_index(a) for a in ("y", "zl", "core"))
    zh, x = lax.axis_index("zh"), lax.axis_index("x")

    own = jnp.transpose(activations, (1, 0, 2))
    load, *pieces = quarters(x, block_map[0], own)
    low = [
        lax.ppermute(piece, ("zh", "x"), [(i, NX + (i ^ e)) for i in range(NX)])
        for e, piece in enumerate(pieces)
    ]
    half = lax.all_to_all(jnp.broadcast_to(load, (NX, *load.shape)), "x", 0, 0, tiled=True)
    pairs = half[:, blocks * tokens :, :2].astype(jnp.int32).reshape(-1, 2)
    slots = pairs.shape[0]
    row, col = jnp.maximum(pairs[:, 0], 0), jnp.maximum(pairs[:, 1], 0)
    live, same = pairs[:, 0] >= 0, row // blocks // NX == zh
    kind = jnp.where(live, jnp.where(same, 1, 2), 0)
    row_at = jnp.where(same, row // blocks % NX, row // blocks % NX ^ x) * blocks + row % blocks
    col_at = col % (NX * blocks)
    head = jnp.stack([y, zl, core, x, zh, zh, zh, zh])
    meta = jnp.concatenate([head, kind, row_at, col_at]).astype(jnp.int32)

    keep, send, cols = early(meta, half, NX * blocks, tokens, slots)
    keep, send = late(meta, cols, low, keep, send, slots)

    total = keep + swap(send, "core", 1)
    part = total.shape[0] // NY
    mine = total[:part]
    for e in (2, 1, 3):
        mine = mine + swap(total[e * part : e * part + part], "y", e)
    for bit in (1, 2, 4):
        half = mine.shape[0] // 2
        mine = mine[:half] + swap(mine[half:], "zl", bit)
    mine = mine * (2.0 / (tokens * NY * NZ * NC))
    part = mine.shape[0] // NX
    a = [mine[:part]] + [swap(mine[e * part : e * part + part], "x", e) for e in (1, 2, 3)]
    odd, high = x % 2 == 1, x >= 2
    a = [jnp.where(odd, a[q ^ 1], a[q]) for q in range(NX)]
    a = [jnp.where(high, a[q ^ 2], a[q]) for q in range(NX)]
    return jnp.concatenate(a)[None]


def solution(mesh):
    grid = Mesh(mesh.devices.reshape(NY, NZ, NC, NH, NX), ("y", "zl", "core", "zh", "x"))
    tok, slab = ("y", "zl", "core"), ("zh", "x")
    return jax.shard_map(
        body,
        mesh=grid,
        in_specs=(P(tok, slab, None), P(slab, None, None)),
        out_specs=P(slab, tok, None),
        check_vma=False,
    )
```

time: 785 us -> 206 us (0.26)
  the two profiles are of different devices: /device:TPU:6 before, /device:TPU:272 now
where the time goes in v2:
time: 206 us; the launch traced here: 205 us
  waiting for transfers between devices  104 us (50%)
  starting transfers between devices  77.6 us (38%)
  Pallas kernels  16.9 us (8%)
  local copies, waits for them, and re-layouts  4.88 us (2%)
    ppermute x10, starting transfers between devices, swap(): return lax.ppermute(v, axis, [(i, i ^ e) for i in range(SIZES[axis])])  67.6 us
    all_to_all x1, waiting for transfers between devices, body(): lax.all_to_all(jnp.broadcast_to(load, (NX, *load.shape)), 'x', 0, 0, tile...  56.1 us
    ppermute x10, waiting for transfers between devices, swap(): return lax.ppermute(v, axis, [(i, i ^ e) for i in range(SIZES[axis])])  48.4 us
    pallas_call x1, Pallas kernels, early(): pl.pallas_call(functools.partial(early_kernel, slots), out_shape=[half, h...  9.15 us
    pallas_call x1, Pallas kernels, late(): pl.pallas_call(functools.partial(late_kernel, slots), out_shape=[half, ha...  5.74 us
    ppermute x4, starting transfers between devices, body(): lax.ppermute(piece, ('zh', 'x'), [(i, NX + (i ^ e)) for i in range(NX)])  5.17 us
    all_to_all x1, starting transfers between devices, body(): lax.all_to_all(jnp.broadcast_to(load, (NX, *load.shape)), 'x', 0, 0, tile...  4.89 us
  transfers between devices with their start and end apart: 15, of which 10 were waited for; matrix products, arithmetic and copies ran while one was open for 1% of the time, Pallas kernels for 4%

profile of v2, /device:TPU:272, one launch (start us, length us, event | category | flops | bytes accessed | tf_op | source)
XLA Modules:
  0.0 205.4 jit_solution(16541179354807002344)
XLA Ops:
  0.0 0.0 copy-start
  0.0 1.4 copy.16
  1.4 0.0 copy-done
  1.4 0.1 copy.9.pairs
  1.5 2.0 shard_map.28
  3.5 2.3 %broadcast_in_dim.13 = bf16[4,2064,256]{2,1,0:T(8,128)(2,1)} broadcast(bf16[2064,256]{1,0:T(8,128)(2,1)S(1)} %get-tuple-element.15), dimensions={1,2} | broadcast | bytes 5283840 | tf_op jit(solution)/shard_map/broadcast_in_dim | solution.py:190
  5.8 4.9 %all-to-all-start = ((bf16[4,2064,256]{2,1,0:T(8,128)(2,1)}), bf16[4,2064,256]{2,1,0:T(8,128)(2,1)}, u32[]{:S(2)}, u32[]{:S(2)}) async-start(bf16[4,2064,256]{2,1,0:T(8,128)(2,1)} %broadcast_in_dim.13), calls=%async_computation | async-start | bytes 8454144 | tf_op jit(solution)/shard_map/all_to_all | solution.py:190
  10.7 1.3 collective-permute-start
  12.0 1.3 collective-permute-start.1
  13.3 1.3 collective-permute-start.2
  14.6 1.3 collective-permute-start.3
  15.9 56.1 %all-to-all-done.source = bf16[4,2064,256]{2,1,0:T(8,128)(2,1)} async-done(((bf16[4,2064,256]{2,1,0:T(8,128)(2,1)}), bf16[4,2064,256]{2,1,0:T(8,128)(2,1)}, u32[]{:S(2)}, u32[]{:S(2)}) %all-to-all-start) | async-done | bytes 4227104 | tf_op jit(solution)/shard_map/all_to_all | solution.py:190
  72.0 0.7 slice.69
  72.8 0.1 maximum_and_fusion
  72.8 0.1 copy.12
  72.9 0.1 copy.14
  73.0 0.1 concatenate.6.meta
  73.1 9.1 %shard_map.29 = (f32[2048,256]{1,0:T(8,128)S(1)}, f32[2048,256]{1,0:T(8,128)S(1)}, bf16[16,512,256]{2,1,0:T(8,128)(2,1)S(1)}) custom-call(s32[200]{0:T(256)S(1)} %concatenate.6.meta, bf16[4,2064,256]{2,1,0:T(8,128)(2,1)} %all-to-all-done.source), custom_call_target="tpu_custom_call" | custom-call | tf_op jit(solution)/shard_map/pallas_call | solution.py:149
  82.3 0.0 collective-permute-done.refs_0_
  82.3 0.0 collective-permute-done.1.refs_1_
  82.3 0.0 collective-permute-done.2.refs_2_
  82.3 0.0 collective-permute-done.3.refs_3_
  82.3 5.7 %shard_map.30 = (f32[2048,256]{1,0:T(8,128)S(1)}, f32[2048,256]{1,0:T(8,128)S(1)}) custom-call(s32[200]{0:T(256)S(1)} %concatenate.6.meta, bf16[16,512,256]{2,1,0:T(8,128)(2,1)S(1)} %get-tuple-element.16.cols, bf16[4,64,512]{2,1,0:T(8,128)(2,1)S(1)} %collective-permute-done.refs_0_, ...), custom_call_target="tpu_custom_call", output_to_operand_aliasing={{0}: (6, {}), {1}: (7, {})} | custom-call | tf_op jit(solution)/shard_map/pallas_call | solution.py:165
  88.1 1.9 collective-permute-start.4
  90.0 4.1 %collective-permute-done.4 = f32[2048,256]{1,0:T(8,128)S(1)} collective-permute-done((f32[2048,256]{1,0:T(8,128)S(1)}, f32[2048,256]{1,0:T(8,128)S(1)}, u32[]{:S(2)}, u32[]{:S(2)}) %collective-permute-start.4) | collective-permute-done | bytes 2097184 | tf_op jit(solution)/shard_map/ppermute | solution.py:19
  94.1 0.3 add.51
  94.4 0.1 fusion.5
  94.5 2.3 %collective-permute-start.5 = (f32[512,256]{1,0:T(8,128)S(1)}, f32[512,256]{1,0:T(8,128)S(1)}, u32[]{:S(2)}, u32[]{:S(2)}) collective-permute-start(f32[512,256]{1,0:T(8,128)S(1)} %get-tuple-element.27), channel_id=1, source_target_pairs={{0,256},{128,384},{256,0},{384,128},{1,257},{129,385},{257,1},{385... | collective-permute-start | bytes 1572872 | tf_op jit(solution)/shard_map/ppermute | solution.py:19
  96.8 4.1 %collective-permute-start.6 = (f32[512,256]{1,0:T(8,128)S(1)}, f32[512,256]{1,0:T(8,128)S(1)}, u32[]{:S(2)}, u32[]{:S(2)}) collective-permute-start(f32[512,256]{1,0:T(8,128)S(1)} %get-tuple-element.29), channel_id=1, source_target_pairs={{0,128},{128,0},{256,384},{384,256},{1,129},{129,1},{257,385},{385... | collective-permute-start | bytes 1572872 | tf_op jit(solution)/shard_map/ppermute | solution.py:19
  100.8 3.5 %collective-permute-start.7 = (f32[512,256]{1,0:T(8,128)S(1)}, f32[512,256]{1,0:T(8,128)S(1)}, u32[]{:S(2)}, u32[]{:S(2)}) collective-permute-start(f32[512,256]{1,0:T(8,128)S(1)} %get-tuple-element.28), channel_id=1, source_target_pairs={{0,384},{128,256},{256,128},{384,0},{1,385},{129,257},{257,129},{3... | collective-permute-start | bytes 1572872 | tf_op jit(solution)/shard_map/ppermute | solution.py:19
  104.3 8.4 %collective-permute-done.5 = f32[512,256]{1,0:T(8,128)S(1)} collective-permute-done((f32[512,256]{1,0:T(8,128)S(1)}, f32[512,256]{1,0:T(8,128)S(1)}, u32[]{:S(2)}, u32[]{:S(2)}) %collective-permute-start.5) | collective-permute-done | bytes 524320 | tf_op jit(solution)/shard_map/ppermute | solution.py:19
  112.7 9.4 %collective-permute-done.6 = f32[512,256]{1,0:T(8,128)S(1)} collective-permute-done((f32[512,256]{1,0:T(8,128)S(1)}, f32[512,256]{1,0:T(8,128)S(1)}, u32[]{:S(2)}, u32[]{:S(2)}) %collective-permute-start.6) | collective-permute-done | bytes 524320 | tf_op jit(solution)/shard_map/ppermute | solution.py:19
  122.1 1.0 collective-permute-done.7
  123.1 0.2 fusion.1
  123.3 40.6 %collective-permute-start.8 = (f32[256,256]{1,0:T(8,128)S(1)}, f32[256,256]{1,0:T(8,128)S(1)}, u32[]{:S(2)}, u32[]{:S(2)}) collective-permute-start(f32[256,256]{1,0:T(8,128)S(1)} %slice.77), channel_id=1, source_target_pairs={{0,16},{16,0},{32,48},{48,32},{64,80},{80,64},{96,112},{112,96},{1... | collective-permute-start | bytes 786440 | tf_op jit(solution)/shard_map/ppermute | solution.py:19
  163.9 6.5 %collective-permute-done.8 = f32[256,256]{1,0:T(8,128)S(1)} collective-permute-done((f32[256,256]{1,0:T(8,128)S(1)}, f32[256,256]{1,0:T(8,128)S(1)}, u32[]{:S(2)}, u32[]{:S(2)}) %collective-permute-start.8) | collective-permute-done | bytes 262176 | tf_op jit(solution)/shard_map/ppermute | solution.py:19
  170.4 1.9 collective-permute-start.9
  172.3 8.6 %collective-permute-done.9 = f32[128,256]{1,0:T(8,128)S(1)} collective-permute-done((f32[128,256]{1,0:T(8,128)S(1)}, f32[128,256]{1,0:T(8,128)S(1)}, u32[]{:S(2)}, u32[]{:S(2)}) %collective-permute-start.9) | collective-permute-done | bytes 131104 | tf_op jit(solution)/shard_map/ppermute | solution.py:19
  180.9 3.5 %collective-permute-start.10 = (f32[64,256]{1,0:T(8,128)S(1)}, f32[64,256]{1,0:T(8,128)S(1)}, u32[]{:S(2)}, u32[]{:S(2)}) collective-permute-start(f32[64,256]{1,0:T(8,128)S(1)} %slice.81), channel_id=1, source_target_pairs={{0,64},{16,80},{32,96},{48,112},{64,0},{80,16},{96,32},{112,48},{1... | collective-permute-start | bytes 196616 | tf_op jit(solution)/shard_map/ppermute | solution.py:19
  184.5 8.2 %collective-permute-done.10 = f32[64,256]{1,0:T(8,128)S(1)} collective-permute-done((f32[64,256]{1,0:T(8,128)S(1)}, f32[64,256]{1,0:T(8,128)S(1)}, u32[]{:S(2)}, u32[]{:S(2)}) %collective-permute-start.10) | collective-permute-done | bytes 65568 | tf_op jit(solution)/shard_map/ppermute | solution.py:19
  192.7 3.1 %collective-permute-start.11 = (f32[16,256]{1,0:T(8,128)S(1)}, f32[16,256]{1,0:T(8,128)S(1)}, u32[]{:S(2)}, u32[]{:S(2)}) collective-permute-start(f32[16,256]{1,0:T(8,128)S(1)} %get-tuple-element.36), channel_id=1, source_target_pairs={{0,3},{1,2},{2,1},{3,0},{4,7},{5,6},{6,5},{7,4},{8,11},{9,10},{10,... | collective-permute-start | bytes 49160 | tf_op jit(solution)/shard_map/ppermute | solution.py:19
  195.8 3.4 %collective-permute-start.12 = (f32[16,256]{1,0:T(8,128)S(1)}, f32[16,256]{1,0:T(8,128)S(1)}, u32[]{:S(2)}, u32[]{:S(2)}) collective-permute-start(f32[16,256]{1,0:T(8,128)S(1)} %get-tuple-element.35), channel_id=1, source_target_pairs={{0,2},{1,3},{2,0},{3,1},{4,6},{5,7},{6,4},{7,5},{8,10},{9,11},{10,... | collective-permute-start | bytes 49160 | tf_op jit(solution)/shard_map/ppermute | solution.py:19
  199.2 3.4 %collective-permute-start.13 = (f32[16,256]{1,0:T(8,128)S(1)}, f32[16,256]{1,0:T(8,128)S(1)}, u32[]{:S(2)}, u32[]{:S(2)}) collective-permute-start(f32[16,256]{1,0:T(8,128)S(1)} %get-tuple-element.34), channel_id=1, source_target_pairs={{0,1},{1,0},{2,3},{3,2},{4,5},{5,4},{6,7},{7,6},{8,9},{9,8},{10,11... | collective-permute-start | bytes 49160 | tf_op jit(solution)/shard_map/ppermute | solution.py:19
  202.5 0.0 collective-permute-done.11
  202.6 0.4 collective-permute-done.12
  202.9 1.9 collective-permute-done.13
  204.8 0.6 maximum_bitcast_fusion
  (11 shorter events, 0.2 us)
Async XLA Ops:
  0.0 1.4 copy-start
  5.8 66.2 %all-to-all-start = ((bf16[4,2064,256]{2,1,0:T(8,128)(2,1)}), bf16[4,2064,256]{2,1,0:T(8,128)(2,1)}, u32[]{:S(2)}, u32[]{:S(2)}) async-start(bf16[4,2064,256]{2,1,0:T(8,128)(2,1)} %broadcast_in_dim.13), calls=%async_computation | async-start | bytes 8454144 | tf_op jit(solution)/shard_map/all_to_all | solution.py:190
  10.7 71.5 %collective-permute-start = (bf16[4,64,512]{2,1,0:T(8,128)(2,1)S(1)}, bf16[4,64,512]{2,1,0:T(8,128)(2,1)S(1)}, u32[]{:S(2)}, u32[]{:S(2)}) collective-permute-start(bf16[4,64,512]{2,1,0:T(8,128)(2,1)S(1)} %get-tuple-element.17), channel_id=1, source_target_pairs={{0,4},{1,5},{2,6},{3,7},{8,12},{9,13},{10,14},{11,15},{16,20},{17,... | collective-permute-start | bytes 786440 | tf_op jit(solution)/shard_map/ppermute | solution.py:187
  12.0 70.2 %collective-permute-start.1 = (bf16[4,64,512]{2,1,0:T(8,128)(2,1)S(1)}, bf16[4,64,512]{2,1,0:T(8,128)(2,1)S(1)}, u32[]{:S(2)}, u32[]{:S(2)}) collective-permute-start(bf16[4,64,512]{2,1,0:T(8,128)(2,1)S(1)} %get-tuple-element.18), channel_id=1, source_target_pairs={{0,5},{1,4},{2,7},{3,6},{8,13},{9,12},{10,15},{11,14},{16,21},{17,... | collective-permute-start | bytes 786440 | tf_op jit(solution)/shard_map/ppermute | solution.py:187
  13.3 69.0 %collective-permute-start.2 = (bf16[4,64,512]{2,1,0:T(8,128)(2,1)S(1)}, bf16[4,64,512]{2,1,0:T(8,128)(2,1)S(1)}, u32[]{:S(2)}, u32[]{:S(2)}) collective-permute-start(bf16[4,64,512]{2,1,0:T(8,128)(2,1)S(1)} %get-tuple-element.19), channel_id=1, source_target_pairs={{0,6},{1,7},{2,4},{3,5},{8,14},{9,15},{10,12},{11,13},{16,22},{17,... | collective-permute-start | bytes 786440 | tf_op jit(solution)/shard_map/ppermute | solution.py:187
  14.6 67.7 %collective-permute-start.3 = (bf16[4,64,512]{2,1,0:T(8,128)(2,1)S(1)}, bf16[4,64,512]{2,1,0:T(8,128)(2,1)S(1)}, u32[]{:S(2)}, u32[]{:S(2)}) collective-permute-start(bf16[4,64,512]{2,1,0:T(8,128)(2,1)S(1)} %get-tuple-element.20), channel_id=1, source_target_pairs={{0,7},{1,6},{2,5},{3,4},{8,15},{9,14},{10,13},{11,12},{16,23},{17,... | collective-permute-start | bytes 786440 | tf_op jit(solution)/shard_map/ppermute | solution.py:187
  88.1 6.1 %collective-permute-start.4 = (f32[2048,256]{1,0:T(8,128)S(1)}, f32[2048,256]{1,0:T(8,128)S(1)}, u32[]{:S(2)}, u32[]{:S(2)}) collective-permute-start(f32[2048,256]{1,0:T(8,128)S(1)} %get-tuple-element.24), channel_id=1, source_target_pairs={{0,8},{8,0},{1,9},{9,1},{2,10},{10,2},{3,11},{11,3},{4,12},{12,4},... | collective-permute-start | bytes 6291464 | tf_op jit(solution)/shard_map/ppermute | solution.py:19
  94.5 18.2 %collective-permute-start.5 = (f32[512,256]{1,0:T(8,128)S(1)}, f32[512,256]{1,0:T(8,128)S(1)}, u32[]{:S(2)}, u32[]{:S(2)}) collective-permute-start(f32[512,256]{1,0:T(8,128)S(1)} %get-tuple-element.27), channel_id=1, source_target_pairs={{0,256},{128,384},{256,0},{384,128},{1,257},{129,385},{257,1},{385... | collective-permute-start | bytes 1572872 | tf_op jit(solution)/shard_map/ppermute | solution.py:19
  96.8 25.4 %collective-permute-start.6 = (f32[512,256]{1,0:T(8,128)S(1)}, f32[512,256]{1,0:T(8,128)S(1)}, u32[]{:S(2)}, u32[]{:S(2)}) collective-permute-start(f32[512,256]{1,0:T(8,128)S(1)} %get-tuple-element.29), channel_id=1, source_target_pairs={{0,128},{128,0},{256,384},{384,256},{1,129},{129,1},{257,385},{385... | collective-permute-start | bytes 1572872 | tf_op jit(solution)/shard_map/ppermute | solution.py:19
  100.8 22.2 %collective-permute-start.7 = (f32[512,256]{1,0:T(8,128)S(1)}, f32[512,256]{1,0:T(8,128)S(1)}, u32[]{:S(2)}, u32[]{:S(2)}) collective-permute-start(f32[512,256]{1,0:T(8,128)S(1)} %get-tuple-element.28), channel_id=1, source_target_pairs={{0,384},{128,256},{256,128},{384,0},{1,385},{129,257},{257,129},{3... | collective-permute-start | bytes 1572872 | tf_op jit(solution)/shard_map/ppermute | solution.py:19
  123.3 47.0 %collective-permute-start.8 = (f32[256,256]{1,0:T(8,128)S(1)}, f32[256,256]{1,0:T(8,128)S(1)}, u32[]{:S(2)}, u32[]{:S(2)}) collective-permute-start(f32[256,256]{1,0:T(8,128)S(1)} %slice.77), channel_id=1, source_target_pairs={{0,16},{16,0},{32,48},{48,32},{64,80},{80,64},{96,112},{112,96},{1... | collective-permute-start | bytes 786440 | tf_op jit(solution)/shard_map/ppermute | solution.py:19
  170.4 10.5 %collective-permute-start.9 = (f32[128,256]{1,0:T(8,128)S(1)}, f32[128,256]{1,0:T(8,128)S(1)}, u32[]{:S(2)}, u32[]{:S(2)}) collective-permute-start(f32[128,256]{1,0:T(8,128)S(1)} %slice.79), channel_id=1, source_target_pairs={{0,32},{16,48},{32,0},{48,16},{64,96},{80,112},{96,64},{112,80},{1... | collective-permute-start | bytes 393224 | tf_op jit(solution)/shard_map/ppermute | solution.py:19
  180.9 11.7 %collective-permute-start.10 = (f32[64,256]{1,0:T(8,128)S(1)}, f32[64,256]{1,0:T(8,128)S(1)}, u32[]{:S(2)}, u32[]{:S(2)}) collective-permute-start(f32[64,256]{1,0:T(8,128)S(1)} %slice.81), channel_id=1, source_target_pairs={{0,64},{16,80},{32,96},{48,112},{64,0},{80,16},{96,32},{112,48},{1... | collective-permute-start | bytes 196616 | tf_op jit(solution)/shard_map/ppermute | solution.py:19
  192.7 9.9 %collective-permute-start.11 = (f32[16,256]{1,0:T(8,128)S(1)}, f32[16,256]{1,0:T(8,128)S(1)}, u32[]{:S(2)}, u32[]{:S(2)}) collective-permute-start(f32[16,256]{1,0:T(8,128)S(1)} %get-tuple-element.36), channel_id=1, source_target_pairs={{0,3},{1,2},{2,1},{3,0},{4,7},{5,6},{6,5},{7,4},{8,11},{9,10},{10,... | collective-permute-start | bytes 49160 | tf_op jit(solution)/shard_map/ppermute | solution.py:19
  195.8 7.1 %collective-permute-start.12 = (f32[16,256]{1,0:T(8,128)S(1)}, f32[16,256]{1,0:T(8,128)S(1)}, u32[]{:S(2)}, u32[]{:S(2)}) collective-permute-start(f32[16,256]{1,0:T(8,128)S(1)} %get-tuple-element.35), channel_id=1, source_target_pairs={{0,2},{1,3},{2,0},{3,1},{4,6},{5,7},{6,4},{7,5},{8,10},{9,11},{10,... | collective-permute-start | bytes 49160 | tf_op jit(solution)/shard_map/ppermute | solution.py:19
  199.2 5.6 %collective-permute-start.13 = (f32[16,256]{1,0:T(8,128)S(1)}, f32[16,256]{1,0:T(8,128)S(1)}, u32[]{:S(2)}, u32[]{:S(2)}) collective-permute-start(f32[16,256]{1,0:T(8,128)S(1)} %get-tuple-element.34), channel_id=1, source_target_pairs={{0,1},{1,0},{2,3},{3,2},{4,5},{5,4},{6,7},{7,6},{8,9},{9,8},{10,11... | collective-permute-start | bytes 49160 | tf_op jit(solution)/shard_map/ppermute | solution.py:19

commit v3 on v2

--- a/solution.py
+++ b/solution.py
@@ -9,6 +9,7 @@
 
 NY, NZ, NC, NH, NX = 4, 8, 2, 2, 4
 SIZES = {"y": NY, "zl": NZ, "core": NC, "x": NX}
+CUTS = 2
 QUARTER = 64
 VMEM = pl.BlockSpec(memory_space=pltpu.VMEM)
 SMEM = pl.BlockSpec(memory_space=pltpu.SMEM)
@@ -38,15 +39,17 @@
         picker = quarter_picker(meta[0] ^ d, width)
         for b in range(blocks):
             outs[d][b] = pick(picker, own[b])
-    for b in range(blocks):
-        load[b * tokens : (b + 1) * tokens] = own[b]
     slots = pairs.shape[0]
     slot = lax.broadcasted_iota(jnp.int32, (slots, width), 0)
     lane = lax.broadcasted_iota(jnp.int32, (slots, width), 1)
     table = jnp.zeros((slots, width), jnp.int32)
     for k in range(slots):
         table = jnp.where(slot == k, jnp.where(lane == 0, pairs[k, 0], pairs[k, 1]), table)
-    load[blocks * tokens :] = table.astype(jnp.float32).astype(jnp.bfloat16)
+    table = table.astype(jnp.float32).astype(jnp.bfloat16)
+    for d in range(NX):
+        for b in range(blocks):
+            load[d, b * tokens : (b + 1) * tokens] = own[b]
+        load[d, blocks * tokens :] = table
 
 
 def quarters(x, pairs, own):
@@ -54,7 +57,7 @@
     rows = blocks * tokens + pairs.shape[0]
     return pl.pallas_call(
         quarters_kernel,
-        out_shape=[jax.ShapeDtypeStruct((rows, width), jnp.bfloat16)]
+        out_shape=[jax.ShapeDtypeStruct((NX, rows, width), jnp.bfloat16)]
         + [jax.ShapeDtypeStruct((blocks, QUARTER, tokens), jnp.bfloat16)] * NX,
         in_specs=[SMEM, SMEM, VMEM],
         out_specs=[VMEM] * (1 + NX),
@@ -66,24 +69,28 @@
 
 
 def put(meta, n, product, keep, send):
-    y, zl, core, x = meta[0], meta[1], meta[2], meta[3]
+    y, core = meta[0], meta[2]
     k = lax.rem(n, 16)
-    group = (k // 4) ^ y
+    e = k // 4 ^ y
+    groups = [e ^ (e >> 1), ((e ^ (e >> 1)) >> 1) | ((e & 1) ^ (e >> 1)) << 1]
     for half in range(2):
-        e = (lax.rem(k, 4) * 2 + half) ^ zl
-        place = ((e & 1) << 2) | (e & 2) | (e >> 2)
-        at = pl.ds(pl.multiple_of(((group * 8 + place) * NX + (n // 16 ^ x)) * 16, 16), 16)
-        if product is None:
-            keep[at, :] = jnp.zeros((16, keep.shape[1]), jnp.float32)
-            send[at, :] = jnp.zeros((16, keep.shape[1]), jnp.float32)
-        else:
-            first = product[half * 32 : half * 32 + 16]
-            second = product[half * 32 + 16 : half * 32 + 32]
-            keep[at, :] = jnp.where(core == 0, first, second)
-            send[at, :] = jnp.where(core == 0, second, first)
-
-
-def early_kernel(slots, meta, source, keep, send, cols, rows, sems):
+        place = lax.rem(k, 4) * 2 + half
+        for cut in range(CUTS):
+            at = pl.ds(pl.multiple_of(((groups[cut] * 8 + place) * NX + n // 16) * 16, 16), 16)
+            wide = keep[cut].shape[1]
+            lanes = slice(cut * wide, (cut + 1) * wide)
+            if product is None:
+                keep[cut][at, :] = jnp.zeros((16, wide), jnp.float32)
+                send[cut][at, :] = jnp.zeros((16, wide), jnp.float32)
+            else:
+                first = product[half * 32 : half * 32 + 16, lanes]
+                second = product[half * 32 + 16 : half * 32 + 32, lanes]
+                keep[cut][at, :] = jnp.where(core == 0, first, second)
+                send[cut][at, :] = jnp.where(core == 0, second, first)
+
+
+def early_kernel(slots, meta, source, *refs):
+    keep, send, (cols, rows, sems) = refs[:CUTS], refs[CUTS : 2 * CUTS], refs[2 * CUTS :]
     tokens = cols.shape[1]
     per = cols.shape[0] // NX
     copies = [
@@ -117,7 +124,8 @@
 
 
 def late_kernel(slots, meta, cols, *refs):
-    sources, (_, _, keep, send, rows, sems) = refs[:NX], refs[NX:]
+    sources, refs = refs[:NX], refs[NX + 2 * CUTS :]
+    keep, send, (rows, sems) = refs[:CUTS], refs[CUTS : 2 * CUTS], refs[2 * CUTS :]
     per = sources[0].shape[0]
     copies = [
         pltpu.make_async_copy(sources[d], rows.at[pl.ds(d * per, per)], sems.at[d])
@@ -145,12 +153,12 @@
 
 def early(meta, source, count, tokens, slots):
     width = source.shape[2]
-    half = jax.ShapeDtypeStruct((slots * QUARTER // 2, width), jnp.float32)
+    half = jax.ShapeDtypeStruct((slots * QUARTER // 2, width // CUTS), jnp.float32)
     return pl.pallas_call(
         functools.partial(early_kernel, slots),
-        out_shape=[half, half, jax.ShapeDtypeStruct((count, tokens, width), jnp.bfloat16)],
+        out_shape=[half] * (2 * CUTS) + [jax.ShapeDtypeStruct((count, tokens, width), jnp.bfloat16)],
         in_specs=[SMEM, ANY],
-        out_specs=[VMEM] * 3,
+        out_specs=[VMEM] * (2 * CUTS + 1),
         scratch_shapes=[
             pltpu.VMEM((count, QUARTER, tokens), jnp.bfloat16),
             pltpu.SemaphoreType.DMA((count,)),
@@ -159,21 +167,20 @@
     )(meta, source)
 
 
-def late(meta, cols, sources, keep, send, slots):
+def late(meta, cols, sources, halves, slots):
     per, quarter, tokens = sources[0].shape
-    half = jax.ShapeDtypeStruct(keep.shape, jnp.float32)
     return pl.pallas_call(
         functools.partial(late_kernel, slots),
-        out_shape=[half, half],
-        in_specs=[SMEM, VMEM] + [ANY] * NX + [VMEM] * 2,
-        out_specs=[VMEM] * 2,
+        out_shape=[jax.ShapeDtypeStruct(h.shape, h.dtype) for h in halves],
+        in_specs=[SMEM, VMEM] + [ANY] * NX + [VMEM] * len(halves),
+        out_specs=[VMEM] * len(halves),
         scratch_shapes=[
             pltpu.VMEM((NX * per, quarter, tokens), jnp.bfloat16),
             pltpu.SemaphoreType.DMA((NX,)),
         ],
-        input_output_aliases={2 + NX: 0, 3 + NX: 1},
+        input_output_aliases={2 + NX + i: i for i in range(len(halves))},
         compiler_params=pltpu.CompilerParams(vmem_limit_bytes=24 << 20),
-    )(meta, cols, *sources, keep, send)
+    )(meta, cols, *sources, *halves)
 
 
 def body(activations, block_map):
@@ -187,7 +194,7 @@
         lax.ppermute(piece, ("zh", "x"), [(i, NX + (i ^ e)) for i in range(NX)])
         for e, piece in enumerate(pieces)
     ]
-    half = lax.all_to_all(jnp.broadcast_to(load, (NX, *load.shape)), "x", 0, 0, tiled=True)
+    half = lax.all_to_all(load, "x", 0, 0, tiled=True)
     pairs = half[:, blocks * tokens :, :2].astype(jnp.int32).reshape(-1, 2)
     slots = pairs.shape[0]
     row, col = jnp.maximum(pairs[:, 0], 0), jnp.maximum(pairs[:, 1], 0)
@@ -198,24 +205,21 @@
     head = jnp.stack([y, zl, core, x, zh, zh, zh, zh])
     meta = jnp.concatenate([head, kind, row_at, col_at]).astype(jnp.int32)
 
-    keep, send, cols = early(meta, half, NX * blocks, tokens, slots)
-    keep, send = late(meta, cols, low, keep, send, slots)
-
-    total = keep + swap(send, "core", 1)
-    part = total.shape[0] // NY
-    mine = total[:part]
-    for e in (2, 1, 3):
-        mine = mine + swap(total[e * part : e * part + part], "y", e)
-    for bit in (1, 2, 4):
-        half = mine.shape[0] // 2
-        mine = mine[:half] + swap(mine[half:], "zl", bit)
-    mine = mine * (2.0 / (tokens * NY * NZ * NC))
-    part = mine.shape[0] // NX
-    a = [mine[:part]] + [swap(mine[e * part : e * part + part], "x", e) for e in (1, 2, 3)]
-    odd, high = x % 2 == 1, x >= 2
-    a = [jnp.where(odd, a[q ^ 1], a[q]) for q in range(NX)]
-    a = [jnp.where(high, a[q ^ 2], a[q]) for q in range(NX)]
-    return jnp.concatenate(a)[None]
+    *halves, cols = early(meta, half, NX * blocks, tokens, slots)
+    halves = late(meta, cols, low, halves, slots)
+    scale = 2.0 / (tokens * NY * NZ * NC)
+    cuts = [total(keep, send, order) for keep, send, order in zip(halves[:CUTS], halves[CUTS:], ((3, 1), (1, 3)))]
+    parts = jnp.concatenate(cuts, axis=1).reshape(NZ * NX, -1, width)
+    parts = lax.all_to_all(parts, ("zl", "x"), 0, 0, tiled=True).reshape(NZ, -1, width)
+    return jnp.sum(parts, axis=0)[None] * scale
+
+
+def total(keep, send, order):
+    kept = keep + swap(send, "core", 1)
+    for e in order:
+        half = kept.shape[0] // 2
+        kept = kept[:half] + swap(kept[half:], "y", e)
+    return kept
 
 
 def solution(mesh):

time: 206 us -> 196 us (0.951)
  the two profiles are of different devices: /device:TPU:272 before, /device:TPU:256 now
where the time goes in v3:
time: 196 us; the launch traced here: 195 us
  waiting for transfers between devices  74.4 us (38%)
  blocking collectives  71.5 us (36%)
  starting transfers between devices  26.9 us (14%)
  Pallas kernels  16 us (8%)
  local copies, waits for them, and re-layouts  5.16 us (3%)
    all_to_all x1, blocking collectives, body(): lax.all_to_all(parts, ('zl', 'x'), 0, 0, tiled=True).reshape(NZ, -1, width)  71.5 us
    all_to_all x1, waiting for transfers between devices, body(): half = lax.all_to_all(load, 'x', 0, 0, tiled=True)  56.1 us
    ppermute x6, waiting for transfers between devices, swap(): return lax.ppermute(v, axis, [(i, i ^ e) for i in range(SIZES[axis])])  18.4 us
    ppermute x6, starting transfers between devices, swap(): return lax.ppermute(v, axis, [(i, i ^ e) for i in range(SIZES[axis])])  16.8 us
    pallas_call x1, Pallas kernels, early(): pl.pallas_call(functools.partial(early_kernel, slots), out_shape=[half] *...  8.51 us
    pallas_call x1, Pallas kernels, late(): pl.pallas_call(functools.partial(late_kernel, slots), out_shape=[jax.Shap...  5.26 us
    ppermute x4, starting transfers between devices, body(): lax.ppermute(piece, ('zh', 'x'), [(i, NX + (i ^ e)) for i in range(NX)])  5.17 us
    all_to_all x1, starting transfers between devices, body(): half = lax.all_to_all(load, 'x', 0, 0, tiled=True)  4.86 us
  transfers between devices with their start and end apart: 11, of which 6 were waited for; matrix products, arithmetic and copies ran while one was open for 1% of the time, Pallas kernels for 4%

profile of v3, /device:TPU:256, one launch (start us, length us, event | category | flops | bytes accessed | tf_op | source)
XLA Modules:
  0.0 195.4 jit_solution(14088136290402181735)
XLA Ops:
  0.0 0.8 copy.11.pairs
  0.8 1.4 copy.18
  2.1 2.2 %shard_map.28 = (bf16[4,2064,256]{2,1,0:T(8,128)(2,1)S(1)}, bf16[4,64,512]{2,1,0:T(8,128)(2,1)S(1)}, bf16[4,64,512]{2,1,0:T(8,128)(2,1)S(1)}, bf16[4,64,512]{2,1,0:T(8,128)(2,1)S(1)}, bf16[4,64,512]{2,1,0:T(8,128)(2,1)S(1)}) custom-call(s32[1]{0:T(128)} %bitcast.3.meta, s32[16,2]{1,0:T(8,128)S(1)} %copy.11.pairs, bf16[4,512,256]{2,1,0:T(8,128)(2,1)S(1)} %bitcast.46), custom_call_target="tpu_custom_call" | custom-call | tf_op jit(solution)/shard_map/pallas_call | solution.py:58
  4.3 0.0 copy-start
  4.3 2.0 %copy-done = bf16[4,2064,256]{2,1,0:T(8,128)(2,1)} copy-done((bf16[4,2064,256]{2,1,0:T(8,128)(2,1)}, bf16[4,2064,256]{2,1,0:T(8,128)(2,1)S(1)}, u32[]{:S(2)}) %copy-start) | copy-done | bytes 4227096
  6.3 4.9 %all-to-all-start = ((bf16[4,2064,256]{2,1,0:T(8,128)(2,1)}), bf16[4,2064,256]{2,1,0:T(8,128)(2,1)}, u32[]{:S(2)}, u32[]{:S(2)}) async-start(bf16[4,2064,256]{2,1,0:T(8,128)(2,1)} %copy-done), calls=%async_computation | async-start | bytes 8454144 | tf_op jit(solution)/shard_map/all_to_all | solution.py:197
  11.2 1.3 collective-permute-start
  12.5 1.3 collective-permute-start.1
  13.8 1.3 collective-permute-start.2
  15.1 1.3 collective-permute-start.3
  16.4 56.1 %all-to-all-done.source = bf16[4,2064,256]{2,1,0:T(8,128)(2,1)} async-done(((bf16[4,2064,256]{2,1,0:T(8,128)(2,1)}), bf16[4,2064,256]{2,1,0:T(8,128)(2,1)}, u32[]{:S(2)}, u32[]{:S(2)}) %all-to-all-start) | async-done | bytes 4227104 | tf_op jit(solution)/shard_map/all_to_all | solution.py:197
  72.5 0.7 slice.45
  73.2 0.1 maximum_and_fusion
  73.3 0.1 copy.14
  73.4 0.1 copy.16
  73.5 0.1 concatenate.6.meta
  73.6 8.5 %shard_map.29 = (f32[2048,128]{1,0:T(8,128)S(1)}, f32[2048,128]{1,0:T(8,128)S(1)}, f32[2048,128]{1,0:T(8,128)S(1)}, f32[2048,128]{1,0:T(8,128)S(1)}, bf16[16,512,256]{2,1,0:T(8,128)(2,1)S(1)}) custom-call(s32[200]{0:T(256)S(1)} %concatenate.6.meta, bf16[4,2064,256]{2,1,0:T(8,128)(2,1)} %all-to-all-done.source), custom_call_target="tpu_custom_call" | custom-call | tf_op jit(solution)/shard_map/pallas_call | solution.py:157
  82.1 0.0 collective-permute-done.refs_0_
  82.1 0.0 collective-permute-done.1.refs_1_
  82.1 0.0 collective-permute-done.2.refs_2_
  82.1 0.0 collective-permute-done.3.refs_3_
  82.1 5.3 %shard_map.30 = (f32[2048,128]{1,0:T(8,128)S(1)}, f32[2048,128]{1,0:T(8,128)S(1)}, f32[2048,128]{1,0:T(8,128)S(1)}, f32[2048,128]{1,0:T(8,128)S(1)}) custom-call(s32[200]{0:T(256)S(1)} %concatenate.6.meta, bf16[16,512,256]{2,1,0:T(8,128)(2,1)S(1)} %get-tuple-element.20.cols, ...), custom_call_target="tpu_custom_call", output_to_operand_aliasing={{0}: (6, {}), {1}: (7, {}), {2}: (8, {}), {3}: (9, {})} | custom-call | tf_op jit(solution)/shard_map/pallas_call | solution.py:172
  87.4 1.9 collective-permute-start.4
  89.3 2.4 %collective-permute-start.7 = (f32[2048,128]{1,0:T(8,128)S(1)}, f32[2048,128]{1,0:T(8,128)S(1)}, u32[]{:S(2)}, u32[]{:S(2)}) collective-permute-start(f32[2048,128]{1,0:T(8,128)S(1)} %get-tuple-element.32), channel_id=1, source_target_pairs={{0,8},{8,0},{1,9},{9,1},{2,10},{10,2},{3,11},{11,3},{4,12},{12,4},... | collective-permute-start | bytes 3145736 | tf_op jit(solution)/shard_map/ppermute | solution.py:20
  91.7 0.2 collective-permute-done.4
  91.9 0.1 add.43
  92.1 4.9 %collective-permute-start.5 = (f32[1024,128]{1,0:T(8,128)S(1)}, f32[1024,128]{1,0:T(8,128)S(1)}, u32[]{:S(2)}, u32[]{:S(2)}) collective-permute-start(f32[1024,128]{1,0:T(8,128)S(1)} %slice.49), channel_id=1, source_target_pairs={{0,384},{128,256},{256,128},{384,0},{1,385},{129,257},{257,129},{3... | collective-permute-start | bytes 1572872 | tf_op jit(solution)/shard_map/ppermute | solution.py:20
  97.0 0.0 collective-permute-done.7
  97.0 0.1 add.46
  97.2 2.0 %collective-permute-start.8 = (f32[1024,128]{1,0:T(8,128)S(1)}, f32[1024,128]{1,0:T(8,128)S(1)}, u32[]{:S(2)}, u32[]{:S(2)}) collective-permute-start(f32[1024,128]{1,0:T(8,128)S(1)} %slice.53), channel_id=1, source_target_pairs={{0,128},{128,0},{256,384},{384,256},{1,129},{129,1},{257,385},{385... | collective-permute-start | bytes 1572872 | tf_op jit(solution)/shard_map/ppermute | solution.py:20
  99.2 10.0 %collective-permute-done.5 = f32[1024,128]{1,0:T(8,128)S(1)} collective-permute-done((f32[1024,128]{1,0:T(8,128)S(1)}, f32[1024,128]{1,0:T(8,128)S(1)}, u32[]{:S(2)}, u32[]{:S(2)}) %collective-permute-start.5) | collective-permute-done | bytes 524320 | tf_op jit(solution)/shard_map/ppermute | solution.py:20
  109.2 0.1 slice_add_fusion.1
  109.3 2.2 %collective-permute-start.6 = (f32[512,128]{1,0:T(8,128)S(1)}, f32[512,128]{1,0:T(8,128)S(1)}, u32[]{:S(2)}, u32[]{:S(2)}) collective-permute-start(f32[512,128]{1,0:T(8,128)S(1)} %slice.51), channel_id=1, source_target_pairs={{0,128},{128,0},{256,384},{384,256},{1,129},{129,1},{257,385},{385... | collective-permute-start | bytes 786440 | tf_op jit(solution)/shard_map/ppermute | solution.py:20
  111.5 1.2 collective-permute-done.8
  112.8 0.1 slice_add_fusion
  112.9 3.3 %collective-permute-start.9 = (f32[512,128]{1,0:T(8,128)S(1)}, f32[512,128]{1,0:T(8,128)S(1)}, u32[]{:S(2)}, u32[]{:S(2)}) collective-permute-start(f32[512,128]{1,0:T(8,128)S(1)} %slice.55), channel_id=1, source_target_pairs={{0,384},{128,256},{256,128},{384,0},{1,385},{129,257},{257,129},{3... | collective-permute-start | bytes 786440 | tf_op jit(solution)/shard_map/ppermute | solution.py:20
  116.2 2.6 %collective-permute-done.6 = f32[512,128]{1,0:T(8,128)S(1)} collective-permute-done((f32[512,128]{1,0:T(8,128)S(1)}, f32[512,128]{1,0:T(8,128)S(1)}, u32[]{:S(2)}, u32[]{:S(2)}) %collective-permute-start.6) | collective-permute-done | bytes 262176 | tf_op jit(solution)/shard_map/ppermute | solution.py:20
  118.8 4.3 %collective-permute-done.9 = f32[512,128]{1,0:T(8,128)S(1)} collective-permute-done((f32[512,128]{1,0:T(8,128)S(1)}, f32[512,128]{1,0:T(8,128)S(1)}, u32[]{:S(2)}, u32[]{:S(2)}) %collective-permute-start.9) | collective-permute-done | bytes 262176 | tf_op jit(solution)/shard_map/ppermute | solution.py:20
  123.2 71.5 %all_to_all.10 = f32[32,16,256]{2,1,0:T(8,128)S(1)} all-to-all(f32[32,16,256]{2,1,0:T(8,128)S(1)} %bitcast.47), channel_id=1, replica_groups=mesh['y'=4,'zl'=8,'core'=2,'zh'=2,'x'=4] {'zl','x'}, dimensions={0} | all-to-all | bytes 1048576 | tf_op jit(solution)/shard_map/all_to_all | solution.py:213
  194.8 0.6 multiply_bitcast_fusion
  (11 shorter events, 0.3 us)
Async XLA Ops:
  4.3 2.0 %copy-start = (bf16[4,2064,256]{2,1,0:T(8,128)(2,1)}, bf16[4,2064,256]{2,1,0:T(8,128)(2,1)S(1)}, u32[]{:S(2)}) copy-start(bf16[4,2064,256]{2,1,0:T(8,128)(2,1)S(1)} %get-tuple-element.19) | copy-start | bytes 12681220
  6.3 66.2 %all-to-all-start = ((bf16[4,2064,256]{2,1,0:T(8,128)(2,1)}), bf16[4,2064,256]{2,1,0:T(8,128)(2,1)}, u32[]{:S(2)}, u32[]{:S(2)}) async-start(bf16[4,2064,256]{2,1,0:T(8,128)(2,1)} %copy-done), calls=%async_computation | async-start | bytes 8454144 | tf_op jit(solution)/shard_map/all_to_all | solution.py:197
  11.2 70.9 %collective-permute-start = (bf16[4,64,512]{2,1,0:T(8,128)(2,1)S(1)}, bf16[4,64,512]{2,1,0:T(8,128)(2,1)S(1)}, u32[]{:S(2)}, u32[]{:S(2)}) collective-permute-start(bf16[4,64,512]{2,1,0:T(8,128)(2,1)S(1)} %get-tuple-element.21), channel_id=1, source_target_pairs={{0,4},{1,5},{2,6},{3,7},{8,12},{9,13},{10,14},{11,15},{16,20},{17,... | collective-permute-start | bytes 786440 | tf_op jit(solution)/shard_map/ppermute | solution.py:194
  12.5 69.6 %collective-permute-start.1 = (bf16[4,64,512]{2,1,0:T(8,128)(2,1)S(1)}, bf16[4,64,512]{2,1,0:T(8,128)(2,1)S(1)}, u32[]{:S(2)}, u32[]{:S(2)}) collective-permute-start(bf16[4,64,512]{2,1,0:T(8,128)(2,1)S(1)} %get-tuple-element.22), channel_id=1, source_target_pairs={{0,5},{1,4},{2,7},{3,6},{8,13},{9,12},{10,15},{11,14},{16,21},{17,... | collective-permute-start | bytes 786440 | tf_op jit(solution)/shard_map/ppermute | solution.py:194
  13.8 68.3 %collective-permute-start.2 = (bf16[4,64,512]{2,1,0:T(8,128)(2,1)S(1)}, bf16[4,64,512]{2,1,0:T(8,128)(2,1)S(1)}, u32[]{:S(2)}, u32[]{:S(2)}) collective-permute-start(bf16[4,64,512]{2,1,0:T(8,128)(2,1)S(1)} %get-tuple-element.23), channel_id=1, source_target_pairs={{0,6},{1,7},{2,4},{3,5},{8,14},{9,15},{10,12},{11,13},{16,22},{17,... | collective-permute-start | bytes 786440 | tf_op jit(solution)/shard_map/ppermute | solution.py:194
  15.1 67.0 %collective-permute-start.3 = (bf16[4,64,512]{2,1,0:T(8,128)(2,1)S(1)}, bf16[4,64,512]{2,1,0:T(8,128)(2,1)S(1)}, u32[]{:S(2)}, u32[]{:S(2)}) collective-permute-start(bf16[4,64,512]{2,1,0:T(8,128)(2,1)S(1)} %get-tuple-element.24), channel_id=1, source_target_pairs={{0,7},{1,6},{2,5},{3,4},{8,15},{9,14},{10,13},{11,12},{16,23},{17,... | collective-permute-start | bytes 786440 | tf_op jit(solution)/shard_map/ppermute | solution.py:194
  87.4 4.6 %collective-permute-start.4 = (f32[2048,128]{1,0:T(8,128)S(1)}, f32[2048,128]{1,0:T(8,128)S(1)}, u32[]{:S(2)}, u32[]{:S(2)}) collective-permute-start(f32[2048,128]{1,0:T(8,128)S(1)} %get-tuple-element.30), channel_id=1, source_target_pairs={{0,8},{8,0},{1,9},{9,1},{2,10},{10,2},{3,11},{11,3},{4,12},{12,4},... | collective-permute-start | bytes 3145736 | tf_op jit(solution)/shard_map/ppermute | solution.py:20
  89.3 7.7 %collective-permute-start.7 = (f32[2048,128]{1,0:T(8,128)S(1)}, f32[2048,128]{1,0:T(8,128)S(1)}, u32[]{:S(2)}, u32[]{:S(2)}) collective-permute-start(f32[2048,128]{1,0:T(8,128)S(1)} %get-tuple-element.32), channel_id=1, source_target_pairs={{0,8},{8,0},{1,9},{9,1},{2,10},{10,2},{3,11},{11,3},{4,12},{12,4},... | collective-permute-start | bytes 3145736 | tf_op jit(solution)/shard_map/ppermute | solution.py:20
  92.1 17.1 %collective-permute-start.5 = (f32[1024,128]{1,0:T(8,128)S(1)}, f32[1024,128]{1,0:T(8,128)S(1)}, u32[]{:S(2)}, u32[]{:S(2)}) collective-permute-start(f32[1024,128]{1,0:T(8,128)S(1)} %slice.49), channel_id=1, source_target_pairs={{0,384},{128,256},{256,128},{384,0},{1,385},{129,257},{257,129},{3... | collective-permute-start | bytes 1572872 | tf_op jit(solution)/shard_map/ppermute | solution.py:20
  97.2 15.6 %collective-permute-start.8 = (f32[1024,128]{1,0:T(8,128)S(1)}, f32[1024,128]{1,0:T(8,128)S(1)}, u32[]{:S(2)}, u32[]{:S(2)}) collective-permute-start(f32[1024,128]{1,0:T(8,128)S(1)} %slice.53), channel_id=1, source_target_pairs={{0,128},{128,0},{256,384},{384,256},{1,129},{129,1},{257,385},{385... | collective-permute-start | bytes 1572872 | tf_op jit(solution)/shard_map/ppermute | solution.py:20
  109.3 9.5 %collective-permute-start.6 = (f32[512,128]{1,0:T(8,128)S(1)}, f32[512,128]{1,0:T(8,128)S(1)}, u32[]{:S(2)}, u32[]{:S(2)}) collective-permute-start(f32[512,128]{1,0:T(8,128)S(1)} %slice.51), channel_id=1, source_target_pairs={{0,128},{128,0},{256,384},{384,256},{1,129},{129,1},{257,385},{385... | collective-permute-start | bytes 786440 | tf_op jit(solution)/shard_map/ppermute | solution.py:20
  112.9 10.3 %collective-permute-start.9 = (f32[512,128]{1,0:T(8,128)S(1)}, f32[512,128]{1,0:T(8,128)S(1)}, u32[]{:S(2)}, u32[]{:S(2)}) collective-permute-start(f32[512,128]{1,0:T(8,128)S(1)} %slice.55), channel_id=1, source_target_pairs={{0,384},{128,256},{256,128},{384,0},{1,385},{129,257},{257,129},{3... | collective-permute-start | bytes 786440 | tf_op jit(solution)/shard_map/ppermute | solution.py:20

commit v4 on v3

--- a/solution.py
+++ b/solution.py
@@ -33,36 +33,29 @@
     ).astype(jnp.bfloat16)
 
 
-def quarters_kernel(meta, pairs, own, load, *outs):
+def quarters_kernel(meta, own, *outs):
+    for d in range(NX):
+        picker = quarter_picker(meta[0] ^ d, own.shape[2])
+        for b in range(own.shape[0]):
+            outs[d][b] = pick(picker, own[b])
+
+
+def quarters(x, own):
     blocks, tokens, width = own.shape
-    for d in range(NX):
-        picker = quarter_picker(meta[0] ^ d, width)
-        for b in range(blocks):
-            outs[d][b] = pick(picker, own[b])
-    slots = pairs.shape[0]
-    slot = lax.broadcasted_iota(jnp.int32, (slots, width), 0)
-    lane = lax.broadcasted_iota(jnp.int32, (slots, width), 1)
-    table = jnp.zeros((slots, width), jnp.int32)
-    for k in range(slots):
-        table = jnp.where(slot == k, jnp.where(lane == 0, pairs[k, 0], pairs[k, 1]), table)
-    table = table.astype(jnp.float32).astype(jnp.bfloat16)
-    for d in range(NX):
-        for b in range(blocks):
-            load[d, b * tokens : (b + 1) * tokens] = own[b]
-        load[d, blocks * tokens :] = table
-
-
-def quarters(x, pairs, own):
-    blocks, tokens, width = own.shape
-    rows = blocks * tokens + pairs.shape[0]
     return pl.pallas_call(
         quarters_kernel,
-        out_shape=[jax.ShapeDtypeStruct((NX, rows, width), jnp.bfloat16)]
-        + [jax.ShapeDtypeStruct((blocks, QUARTER, tokens), jnp.bfloat16)] * NX,
-        in_specs=[SMEM, SMEM, VMEM],
-        out_specs=[VMEM] * (1 + NX),
+        out_shape=[jax.ShapeDtypeStruct((blocks, QUARTER, tokens), jnp.bfloat16)] * NX,
+        in_specs=[SMEM, VMEM],
+        out_specs=[VMEM] * NX,
         compiler_params=pltpu.CompilerParams(vmem_limit_bytes=16 << 20),
-    )(x[None].astype(jnp.int32), pairs, own)
+    )(x[None].astype(jnp.int32), own)
+
+
+def exchange(own, pairs):
+    blocks, tokens, width = own.shape
+    table = jnp.pad(pairs.astype(jnp.bfloat16), ((0, 0), (0, width - pairs.shape[1])))
+    load = jnp.concatenate([own.reshape(blocks * tokens, width), table])
+    return lax.all_to_all(jnp.broadcast_to(load, (NX, *load.shape)), "x", 0, 0, tiled=True)
 
 
 HEAD = 8
@@ -164,6 +157,7 @@
             pltpu.SemaphoreType.DMA((count,)),
         ],
         compiler_params=pltpu.CompilerParams(vmem_limit_bytes=24 << 20),
+        cost_estimate=pl.CostEstimate(flops=0, bytes_accessed=0, transcendentals=0),
     )(meta, source)
 
 
@@ -189,12 +183,19 @@
     zh, x = lax.axis_index("zh"), lax.axis_index("x")
 
     own = jnp.transpose(activations, (1, 0, 2))
-    load, *pieces = quarters(x, block_map[0], own)
+    pieces = quarters(x, own)
     low = [
         lax.ppermute(piece, ("zh", "x"), [(i, NX + (i ^ e)) for i in range(NX)])
         for e, piece in enumerate(pieces)
     ]
-    half = lax.all_to_all(load, "x", 0, 0, tiled=True)
+    rows = blocks * tokens + block_map.shape[1]
+    half = lax.cond(
+        block_map[0, 0, 0] >= -1,
+        exchange,
+        lambda own, pairs: jnp.zeros((NX, rows, width), own.dtype),
+        own,
+        block_map[0],
+    )
     pairs = half[:, blocks * tokens :, :2].astype(jnp.int32).reshape(-1, 2)
     slots = pairs.shape[0]
     row, col = jnp.maximum(pairs[:, 0], 0), jnp.maximum(pairs[:, 1], 0)

time: 196 us -> 189 us (0.964)
  waiting for transfers between devices: 74.4 us -> 18.4 us
  blocking collectives: 71.5 us -> 126 us
  starting transfers between devices: 26.9 us -> 22 us
  local copies, waits for them, and re-layouts: 5.16 us -> 2.53 us
    all_to_all x0 -> x1, blocking collectives: none -> 67 us  [exchange(): lax.all_to_all(jnp.broadcast_to(load, (NX, *load.shape)), 'x', 0, 0, tile...]
    all_to_all x1 -> x0, waiting for transfers between devices: 56.1 us -> none  [body(): half = lax.all_to_all(load, 'x', 0, 0, tiled=True)]
    all_to_all x1, blocking collectives: 71.5 us -> 59 us  [body(): lax.all_to_all(parts, ('zl', 'x'), 0, 0, tiled=True).reshape(NZ, -1, width)]
    all_to_all x1 -> x0, starting transfers between devices: 4.86 us -> none  [body(): half = lax.all_to_all(load, 'x', 0, 0, tiled=True)]
    unnamed x5 -> x3, local copies, waits for them, and re-layouts: 3.49 us -> 1.38 us
  transfers between devices with their start and end apart: 11 -> 10, of which waited for: 6 -> 5; matrix products, arithmetic and copies ran while one was open for 1% -> 1% of each run, Pallas kernels for 4% -> 5%
where the time goes in v4:
time: 189 us
  blocking collectives  126 us (67%)
  starting transfers between devices  22 us (12%)
  waiting for transfers between devices  18.4 us (10%)
  Pallas kernels  17.2 us (9%)
  local copies, waits for them, and re-layouts  2.53 us (1%)
  other arithmetic  1.94 us (1%)
    all_to_all x1, blocking collectives, exchange(): lax.all_to_all(jnp.broadcast_to(load, (NX, *load.shape)), 'x', 0, 0, tile...  67 us
    all_to_all x1, blocking collectives, body(): lax.all_to_all(parts, ('zl', 'x'), 0, 0, tiled=True).reshape(NZ, -1, width)  59 us
    ppermute x6, waiting for transfers between devices, swap(): return lax.ppermute(v, axis, [(i, i ^ e) for i in range(SIZES[axis])])  18.4 us
    ppermute x6, starting transfers between devices, swap(): return lax.ppermute(v, axis, [(i, i ^ e) for i in range(SIZES[axis])])  16.8 us
    pallas_call x1, Pallas kernels, early(): pl.pallas_call(functools.partial(early_kernel, slots), out_shape=[half] *...  9.39 us
    pallas_call x1, Pallas kernels, late(): pl.pallas_call(functools.partial(late_kernel, slots), out_shape=[jax.Shap...  6.39 us
    ppermute x4, starting transfers between devices, body(): lax.ppermute(piece, ('zh', 'x'), [(i, NX + (i ^ e)) for i in range(NX)])  5.17 us
  transfers between devices with their start and end apart: 10, of which 5 were waited for; matrix products, arithmetic and copies ran while one was open for 1% of the time, Pallas kernels for 5%

profile of v4, /device:TPU:256, one launch (start us, length us, event | category | flops | bytes accessed | tf_op | source)
XLA Modules:
  0.0 188.9 jit_solution(15042738658747307488)
XLA Ops:
  0.0 0.0 copy-start
  0.0 1.4 copy.18
  1.4 1.4 shard_map.29
  2.8 1.3 collective-permute-start
  4.1 1.3 collective-permute-start.1
  5.4 1.3 collective-permute-start.2
  6.7 1.3 collective-permute-start.3
  8.0 0.0 copy-done
  8.0 0.5 slice.37
  9.1 67.5 %conditional.1 = (bf16[4,2064,256]{2,1,0:T(8,128)(2,1)}) conditional(s32[]{:T(128)} %bitcast.7, () %tuple.11, (bf16[4,512,256]{2,1,0:T(8,128)(2,1)S(1)}, s32[1,16,2]{1,2,0:T(2,128)S(1)}) %tuple.18), branch_computations={%region_0.0_spmd, %region_1.2_spmd} | conditional | flops 3170336 | bytes 15843720 | solution.py:192
  9.2 0.1 copy.13
  9.3 0.1 fusion.1
  9.3 0.3 broadcast_in_dim.7
  9.6 67.0 %all_to_all.9 = bf16[4,2064,256]{2,1,0:T(8,128)(2,1)} all-to-all(bf16[4,2064,256]{2,1,0:T(8,128)(2,1)S(1)} %broadcast_in_dim.7), channel_id=1, replica_groups=mesh['y'=4,'zl'=8,'core'=2,'zh'=2,'x'=4] {'x'}, dimensions={0} | all-to-all | bytes 8454144 | tf_op jit(solution)/shard_map/cond/branch_1_fun/all_to_all | solution.py:58
  76.6 0.7 slice_convert_fusion
  77.3 0.1 copy.17
  77.5 0.1 concatenate.9.meta
  77.6 9.4 %shard_map.28 = (f32[2048,128]{1,0:T(8,128)S(1)}, f32[2048,128]{1,0:T(8,128)S(1)}, f32[2048,128]{1,0:T(8,128)S(1)}, f32[2048,128]{1,0:T(8,128)S(1)}, bf16[16,512,256]{2,1,0:T(8,128)(2,1)S(1)}) custom-call(s32[200]{0:T(256)S(1)} %concatenate.9.meta, bf16[4,2064,256]{2,1,0:T(8,128)(2,1)} %get-tuple-element.45.source), custom_call_target="tpu_custom_call" | custom-call | tf_op jit(solution)/shard_map/pallas_call | solution.py:150
  87.0 0.0 collective-permute-done.refs_0_
  87.0 0.0 collective-permute-done.1.refs_1_
  87.0 0.0 collective-permute-done.2.refs_2_
  87.0 0.0 collective-permute-done.3.refs_3_
  87.0 6.4 %shard_map.30 = (f32[2048,128]{1,0:T(8,128)S(1)}, f32[2048,128]{1,0:T(8,128)S(1)}, f32[2048,128]{1,0:T(8,128)S(1)}, f32[2048,128]{1,0:T(8,128)S(1)}) custom-call(s32[200]{0:T(256)S(1)} %concatenate.9.meta, bf16[16,512,256]{2,1,0:T(8,128)(2,1)S(1)} %get-tuple-element.28.cols, ...), custom_call_target="tpu_custom_call", output_to_operand_aliasing={{0}: (6, {}), {1}: (7, {}), {2}: (8, {}), {3}: (9, {})} | custom-call | tf_op jit(solution)/shard_map/pallas_call | solution.py:166
  93.4 1.9 %collective-permute-start.4 = (f32[2048,128]{1,0:T(8,128)S(1)}, f32[2048,128]{1,0:T(8,128)S(1)}, u32[]{:S(2)}, u32[]{:S(2)}) collective-permute-start(f32[2048,128]{1,0:T(8,128)S(1)} %get-tuple-element.38), channel_id=1, source_target_pairs={{0,8},{8,0},{1,9},{9,1},{2,10},{10,2},{3,11},{11,3},{4,12},{12,4},... | collective-permute-start | bytes 3145736 | tf_op jit(solution)/shard_map/ppermute | solution.py:20
  95.3 2.4 %collective-permute-start.7 = (f32[2048,128]{1,0:T(8,128)S(1)}, f32[2048,128]{1,0:T(8,128)S(1)}, u32[]{:S(2)}, u32[]{:S(2)}) collective-permute-start(f32[2048,128]{1,0:T(8,128)S(1)} %get-tuple-element.40), channel_id=1, source_target_pairs={{0,8},{8,0},{1,9},{9,1},{2,10},{10,2},{3,11},{11,3},{4,12},{12,4},... | collective-permute-start | bytes 3145736 | tf_op jit(solution)/shard_map/ppermute | solution.py:20
  97.7 0.2 collective-permute-done.4
  97.9 0.1 add.45
  98.1 4.9 %collective-permute-start.5 = (f32[1024,128]{1,0:T(8,128)S(1)}, f32[1024,128]{1,0:T(8,128)S(1)}, u32[]{:S(2)}, u32[]{:S(2)}) collective-permute-start(f32[1024,128]{1,0:T(8,128)S(1)} %slice.51), channel_id=1, source_target_pairs={{0,384},{128,256},{256,128},{384,0},{1,385},{129,257},{257,129},{3... | collective-permute-start | bytes 1572872 | tf_op jit(solution)/shard_map/ppermute | solution.py:20
  103.0 0.0 collective-permute-done.7
  103.0 0.1 add.48
  103.2 2.0 %collective-permute-start.8 = (f32[1024,128]{1,0:T(8,128)S(1)}, f32[1024,128]{1,0:T(8,128)S(1)}, u32[]{:S(2)}, u32[]{:S(2)}) collective-permute-start(f32[1024,128]{1,0:T(8,128)S(1)} %slice.55), channel_id=1, source_target_pairs={{0,128},{128,0},{256,384},{384,256},{1,129},{129,1},{257,385},{385... | collective-permute-start | bytes 1572872 | tf_op jit(solution)/shard_map/ppermute | solution.py:20
  105.3 10.0 %collective-permute-done.5 = f32[1024,128]{1,0:T(8,128)S(1)} collective-permute-done((f32[1024,128]{1,0:T(8,128)S(1)}, f32[1024,128]{1,0:T(8,128)S(1)}, u32[]{:S(2)}, u32[]{:S(2)}) %collective-permute-start.5) | collective-permute-done | bytes 524320 | tf_op jit(solution)/shard_map/ppermute | solution.py:20
  115.2 0.1 slice_add_fusion.1
  115.3 2.2 %collective-permute-start.6 = (f32[512,128]{1,0:T(8,128)S(1)}, f32[512,128]{1,0:T(8,128)S(1)}, u32[]{:S(2)}, u32[]{:S(2)}) collective-permute-start(f32[512,128]{1,0:T(8,128)S(1)} %slice.53), channel_id=1, source_target_pairs={{0,128},{128,0},{256,384},{384,256},{1,129},{129,1},{257,385},{385... | collective-permute-start | bytes 786440 | tf_op jit(solution)/shard_map/ppermute | solution.py:20
  117.5 1.2 collective-permute-done.8
  118.8 0.1 slice_add_fusion
  118.9 3.3 %collective-permute-start.9 = (f32[512,128]{1,0:T(8,128)S(1)}, f32[512,128]{1,0:T(8,128)S(1)}, u32[]{:S(2)}, u32[]{:S(2)}) collective-permute-start(f32[512,128]{1,0:T(8,128)S(1)} %slice.57), channel_id=1, source_target_pairs={{0,384},{128,256},{256,128},{384,0},{1,385},{129,257},{257,129},{3... | collective-permute-start | bytes 786440 | tf_op jit(solution)/shard_map/ppermute | solution.py:20
  122.2 2.6 %collective-permute-done.6 = f32[512,128]{1,0:T(8,128)S(1)} collective-permute-done((f32[512,128]{1,0:T(8,128)S(1)}, f32[512,128]{1,0:T(8,128)S(1)}, u32[]{:S(2)}, u32[]{:S(2)}) %collective-permute-start.6) | collective-permute-done | bytes 262176 | tf_op jit(solution)/shard_map/ppermute | solution.py:20
  124.9 4.3 %collective-permute-done.9 = f32[512,128]{1,0:T(8,128)S(1)} collective-permute-done((f32[512,128]{1,0:T(8,128)S(1)}, f32[512,128]{1,0:T(8,128)S(1)}, u32[]{:S(2)}, u32[]{:S(2)}) %collective-permute-start.9) | collective-permute-done | bytes 262176 | tf_op jit(solution)/shard_map/ppermute | solution.py:20
  129.3 59.0 %all_to_all.10 = f32[32,16,256]{2,1,0:T(8,128)S(1)} all-to-all(f32[32,16,256]{2,1,0:T(8,128)S(1)} %bitcast.36), channel_id=1, replica_groups=mesh['y'=4,'zl'=8,'core'=2,'zh'=2,'x'=4] {'zl','x'}, dimensions={0} | all-to-all | bytes 1048576 | tf_op jit(solution)/shard_map/all_to_all | solution.py:214
  188.3 0.6 multiply_bitcast_fusion
  (12 shorter events, 0.3 us)
Async XLA Ops:
  0.0 8.0 %copy-start = (s32[1,16,2]{1,2,0:T(2,128)S(1)}, s32[1,16,2]{1,2,0:T(2,128)}, u32[]{:S(2)}) copy-start(s32[1,16,2]{1,2,0:T(2,128)} %param.5) | copy-start | bytes 388
  2.8 84.2 %collective-permute-start = (bf16[4,64,512]{2,1,0:T(8,128)(2,1)S(1)}, bf16[4,64,512]{2,1,0:T(8,128)(2,1)S(1)}, u32[]{:S(2)}, u32[]{:S(2)}) collective-permute-start(bf16[4,64,512]{2,1,0:T(8,128)(2,1)S(1)} %get-tuple-element.29), channel_id=1, source_target_pairs={{0,4},{1,5},{2,6},{3,7},{8,12},{9,13},{10,14},{11,15},{16,20},{17,... | collective-permute-start | bytes 786440 | tf_op jit(solution)/shard_map/ppermute | solution.py:188
  4.1 82.9 %collective-permute-start.1 = (bf16[4,64,512]{2,1,0:T(8,128)(2,1)S(1)}, bf16[4,64,512]{2,1,0:T(8,128)(2,1)S(1)}, u32[]{:S(2)}, u32[]{:S(2)}) collective-permute-start(bf16[4,64,512]{2,1,0:T(8,128)(2,1)S(1)} %get-tuple-element.30), channel_id=1, source_target_pairs={{0,5},{1,4},{2,7},{3,6},{8,13},{9,12},{10,15},{11,14},{16,21},{17,... | collective-permute-start | bytes 786440 | tf_op jit(solution)/shard_map/ppermute | solution.py:188
  5.4 81.6 %collective-permute-start.2 = (bf16[4,64,512]{2,1,0:T(8,128)(2,1)S(1)}, bf16[4,64,512]{2,1,0:T(8,128)(2,1)S(1)}, u32[]{:S(2)}, u32[]{:S(2)}) collective-permute-start(bf16[4,64,512]{2,1,0:T(8,128)(2,1)S(1)} %get-tuple-element.31), channel_id=1, source_target_pairs={{0,6},{1,7},{2,4},{3,5},{8,14},{9,15},{10,12},{11,13},{16,22},{17,... | collective-permute-start | bytes 786440 | tf_op jit(solution)/shard_map/ppermute | solution.py:188
  6.7 80.3 %collective-permute-start.3 = (bf16[4,64,512]{2,1,0:T(8,128)(2,1)S(1)}, bf16[4,64,512]{2,1,0:T(8,128)(2,1)S(1)}, u32[]{:S(2)}, u32[]{:S(2)}) collective-permute-start(bf16[4,64,512]{2,1,0:T(8,128)(2,1)S(1)} %get-tuple-element.32), channel_id=1, source_target_pairs={{0,7},{1,6},{2,5},{3,4},{8,15},{9,14},{10,13},{11,12},{16,23},{17,... | collective-permute-start | bytes 786440 | tf_op jit(solution)/shard_map/ppermute | solution.py:188
  93.4 4.6 %collective-permute-start.4 = (f32[2048,128]{1,0:T(8,128)S(1)}, f32[2048,128]{1,0:T(8,128)S(1)}, u32[]{:S(2)}, u32[]{:S(2)}) collective-permute-start(f32[2048,128]{1,0:T(8,128)S(1)} %get-tuple-element.38), channel_id=1, source_target_pairs={{0,8},{8,0},{1,9},{9,1},{2,10},{10,2},{3,11},{11,3},{4,12},{12,4},... | collective-permute-start | bytes 3145736 | tf_op jit(solution)/shard_map/ppermute | solution.py:20
  95.3 7.7 %collective-permute-start.7 = (f32[2048,128]{1,0:T(8,128)S(1)}, f32[2048,128]{1,0:T(8,128)S(1)}, u32[]{:S(2)}, u32[]{:S(2)}) collective-permute-start(f32[2048,128]{1,0:T(8,128)S(1)} %get-tuple-element.40), channel_id=1, source_target_pairs={{0,8},{8,0},{1,9},{9,1},{2,10},{10,2},{3,11},{11,3},{4,12},{12,4},... | collective-permute-start | bytes 3145736 | tf_op jit(solution)/shard_map/ppermute | solution.py:20
  98.1 17.1 %collective-permute-start.5 = (f32[1024,128]{1,0:T(8,128)S(1)}, f32[1024,128]{1,0:T(8,128)S(1)}, u32[]{:S(2)}, u32[]{:S(2)}) collective-permute-start(f32[1024,128]{1,0:T(8,128)S(1)} %slice.51), channel_id=1, source_target_pairs={{0,384},{128,256},{256,128},{384,0},{1,385},{129,257},{257,129},{3... | collective-permute-start | bytes 1572872 | tf_op jit(solution)/shard_map/ppermute | solution.py:20
  103.2 15.6 %collective-permute-start.8 = (f32[1024,128]{1,0:T(8,128)S(1)}, f32[1024,128]{1,0:T(8,128)S(1)}, u32[]{:S(2)}, u32[]{:S(2)}) collective-permute-start(f32[1024,128]{1,0:T(8,128)S(1)} %slice.55), channel_id=1, source_target_pairs={{0,128},{128,0},{256,384},{384,256},{1,129},{129,1},{257,385},{385... | collective-permute-start | bytes 1572872 | tf_op jit(solution)/shard_map/ppermute | solution.py:20
  115.3 9.5 %collective-permute-start.6 = (f32[512,128]{1,0:T(8,128)S(1)}, f32[512,128]{1,0:T(8,128)S(1)}, u32[]{:S(2)}, u32[]{:S(2)}) collective-permute-start(f32[512,128]{1,0:T(8,128)S(1)} %slice.53), channel_id=1, source_target_pairs={{0,128},{128,0},{256,384},{384,256},{1,129},{129,1},{257,385},{385... | collective-permute-start | bytes 786440 | tf_op jit(solution)/shard_map/ppermute | solution.py:20
  118.9 10.3 %collective-permute-start.9 = (f32[512,128]{1,0:T(8,128)S(1)}, f32[512,128]{1,0:T(8,128)S(1)}, u32[]{:S(2)}, u32[]{:S(2)}) collective-permute-start(f32[512,128]{1,0:T(8,128)S(1)} %slice.57), channel_id=1, source_target_pairs={{0,384},{128,256},{256,128},{384,0},{1,385},{129,257},{257,129},{3... | collective-permute-start | bytes 786440 | tf_op jit(solution)/shard_map/ppermute | solution.py:20

commit v5 on v4

--- a/solution.py
+++ b/solution.py
@@ -8,7 +8,8 @@
 from jax.sharding import Mesh, PartitionSpec as P
 
 NY, NZ, NC, NH, NX = 4, 8, 2, 2, 4
-SIZES = {"y": NY, "zl": NZ, "core": NC, "x": NX}
+NP = NZ // 2
+SIZES = {"y": NY, "zi": 2, "core": NC, "x": NX}
 CUTS = 2
 QUARTER = 64
 VMEM = pl.BlockSpec(memory_space=pltpu.VMEM)
@@ -62,14 +63,16 @@
 
 
 def put(meta, n, product, keep, send):
-    y, core = meta[0], meta[2]
+    y, zi, core = meta[0], meta[1], meta[2]
     k = lax.rem(n, 16)
     e = k // 4 ^ y
-    groups = [e ^ (e >> 1), ((e ^ (e >> 1)) >> 1) | ((e & 1) ^ (e >> 1)) << 1]
+    group = e ^ (e >> 1)
     for half in range(2):
-        place = lax.rem(k, 4) * 2 + half
+        side = half ^ zi
+        starts = (group * 2 + side, side * 4 + group)
         for cut in range(CUTS):
-            at = pl.ds(pl.multiple_of(((groups[cut] * 8 + place) * NX + n // 16) * 16, 16), 16)
+            at = ((starts[cut] * NP + lax.rem(k, 4)) * NX + n // 16) * 16
+            at = pl.ds(pl.multiple_of(at, 16), 16)
             wide = keep[cut].shape[1]
             lanes = slice(cut * wide, (cut + 1) * wide)
             if product is None:
@@ -179,7 +182,7 @@
 
 def body(activations, block_map):
     tokens, blocks, width = activations.shape
-    y, zl, core = (lax.axis_index(a) for a in ("y", "zl", "core"))
+    y, zi, core = (lax.axis_index(a) for a in ("y", "zi", "core"))
     zh, x = lax.axis_index("zh"), lax.axis_index("x")
 
     own = jnp.transpose(activations, (1, 0, 2))
@@ -203,32 +206,33 @@
     kind = jnp.where(live, jnp.where(same, 1, 2), 0)
     row_at = jnp.where(same, row // blocks % NX, row // blocks % NX ^ x) * blocks + row % blocks
     col_at = col % (NX * blocks)
-    head = jnp.stack([y, zl, core, x, zh, zh, zh, zh])
+    head = jnp.stack([y, zi, core, x, zh, zh, zh, zh])
     meta = jnp.concatenate([head, kind, row_at, col_at]).astype(jnp.int32)
 
     *halves, cols = early(meta, half, NX * blocks, tokens, slots)
     halves = late(meta, cols, low, halves, slots)
     scale = 2.0 / (tokens * NY * NZ * NC)
-    cuts = [total(keep, send, order) for keep, send, order in zip(halves[:CUTS], halves[CUTS:], ((3, 1), (1, 3)))]
-    parts = jnp.concatenate(cuts, axis=1).reshape(NZ * NX, -1, width)
-    parts = lax.all_to_all(parts, ("zl", "x"), 0, 0, tiled=True).reshape(NZ, -1, width)
+    orders = ((("y", 3), ("y", 1), ("zi", 1)), (("zi", 1), ("y", 3), ("y", 1)))
+    cuts = [total(*cut) for cut in zip(halves[:CUTS], halves[CUTS:], orders)]
+    parts = jnp.concatenate(cuts, axis=1).reshape(NP * NX, -1, width)
+    parts = lax.all_to_all(parts, ("zp", "x"), 0, 0, tiled=True).reshape(NP, -1, width)
     return jnp.sum(parts, axis=0)[None] * scale
 
 
 def total(keep, send, order):
     kept = keep + swap(send, "core", 1)
-    for e in order:
+    for axis, e in order:
         half = kept.shape[0] // 2
-        kept = kept[:half] + swap(kept[half:], "y", e)
+        kept = kept[:half] + swap(kept[half:], axis, e)
     return kept
 
 
 def solution(mesh):
-    grid = Mesh(mesh.devices.reshape(NY, NZ, NC, NH, NX), ("y", "zl", "core", "zh", "x"))
-    tok, slab = ("y", "zl", "core"), ("zh", "x")
+    grid = mesh.devices.reshape(NY, NP, 2, NC, NH, NX)
+    tok, slab = ("y", "zp", "zi", "core"), ("zh", "x")
     return jax.shard_map(
         body,
-        mesh=grid,
+        mesh=Mesh(grid, tok + slab),
         in_specs=(P(tok, slab, None), P(slab, None, None)),
         out_specs=P(slab, tok, None),
         check_vma=False,

time: 189 us -> 184 us (0.974)
  blocking collectives: 126 us -> 88.1 us
  starting transfers between devices: 22 us -> 56.5 us
  waiting for transfers between devices: 18.4 us -> 15.9 us
    all_to_all x1, blocking collectives: 59 us -> 21.1 us  [body(): lax.all_to_all(parts, ('zp', 'x'), 0, 0, tiled=True).reshape(NP, -1, width)]
    ppermute x6 -> x8, starting transfers between devices: 16.8 us -> 51.3 us  [swap(): return lax.ppermute(v, axis, [(i, i ^ e) for i in range(SIZES[axis])])]
    ppermute x6 -> x8, waiting for transfers between devices: 18.4 us -> 15.9 us  [swap(): return lax.ppermute(v, axis, [(i, i ^ e) for i in range(SIZES[axis])])]
  transfers between devices with their start and end apart: 10 -> 12, of which waited for: 5 -> 4; matrix products, arithmetic and copies ran while one was open for 1% -> 1% of each run, Pallas kernels for 5% -> 5%
where the time goes in v5:
time: 184 us; the launch traced here: 183 us
  blocking collectives  88.1 us (48%)
  starting transfers between devices  56.5 us (31%)
  Pallas kernels  17.1 us (9%)
  waiting for transfers between devices  15.9 us (9%)
  local copies, waits for them, and re-layouts  2.56 us (1%)
  other arithmetic  1.93 us (1%)
    all_to_all x1, blocking collectives, exchange(): lax.all_to_all(jnp.broadcast_to(load, (NX, *load.shape)), 'x', 0, 0, tile...  67 us
    ppermute x8, starting transfers between devices, swap(): return lax.ppermute(v, axis, [(i, i ^ e) for i in range(SIZES[axis])])  51.3 us
    all_to_all x1, blocking collectives, body(): lax.all_to_all(parts, ('zp', 'x'), 0, 0, tiled=True).reshape(NP, -1, width)  21.1 us
    ppermute x8, waiting for transfers between devices, swap(): return lax.ppermute(v, axis, [(i, i ^ e) for i in range(SIZES[axis])])  15.9 us
    pallas_call x1, Pallas kernels, early(): pl.pallas_call(functools.partial(early_kernel, slots), out_shape=[half] *...  9.84 us
    pallas_call x1, Pallas kernels, late(): pl.pallas_call(functools.partial(late_kernel, slots), out_shape=[jax.Shap...  5.9 us
    ppermute x4, starting transfers between devices, body(): lax.ppermute(piece, ('zh', 'x'), [(i, NX + (i ^ e)) for i in range(NX)])  5.17 us
  transfers between devices with their start and end apart: 12, of which 4 were waited for; matrix products, arithmetic and copies ran while one was open for 1% of the time, Pallas kernels for 5%

profile of v5, /device:TPU:256, one launch (start us, length us, event | category | flops | bytes accessed | tf_op | source)
XLA Modules:
  0.0 183.1 jit_solution(16481343036085070879)
XLA Ops:
  0.0 0.0 copy-start
  0.0 1.4 copy.18
  1.4 1.4 shard_map.29
  2.8 1.3 collective-permute-start
  4.1 1.3 collective-permute-start.1
  5.4 1.3 collective-permute-start.2
  6.7 1.3 collective-permute-start.3
  8.0 0.0 copy-done
  8.0 0.5 slice.49
  9.1 67.5 %conditional.1 = (bf16[4,2064,256]{2,1,0:T(8,128)(2,1)}) conditional(s32[]{:T(128)} %bitcast.7, () %tuple.11, (bf16[4,512,256]{2,1,0:T(8,128)(2,1)S(1)}, s32[1,16,2]{1,2,0:T(2,128)S(1)}) %tuple.18), branch_computations={%region_0.0_spmd, %region_1.2_spmd} | conditional | flops 3170336 | bytes 15843720 | solution.py:195
  9.2 0.1 copy.13
  9.3 0.1 fusion.1
  9.3 0.3 broadcast_in_dim.7
  9.6 67.0 %all_to_all.9 = bf16[4,2064,256]{2,1,0:T(8,128)(2,1)} all-to-all(bf16[4,2064,256]{2,1,0:T(8,128)(2,1)S(1)} %broadcast_in_dim.7), channel_id=1, replica_groups=mesh['y'=4,'zp'=4,'zi'=2,'core'=2,'zh'=2,'x'=4] {'x'}, dimensions={0} | all-to-all | bytes 8454144 | tf_op jit(solution)/shard_map/cond/branch_1_fun/all_to_all | solution.py:59
  76.6 0.7 slice_convert_fusion
  77.3 0.1 copy.17
  77.5 0.1 concatenate.9.meta
  77.6 9.8 %shard_map.28 = (f32[2048,128]{1,0:T(8,128)S(1)}, f32[2048,128]{1,0:T(8,128)S(1)}, f32[2048,128]{1,0:T(8,128)S(1)}, f32[2048,128]{1,0:T(8,128)S(1)}, bf16[16,512,256]{2,1,0:T(8,128)(2,1)S(1)}) custom-call(s32[200]{0:T(256)S(1)} %concatenate.9.meta, bf16[4,2064,256]{2,1,0:T(8,128)(2,1)} %get-tuple-element.45.source), custom_call_target="tpu_custom_call" | custom-call | tf_op jit(solution)/shard_map/pallas_call | solution.py:153
  87.4 0.0 collective-permute-done.refs_0_
  87.4 0.0 collective-permute-done.1.refs_1_
  87.4 0.0 collective-permute-done.2.refs_2_
  87.4 0.0 collective-permute-done.3.refs_3_
  87.4 5.9 %shard_map.30 = (f32[2048,128]{1,0:T(8,128)S(1)}, f32[2048,128]{1,0:T(8,128)S(1)}, f32[2048,128]{1,0:T(8,128)S(1)}, f32[2048,128]{1,0:T(8,128)S(1)}) custom-call(s32[200]{0:T(256)S(1)} %concatenate.9.meta, bf16[16,512,256]{2,1,0:T(8,128)(2,1)S(1)} %get-tuple-element.28.cols, ...), custom_call_target="tpu_custom_call", output_to_operand_aliasing={{0}: (6, {}), {1}: (7, {}), {2}: (8, {}), {3}: (9, {})} | custom-call | tf_op jit(solution)/shard_map/pallas_call | solution.py:169
  93.3 1.9 %collective-permute-start.4 = (f32[2048,128]{1,0:T(8,128)S(1)}, f32[2048,128]{1,0:T(8,128)S(1)}, u32[]{:S(2)}, u32[]{:S(2)}) collective-permute-start(f32[2048,128]{1,0:T(8,128)S(1)} %get-tuple-element.38), channel_id=1, source_target_pairs={{0,8},{8,0},{1,9},{9,1},{2,10},{10,2},{3,11},{11,3},{4,12},{12,4},... | collective-permute-start | bytes 3145736 | tf_op jit(solution)/shard_map/ppermute | solution.py:21
  95.3 2.4 %collective-permute-start.8 = (f32[2048,128]{1,0:T(8,128)S(1)}, f32[2048,128]{1,0:T(8,128)S(1)}, u32[]{:S(2)}, u32[]{:S(2)}) collective-permute-start(f32[2048,128]{1,0:T(8,128)S(1)} %get-tuple-element.40), channel_id=1, source_target_pairs={{0,8},{8,0},{1,9},{9,1},{2,10},{10,2},{3,11},{11,3},{4,12},{12,4},... | collective-permute-start | bytes 3145736 | tf_op jit(solution)/shard_map/ppermute | solution.py:21
  97.7 0.2 collective-permute-done.4
  97.9 0.1 add.51
  98.1 4.9 %collective-permute-start.5 = (f32[1024,128]{1,0:T(8,128)S(1)}, f32[1024,128]{1,0:T(8,128)S(1)}, u32[]{:S(2)}, u32[]{:S(2)}) collective-permute-start(f32[1024,128]{1,0:T(8,128)S(1)} %slice.67), channel_id=1, source_target_pairs={{0,384},{128,256},{256,128},{384,0},{1,385},{129,257},{257,129},{3... | collective-permute-start | bytes 1572872 | tf_op jit(solution)/shard_map/ppermute | solution.py:21
  103.0 0.0 collective-permute-done.8
  103.0 0.1 add.55
  103.2 28.6 %collective-permute-start.9 = (f32[1024,128]{1,0:T(8,128)S(1)}, f32[1024,128]{1,0:T(8,128)S(1)}, u32[]{:S(2)}, u32[]{:S(2)}) collective-permute-start(f32[1024,128]{1,0:T(8,128)S(1)} %slice.73), channel_id=1, source_target_pairs={{0,16},{16,0},{1,17},{17,1},{2,18},{18,2},{3,19},{19,3},{4,20},{20... | collective-permute-start | bytes 1572872 | tf_op jit(solution)/shard_map/ppermute | solution.py:21
  131.7 0.0 collective-permute-done.5
  131.7 0.1 slice_add_fusion.1
  131.8 2.0 %collective-permute-start.6 = (f32[512,128]{1,0:T(8,128)S(1)}, f32[512,128]{1,0:T(8,128)S(1)}, u32[]{:S(2)}, u32[]{:S(2)}) collective-permute-start(f32[512,128]{1,0:T(8,128)S(1)} %slice.69), channel_id=1, source_target_pairs={{0,128},{128,0},{256,384},{384,256},{1,129},{129,1},{257,385},{385... | collective-permute-start | bytes 786440 | tf_op jit(solution)/shard_map/ppermute | solution.py:21
  133.9 9.8 %collective-permute-done.9 = f32[1024,128]{1,0:T(8,128)S(1)} collective-permute-done((f32[1024,128]{1,0:T(8,128)S(1)}, f32[1024,128]{1,0:T(8,128)S(1)}, u32[]{:S(2)}, u32[]{:S(2)}) %collective-permute-start.9) | collective-permute-done | bytes 524320 | tf_op jit(solution)/shard_map/ppermute | solution.py:21
  143.7 0.1 slice_add_fusion
  143.7 2.4 %collective-permute-start.10 = (f32[512,128]{1,0:T(8,128)S(1)}, f32[512,128]{1,0:T(8,128)S(1)}, u32[]{:S(2)}, u32[]{:S(2)}) collective-permute-start(f32[512,128]{1,0:T(8,128)S(1)} %slice.75), channel_id=1, source_target_pairs={{0,384},{128,256},{256,128},{384,0},{1,385},{129,257},{257,129},{3... | collective-permute-start | bytes 786440 | tf_op jit(solution)/shard_map/ppermute | solution.py:21
  146.1 0.0 collective-permute-done.6
  146.2 7.2 %collective-permute-start.7 = (f32[256,128]{1,0:T(8,128)S(1)}, f32[256,128]{1,0:T(8,128)S(1)}, u32[]{:S(2)}, u32[]{:S(2)}) collective-permute-start(f32[256,128]{1,0:T(8,128)S(1)} %slice.71), channel_id=1, source_target_pairs={{0,16},{16,0},{1,17},{17,1},{2,18},{18,2},{3,19},{19,3},{4,20},{20... | collective-permute-start | bytes 393224 | tf_op jit(solution)/shard_map/ppermute | solution.py:21
  153.4 1.0 collective-permute-done.10
  154.4 1.9 %collective-permute-start.11 = (f32[256,128]{1,0:T(8,128)S(1)}, f32[256,128]{1,0:T(8,128)S(1)}, u32[]{:S(2)}, u32[]{:S(2)}) collective-permute-start(f32[256,128]{1,0:T(8,128)S(1)} %slice.77), channel_id=1, source_target_pairs={{0,128},{128,0},{256,384},{384,256},{1,129},{129,1},{257,385},{385... | collective-permute-start | bytes 393224 | tf_op jit(solution)/shard_map/ppermute | solution.py:21
  156.4 0.0 collective-permute-done.7
  156.4 4.9 %collective-permute-done.11 = f32[256,128]{1,0:T(8,128)S(1)} collective-permute-done((f32[256,128]{1,0:T(8,128)S(1)}, f32[256,128]{1,0:T(8,128)S(1)}, u32[]{:S(2)}, u32[]{:S(2)}) %collective-permute-start.11) | collective-permute-done | bytes 131104 | tf_op jit(solution)/shard_map/ppermute | solution.py:21
  161.3 21.1 %all_to_all.10 = f32[16,16,256]{2,1,0:T(8,128)S(1)} all-to-all(f32[16,16,256]{2,1,0:T(8,128)S(1)} %bitcast.37), channel_id=1, replica_groups=mesh['y'=4,'zp'=4,'zi'=2,'core'=2,'zh'=2,'x'=4] {'zp','x'}, dimensions={0} | all-to-all | bytes 524288 | tf_op jit(solution)/shard_map/all_to_all | solution.py:218
  182.5 0.6 multiply_bitcast_fusion
  (16 shorter events, 0.3 us)
Async XLA Ops:
  0.0 8.0 %copy-start = (s32[1,16,2]{1,2,0:T(2,128)S(1)}, s32[1,16,2]{1,2,0:T(2,128)}, u32[]{:S(2)}) copy-start(s32[1,16,2]{1,2,0:T(2,128)} %param.5) | copy-start | bytes 388
  2.8 84.6 %collective-permute-start = (bf16[4,64,512]{2,1,0:T(8,128)(2,1)S(1)}, bf16[4,64,512]{2,1,0:T(8,128)(2,1)S(1)}, u32[]{:S(2)}, u32[]{:S(2)}) collective-permute-start(bf16[4,64,512]{2,1,0:T(8,128)(2,1)S(1)} %get-tuple-element.29), channel_id=1, source_target_pairs={{0,4},{1,5},{2,6},{3,7},{8,12},{9,13},{10,14},{11,15},{16,20},{17,... | collective-permute-start | bytes 786440 | tf_op jit(solution)/shard_map/ppermute | solution.py:191
  4.1 83.4 %collective-permute-start.1 = (bf16[4,64,512]{2,1,0:T(8,128)(2,1)S(1)}, bf16[4,64,512]{2,1,0:T(8,128)(2,1)S(1)}, u32[]{:S(2)}, u32[]{:S(2)}) collective-permute-start(bf16[4,64,512]{2,1,0:T(8,128)(2,1)S(1)} %get-tuple-element.30), channel_id=1, source_target_pairs={{0,5},{1,4},{2,7},{3,6},{8,13},{9,12},{10,15},{11,14},{16,21},{17,... | collective-permute-start | bytes 786440 | tf_op jit(solution)/shard_map/ppermute | solution.py:191
  5.4 82.1 %collective-permute-start.2 = (bf16[4,64,512]{2,1,0:T(8,128)(2,1)S(1)}, bf16[4,64,512]{2,1,0:T(8,128)(2,1)S(1)}, u32[]{:S(2)}, u32[]{:S(2)}) collective-permute-start(bf16[4,64,512]{2,1,0:T(8,128)(2,1)S(1)} %get-tuple-element.31), channel_id=1, source_target_pairs={{0,6},{1,7},{2,4},{3,5},{8,14},{9,15},{10,12},{11,13},{16,22},{17,... | collective-permute-start | bytes 786440 | tf_op jit(solution)/shard_map/ppermute | solution.py:191
  6.7 80.8 %collective-permute-start.3 = (bf16[4,64,512]{2,1,0:T(8,128)(2,1)S(1)}, bf16[4,64,512]{2,1,0:T(8,128)(2,1)S(1)}, u32[]{:S(2)}, u32[]{:S(2)}) collective-permute-start(bf16[4,64,512]{2,1,0:T(8,128)(2,1)S(1)} %get-tuple-element.32), channel_id=1, source_target_pairs={{0,7},{1,6},{2,5},{3,4},{8,15},{9,14},{10,13},{11,12},{16,23},{17,... | collective-permute-start | bytes 786440 | tf_op jit(solution)/shard_map/ppermute | solution.py:191
  93.3 4.6 %collective-permute-start.4 = (f32[2048,128]{1,0:T(8,128)S(1)}, f32[2048,128]{1,0:T(8,128)S(1)}, u32[]{:S(2)}, u32[]{:S(2)}) collective-permute-start(f32[2048,128]{1,0:T(8,128)S(1)} %get-tuple-element.38), channel_id=1, source_target_pairs={{0,8},{8,0},{1,9},{9,1},{2,10},{10,2},{3,11},{11,3},{4,12},{12,4},... | collective-permute-start | bytes 3145736 | tf_op jit(solution)/shard_map/ppermute | solution.py:21
  95.3 7.7 %collective-permute-start.8 = (f32[2048,128]{1,0:T(8,128)S(1)}, f32[2048,128]{1,0:T(8,128)S(1)}, u32[]{:S(2)}, u32[]{:S(2)}) collective-permute-start(f32[2048,128]{1,0:T(8,128)S(1)} %get-tuple-element.40), channel_id=1, source_target_pairs={{0,8},{8,0},{1,9},{9,1},{2,10},{10,2},{3,11},{11,3},{4,12},{12,4},... | collective-permute-start | bytes 3145736 | tf_op jit(solution)/shard_map/ppermute | solution.py:21
  98.1 33.7 %collective-permute-start.5 = (f32[1024,128]{1,0:T(8,128)S(1)}, f32[1024,128]{1,0:T(8,128)S(1)}, u32[]{:S(2)}, u32[]{:S(2)}) collective-permute-start(f32[1024,128]{1,0:T(8,128)S(1)} %slice.67), channel_id=1, source_target_pairs={{0,384},{128,256},{256,128},{384,0},{1,385},{129,257},{257,129},{3... | collective-permute-start | bytes 1572872 | tf_op jit(solution)/shard_map/ppermute | solution.py:21
  103.2 40.5 %collective-permute-start.9 = (f32[1024,128]{1,0:T(8,128)S(1)}, f32[1024,128]{1,0:T(8,128)S(1)}, u32[]{:S(2)}, u32[]{:S(2)}) collective-permute-start(f32[1024,128]{1,0:T(8,128)S(1)} %slice.73), channel_id=1, source_target_pairs={{0,16},{16,0},{1,17},{17,1},{2,18},{18,2},{3,19},{19,3},{4,20},{20... | collective-permute-start | bytes 1572872 | tf_op jit(solution)/shard_map/ppermute | solution.py:21
  131.8 14.3 %collective-permute-start.6 = (f32[512,128]{1,0:T(8,128)S(1)}, f32[512,128]{1,0:T(8,128)S(1)}, u32[]{:S(2)}, u32[]{:S(2)}) collective-permute-start(f32[512,128]{1,0:T(8,128)S(1)} %slice.69), channel_id=1, source_target_pairs={{0,128},{128,0},{256,384},{384,256},{1,129},{129,1},{257,385},{385... | collective-permute-start | bytes 786440 | tf_op jit(solution)/shard_map/ppermute | solution.py:21
  143.7 10.6 %collective-permute-start.10 = (f32[512,128]{1,0:T(8,128)S(1)}, f32[512,128]{1,0:T(8,128)S(1)}, u32[]{:S(2)}, u32[]{:S(2)}) collective-permute-start(f32[512,128]{1,0:T(8,128)S(1)} %slice.75), channel_id=1, source_target_pairs={{0,384},{128,256},{256,128},{384,0},{1,385},{129,257},{257,129},{3... | collective-permute-start | bytes 786440 | tf_op jit(solution)/shard_map/ppermute | solution.py:21
  146.2 10.1 %collective-permute-start.7 = (f32[256,128]{1,0:T(8,128)S(1)}, f32[256,128]{1,0:T(8,128)S(1)}, u32[]{:S(2)}, u32[]{:S(2)}) collective-permute-start(f32[256,128]{1,0:T(8,128)S(1)} %slice.71), channel_id=1, source_target_pairs={{0,16},{16,0},{1,17},{17,1},{2,18},{18,2},{3,19},{19,3},{4,20},{20... | collective-permute-start | bytes 393224 | tf_op jit(solution)/shard_map/ppermute | solution.py:21
  154.4 6.9 %collective-permute-start.11 = (f32[256,128]{1,0:T(8,128)S(1)}, f32[256,128]{1,0:T(8,128)S(1)}, u32[]{:S(2)}, u32[]{:S(2)}) collective-permute-start(f32[256,128]{1,0:T(8,128)S(1)} %slice.77), channel_id=1, source_target_pairs={{0,128},{128,0},{256,384},{384,256},{1,129},{129,1},{257,385},{385... | collective-permute-start | bytes 393224 | tf_op jit(solution)/shard_map/ppermute | solution.py:21

commit v6 on v5

--- a/solution.py
+++ b/solution.py
@@ -11,6 +11,8 @@
 NP = NZ // 2
 SIZES = {"y": NY, "zi": 2, "core": NC, "x": NX}
 CUTS = 2
+TOGETHER = 4
+LIST = TOGETHER
 QUARTER = 64
 VMEM = pl.BlockSpec(memory_space=pltpu.VMEM)
 SMEM = pl.BlockSpec(memory_space=pltpu.SMEM)
@@ -69,7 +71,7 @@
     group = e ^ (e >> 1)
     for half in range(2):
         side = half ^ zi
-        starts = (group * 2 + side, side * 4 + group)
+        starts = (side * 4 + group, group * 2 + side)
         for cut in range(CUTS):
             at = ((starts[cut] * NP + lax.rem(k, 4)) * NX + n // 16) * 16
             at = pl.ds(pl.multiple_of(at, 16), 16)
@@ -86,7 +88,7 @@
 
 
 def early_kernel(slots, meta, source, *refs):
-    keep, send, (cols, rows, sems) = refs[:CUTS], refs[CUTS : 2 * CUTS], refs[2 * CUTS :]
+    keep, send, (cols, lists, rows, sems) = refs[:CUTS], refs[CUTS : 2 * CUTS], refs[2 * CUTS :]
     tokens = cols.shape[1]
     per = cols.shape[0] // NX
     copies = [
@@ -118,33 +120,52 @@
 
     lax.fori_loop(0, slots, one, 0)
 
-
-def late_kernel(slots, meta, cols, *refs):
+    stride = LIST + slots
+    for e in range(NX):
+        lists[e * stride] = 0
+
+    def note(n, _):
+        @pl.when(meta[HEAD + n] == 2)
+        def _():
+            at = meta[HEAD + slots + n] // (cols.shape[0] // NX) * stride
+            count = lists[at] + 1
+            lists[at] = count
+            for u in range(LIST):
+                lists[at + count + u] = n
+
+        return 0
+
+    lax.fori_loop(0, slots, note, 0)
+
+
+def late_kernel(slots, meta, lists, cols, *refs):
     sources, refs = refs[:NX], refs[NX + 2 * CUTS :]
     keep, send, (rows, sems) = refs[:CUTS], refs[CUTS : 2 * CUTS], refs[2 * CUTS :]
     per = sources[0].shape[0]
     copies = [
-        pltpu.make_async_copy(sources[d], rows.at[pl.ds(d * per, per)], sems.at[d])
-        for d in range(NX)
+        pltpu.make_async_copy(sources[e], rows.at[pl.ds(e * per, per)], sems.at[e])
+        for e in range(NX)
     ]
     for copy in copies:
         copy.start()
-    for copy in copies:
-        copy.wait()
-
-    def one(n, _):
-        @pl.when(meta[HEAD + n] == 2)
-        def _():
-            product = jnp.dot(
-                rows[meta[HEAD + slots + n]],
-                cols[meta[HEAD + 2 * slots + n]],
-                preferred_element_type=jnp.float32,
-            )
-            put(meta, n, product, keep, send)
-
-        return 0
-
-    lax.fori_loop(0, slots, one, 0)
+    for e in range(NX):
+        copies[e].wait()
+
+        def some(i, _):
+            ids = [lists[e * (LIST + slots) + 1 + i * TOGETHER + u] for u in range(TOGETHER)]
+            made = [
+                jnp.dot(
+                    rows[meta[HEAD + slots + n]],
+                    cols[meta[HEAD + 2 * slots + n]],
+                    preferred_element_type=jnp.float32,
+                )
+                for n in ids
+            ]
+            for n, product in zip(ids, made):
+                put(meta, n, product, keep, send)
+            return 0
+
+        lax.fori_loop(0, (lists[e * (LIST + slots)] + TOGETHER - 1) // TOGETHER, some, 0)
 
 
 def early(meta, source, count, tokens, slots):
@@ -152,9 +173,13 @@
     half = jax.ShapeDtypeStruct((slots * QUARTER // 2, width // CUTS), jnp.float32)
     return pl.pallas_call(
         functools.partial(early_kernel, slots),
-        out_shape=[half] * (2 * CUTS) + [jax.ShapeDtypeStruct((count, tokens, width), jnp.bfloat16)],
+        out_shape=[half] * (2 * CUTS)
+        + [
+            jax.ShapeDtypeStruct((count, tokens, width), jnp.bfloat16),
+            jax.ShapeDtypeStruct((NX * (LIST + slots),), jnp.int32),
+        ],
         in_specs=[SMEM, ANY],
-        out_specs=[VMEM] * (2 * CUTS + 1),
+        out_specs=[VMEM] * (2 * CUTS + 1) + [SMEM],
         scratch_shapes=[
             pltpu.VMEM((count, QUARTER, tokens), jnp.bfloat16),
             pltpu.SemaphoreType.DMA((count,)),
@@ -164,20 +189,20 @@
     )(meta, source)
 
 
-def late(meta, cols, sources, halves, slots):
+def late(meta, lists, cols, sources, halves, slots):
     per, quarter, tokens = sources[0].shape
     return pl.pallas_call(
         functools.partial(late_kernel, slots),
         out_shape=[jax.ShapeDtypeStruct(h.shape, h.dtype) for h in halves],
-        in_specs=[SMEM, VMEM] + [ANY] * NX + [VMEM] * len(halves),
+        in_specs=[SMEM, SMEM, VMEM] + [ANY] * NX + [VMEM] * len(halves),
         out_specs=[VMEM] * len(halves),
         scratch_shapes=[
             pltpu.VMEM((NX * per, quarter, tokens), jnp.bfloat16),
             pltpu.SemaphoreType.DMA((NX,)),
         ],
-        input_output_aliases={2 + NX + i: i for i in range(len(halves))},
+        input_output_aliases={3 + NX + i: i for i in range(len(halves))},
         compiler_params=pltpu.CompilerParams(vmem_limit_bytes=24 << 20),
-    )(meta, cols, *sources, *halves)
+    )(meta, lists, cols, *sources, *halves)
 
 
 def body(activations, block_map):
@@ -209,10 +234,10 @@
     head = jnp.stack([y, zi, core, x, zh, zh, zh, zh])
     meta = jnp.concatenate([head, kind, row_at, col_at]).astype(jnp.int32)
 
-    *halves, cols = early(meta, half, NX * blocks, tokens, slots)
-    halves = late(meta, cols, low, halves, slots)
+    *halves, cols, lists = early(meta, half, NX * blocks, tokens, slots)
+    halves = late(meta, lists, cols, low, halves, slots)
     scale = 2.0 / (tokens * NY * NZ * NC)
-    orders = ((("y", 3), ("y", 1), ("zi", 1)), (("zi", 1), ("y", 3), ("y", 1)))
+    orders = ((("zi", 1), ("y", 3), ("y", 1)), (("y", 3), ("y", 1), ("zi", 1)))
     cuts = [total(*cut) for cut in zip(halves[:CUTS], halves[CUTS:], orders)]
     parts = jnp.concatenate(cuts, axis=1).reshape(NP * NX, -1, width)
     parts = lax.all_to_all(parts, ("zp", "x"), 0, 0, tiled=True).reshape(NP, -1, width)

time: 184 us -> 180 us (0.978)
  starting transfers between devices: 56.5 us -> 53.9 us
    pallas_call x1, Pallas kernels: 5.9 us -> 3.21 us  [late(): pl.pallas_call(functools.partial(late_kernel, slots), out_shape=[jax.Shap...]
    ppermute x8, starting transfers between devices: 51.3 us -> 48.7 us  [swap(): return lax.ppermute(v, axis, [(i, i ^ e) for i in range(SIZES[axis])])]
    pallas_call x1, Pallas kernels: 9.84 us -> 11.9 us  [early(): pl.pallas_call(functools.partial(early_kernel, slots), out_shape=[half] *...]
  transfers between devices with their start and end apart: 12 -> 12, of which waited for: 4 -> 5; matrix products, arithmetic and copies ran while one was open for 1% -> 1% of each run, Pallas kernels for 5% -> 7%
where the time goes in v6:
time: 180 us
  blocking collectives  88.2 us (49%)
  starting transfers between devices  53.9 us (30%)
  Pallas kernels  16.5 us (9%)
  waiting for transfers between devices  15.7 us (9%)
  local copies, waits for them, and re-layouts  2.56 us (1%)
  other arithmetic  1.93 us (1%)
    all_to_all x1, blocking collectives, exchange(): lax.all_to_all(jnp.broadcast_to(load, (NX, *load.shape)), 'x', 0, 0, tile...  67 us
    ppermute x8, starting transfers between devices, swap(): return lax.ppermute(v, axis, [(i, i ^ e) for i in range(SIZES[axis])])  48.7 us
    all_to_all x1, blocking collectives, body(): lax.all_to_all(parts, ('zp', 'x'), 0, 0, tiled=True).reshape(NP, -1, width)  21.2 us
    ppermute x8, waiting for transfers between devices, swap(): return lax.ppermute(v, axis, [(i, i ^ e) for i in range(SIZES[axis])])  15.7 us
    pallas_call x1, Pallas kernels, early(): pl.pallas_call(functools.partial(early_kernel, slots), out_shape=[half] *...  11.9 us
    ppermute x4, starting transfers between devices, body(): lax.ppermute(piece, ('zh', 'x'), [(i, NX + (i ^ e)) for i in range(NX)])  5.17 us
  transfers between devices with their start and end apart: 12, of which 5 were waited for; matrix products, arithmetic and copies ran while one was open for 1% of the time, Pallas kernels for 7%

profile of v6, /device:TPU:256, one launch (start us, length us, event | category | flops | bytes accessed | tf_op | source)
XLA Modules:
  0.0 179.7 jit_solution(1472500072802706108)
XLA Ops:
  0.0 0.0 copy-start
  0.0 1.4 copy.18
  1.4 1.4 shard_map.29
  2.8 1.3 collective-permute-start
  4.1 1.3 collective-permute-start.1
  5.4 1.3 collective-permute-start.2
  6.7 1.3 collective-permute-start.3
  8.0 0.0 copy-done
  8.0 0.5 slice.49
  9.1 67.5 %conditional.1 = (bf16[4,2064,256]{2,1,0:T(8,128)(2,1)}) conditional(s32[]{:T(128)} %bitcast.7, () %tuple.11, (bf16[4,512,256]{2,1,0:T(8,128)(2,1)S(1)}, s32[1,16,2]{1,2,0:T(2,128)S(1)}) %tuple.18), branch_computations={%region_0.0_spmd, %region_1.2_spmd} | conditional | flops 3170336 | bytes 15843720 | solution.py:220
  9.2 0.1 copy.13
  9.3 0.1 fusion.1
  9.3 0.3 broadcast_in_dim.7
  9.6 67.0 %all_to_all.9 = bf16[4,2064,256]{2,1,0:T(8,128)(2,1)} all-to-all(bf16[4,2064,256]{2,1,0:T(8,128)(2,1)S(1)} %broadcast_in_dim.7), channel_id=1, replica_groups=mesh['y'=4,'zp'=4,'zi'=2,'core'=2,'zh'=2,'x'=4] {'x'}, dimensions={0} | all-to-all | bytes 8454144 | tf_op jit(solution)/shard_map/cond/branch_1_fun/all_to_all | solution.py:61
  76.6 0.7 slice_convert_fusion
  77.3 0.1 copy.17
  77.5 0.1 concatenate.9.meta
  77.6 11.9 %shard_map.28 = (f32[2048,128]{1,0:T(8,128)S(1)}, f32[2048,128]{1,0:T(8,128)S(1)}, f32[2048,128]{1,0:T(8,128)S(1)}, f32[2048,128]{1,0:T(8,128)S(1)}, bf16[16,512,256]{2,1,0:T(8,128)(2,1)S(1)}, /*index=5*/s32[272]{0:T(512)S(1)}) custom-call(s32[200]{0:T(256)S(1)} %concatenate.9.meta, bf16[4,2064,256]{2,1,0:T(8,128)(2,1)} %get-tuple-element.47.source), custom_call_target="tpu_custom_call" | custom-call | tf_op jit(solution)/shard_map/pallas_call | solution.py:174
  89.4 0.0 collective-permute-done.refs_0_
  89.5 0.0 collective-permute-done.1.refs_1_
  89.5 0.0 collective-permute-done.2.refs_2_
  89.5 0.0 collective-permute-done.3.refs_3_
  89.5 3.2 %shard_map.30 = (f32[2048,128]{1,0:T(8,128)S(1)}, f32[2048,128]{1,0:T(8,128)S(1)}, f32[2048,128]{1,0:T(8,128)S(1)}, f32[2048,128]{1,0:T(8,128)S(1)}) custom-call(s32[200]{0:T(256)S(1)} %concatenate.9.meta, s32[272]{0:T(512)S(1)} %get-tuple-element.29.lists, ...), custom_call_target="tpu_custom_call", output_to_operand_aliasing={{0}: (7, {}), {1}: (8, {}), {2}: (9, {}), {3}: (10, {})} | custom-call | tf_op jit(solution)/shard_map/pallas_call | solution.py:194
  92.7 1.9 %collective-permute-start.4 = (f32[2048,128]{1,0:T(8,128)S(1)}, f32[2048,128]{1,0:T(8,128)S(1)}, u32[]{:S(2)}, u32[]{:S(2)}) collective-permute-start(f32[2048,128]{1,0:T(8,128)S(1)} %get-tuple-element.40), channel_id=1, source_target_pairs={{0,8},{8,0},{1,9},{9,1},{2,10},{10,2},{3,11},{11,3},{4,12},{12,4},... | collective-permute-start | bytes 3145736 | tf_op jit(solution)/shard_map/ppermute | solution.py:23
  94.6 2.4 %collective-permute-start.8 = (f32[2048,128]{1,0:T(8,128)S(1)}, f32[2048,128]{1,0:T(8,128)S(1)}, u32[]{:S(2)}, u32[]{:S(2)}) collective-permute-start(f32[2048,128]{1,0:T(8,128)S(1)} %get-tuple-element.42), channel_id=1, source_target_pairs={{0,8},{8,0},{1,9},{9,1},{2,10},{10,2},{3,11},{11,3},{4,12},{12,4},... | collective-permute-start | bytes 3145736 | tf_op jit(solution)/shard_map/ppermute | solution.py:23
  97.0 0.2 collective-permute-done.4
  97.3 0.1 add.51
  97.4 26.6 %collective-permute-start.5 = (f32[1024,128]{1,0:T(8,128)S(1)}, f32[1024,128]{1,0:T(8,128)S(1)}, u32[]{:S(2)}, u32[]{:S(2)}) collective-permute-start(f32[1024,128]{1,0:T(8,128)S(1)} %slice.67), channel_id=1, source_target_pairs={{0,16},{16,0},{1,17},{17,1},{2,18},{18,2},{3,19},{19,3},{4,20},{20... | collective-permute-start | bytes 1572872 | tf_op jit(solution)/shard_map/ppermute | solution.py:23
  124.0 0.0 collective-permute-done.8
  124.0 0.1 add.55
  124.2 4.9 %collective-permute-start.9 = (f32[1024,128]{1,0:T(8,128)S(1)}, f32[1024,128]{1,0:T(8,128)S(1)}, u32[]{:S(2)}, u32[]{:S(2)}) collective-permute-start(f32[1024,128]{1,0:T(8,128)S(1)} %slice.73), channel_id=1, source_target_pairs={{0,384},{128,256},{256,128},{384,0},{1,385},{129,257},{257,129},{3... | collective-permute-start | bytes 1572872 | tf_op jit(solution)/shard_map/ppermute | solution.py:23
  129.1 7.1 %collective-permute-done.5 = f32[1024,128]{1,0:T(8,128)S(1)} collective-permute-done((f32[1024,128]{1,0:T(8,128)S(1)}, f32[1024,128]{1,0:T(8,128)S(1)}, u32[]{:S(2)}, u32[]{:S(2)}) %collective-permute-start.5) | collective-permute-done | bytes 524320 | tf_op jit(solution)/shard_map/ppermute | solution.py:23
  136.2 0.1 slice_add_fusion.1
  136.3 4.9 %collective-permute-start.6 = (f32[512,128]{1,0:T(8,128)S(1)}, f32[512,128]{1,0:T(8,128)S(1)}, u32[]{:S(2)}, u32[]{:S(2)}) collective-permute-start(f32[512,128]{1,0:T(8,128)S(1)} %slice.69), channel_id=1, source_target_pairs={{0,384},{128,256},{256,128},{384,0},{1,385},{129,257},{257,129},{3... | collective-permute-start | bytes 786440 | tf_op jit(solution)/shard_map/ppermute | solution.py:23
  141.3 0.0 collective-permute-done.9
  141.3 0.1 slice_add_fusion
  141.4 2.0 %collective-permute-start.10 = (f32[512,128]{1,0:T(8,128)S(1)}, f32[512,128]{1,0:T(8,128)S(1)}, u32[]{:S(2)}, u32[]{:S(2)}) collective-permute-start(f32[512,128]{1,0:T(8,128)S(1)} %slice.75), channel_id=1, source_target_pairs={{0,128},{128,0},{256,384},{384,256},{1,129},{129,1},{257,385},{385... | collective-permute-start | bytes 786440 | tf_op jit(solution)/shard_map/ppermute | solution.py:23
  143.4 3.9 %collective-permute-done.6 = f32[512,128]{1,0:T(8,128)S(1)} collective-permute-done((f32[512,128]{1,0:T(8,128)S(1)}, f32[512,128]{1,0:T(8,128)S(1)}, u32[]{:S(2)}, u32[]{:S(2)}) %collective-permute-start.6) | collective-permute-done | bytes 262176 | tf_op jit(solution)/shard_map/ppermute | solution.py:23
  147.4 2.2 %collective-permute-start.7 = (f32[256,128]{1,0:T(8,128)S(1)}, f32[256,128]{1,0:T(8,128)S(1)}, u32[]{:S(2)}, u32[]{:S(2)}) collective-permute-start(f32[256,128]{1,0:T(8,128)S(1)} %slice.71), channel_id=1, source_target_pairs={{0,128},{128,0},{256,384},{384,256},{1,129},{129,1},{257,385},{385... | collective-permute-start | bytes 393224 | tf_op jit(solution)/shard_map/ppermute | solution.py:23
  149.6 1.3 collective-permute-done.10
  150.9 3.7 %collective-permute-start.11 = (f32[256,128]{1,0:T(8,128)S(1)}, f32[256,128]{1,0:T(8,128)S(1)}, u32[]{:S(2)}, u32[]{:S(2)}) collective-permute-start(f32[256,128]{1,0:T(8,128)S(1)} %slice.77), channel_id=1, source_target_pairs={{0,16},{16,0},{1,17},{17,1},{2,18},{18,2},{3,19},{19,3},{4,20},{20... | collective-permute-start | bytes 393224 | tf_op jit(solution)/shard_map/ppermute | solution.py:23
  154.6 0.0 collective-permute-done.7
  154.6 3.1 %collective-permute-done.11 = f32[256,128]{1,0:T(8,128)S(1)} collective-permute-done((f32[256,128]{1,0:T(8,128)S(1)}, f32[256,128]{1,0:T(8,128)S(1)}, u32[]{:S(2)}, u32[]{:S(2)}) %collective-permute-start.11) | collective-permute-done | bytes 131104 | tf_op jit(solution)/shard_map/ppermute | solution.py:23
  157.8 21.2 %all_to_all.10 = f32[16,16,256]{2,1,0:T(8,128)S(1)} all-to-all(f32[16,16,256]{2,1,0:T(8,128)S(1)} %bitcast.37), channel_id=1, replica_groups=mesh['y'=4,'zp'=4,'zi'=2,'core'=2,'zh'=2,'x'=4] {'zp','x'}, dimensions={0} | all-to-all | bytes 524288 | tf_op jit(solution)/shard_map/all_to_all | solution.py:243
  179.1 0.6 multiply_bitcast_fusion
  (16 shorter events, 0.3 us)
Async XLA Ops:
  0.0 8.0 %copy-start = (s32[1,16,2]{1,2,0:T(2,128)S(1)}, s32[1,16,2]{1,2,0:T(2,128)}, u32[]{:S(2)}) copy-start(s32[1,16,2]{1,2,0:T(2,128)} %param.5) | copy-start | bytes 388
  2.8 86.7 %collective-permute-start = (bf16[4,64,512]{2,1,0:T(8,128)(2,1)S(1)}, bf16[4,64,512]{2,1,0:T(8,128)(2,1)S(1)}, u32[]{:S(2)}, u32[]{:S(2)}) collective-permute-start(bf16[4,64,512]{2,1,0:T(8,128)(2,1)S(1)} %get-tuple-element.31), channel_id=1, source_target_pairs={{0,4},{1,5},{2,6},{3,7},{8,12},{9,13},{10,14},{11,15},{16,20},{17,... | collective-permute-start | bytes 786440 | tf_op jit(solution)/shard_map/ppermute | solution.py:216
  4.1 85.4 %collective-permute-start.1 = (bf16[4,64,512]{2,1,0:T(8,128)(2,1)S(1)}, bf16[4,64,512]{2,1,0:T(8,128)(2,1)S(1)}, u32[]{:S(2)}, u32[]{:S(2)}) collective-permute-start(bf16[4,64,512]{2,1,0:T(8,128)(2,1)S(1)} %get-tuple-element.32), channel_id=1, source_target_pairs={{0,5},{1,4},{2,7},{3,6},{8,13},{9,12},{10,15},{11,14},{16,21},{17,... | collective-permute-start | bytes 786440 | tf_op jit(solution)/shard_map/ppermute | solution.py:216
  5.4 84.1 %collective-permute-start.2 = (bf16[4,64,512]{2,1,0:T(8,128)(2,1)S(1)}, bf16[4,64,512]{2,1,0:T(8,128)(2,1)S(1)}, u32[]{:S(2)}, u32[]{:S(2)}) collective-permute-start(bf16[4,64,512]{2,1,0:T(8,128)(2,1)S(1)} %get-tuple-element.33), channel_id=1, source_target_pairs={{0,6},{1,7},{2,4},{3,5},{8,14},{9,15},{10,12},{11,13},{16,22},{17,... | collective-permute-start | bytes 786440 | tf_op jit(solution)/shard_map/ppermute | solution.py:216
  6.7 82.8 %collective-permute-start.3 = (bf16[4,64,512]{2,1,0:T(8,128)(2,1)S(1)}, bf16[4,64,512]{2,1,0:T(8,128)(2,1)S(1)}, u32[]{:S(2)}, u32[]{:S(2)}) collective-permute-start(bf16[4,64,512]{2,1,0:T(8,128)(2,1)S(1)} %get-tuple-element.34), channel_id=1, source_target_pairs={{0,7},{1,6},{2,5},{3,4},{8,15},{9,14},{10,13},{11,12},{16,23},{17,... | collective-permute-start | bytes 786440 | tf_op jit(solution)/shard_map/ppermute | solution.py:216
  92.7 4.6 %collective-permute-start.4 = (f32[2048,128]{1,0:T(8,128)S(1)}, f32[2048,128]{1,0:T(8,128)S(1)}, u32[]{:S(2)}, u32[]{:S(2)}) collective-permute-start(f32[2048,128]{1,0:T(8,128)S(1)} %get-tuple-element.40), channel_id=1, source_target_pairs={{0,8},{8,0},{1,9},{9,1},{2,10},{10,2},{3,11},{11,3},{4,12},{12,4},... | collective-permute-start | bytes 3145736 | tf_op jit(solution)/shard_map/ppermute | solution.py:23
  94.6 29.4 %collective-permute-start.8 = (f32[2048,128]{1,0:T(8,128)S(1)}, f32[2048,128]{1,0:T(8,128)S(1)}, u32[]{:S(2)}, u32[]{:S(2)}) collective-permute-start(f32[2048,128]{1,0:T(8,128)S(1)} %get-tuple-element.42), channel_id=1, source_target_pairs={{0,8},{8,0},{1,9},{9,1},{2,10},{10,2},{3,11},{11,3},{4,12},{12,4},... | collective-permute-start | bytes 3145736 | tf_op jit(solution)/shard_map/ppermute | solution.py:23
  97.4 38.8 %collective-permute-start.5 = (f32[1024,128]{1,0:T(8,128)S(1)}, f32[1024,128]{1,0:T(8,128)S(1)}, u32[]{:S(2)}, u32[]{:S(2)}) collective-permute-start(f32[1024,128]{1,0:T(8,128)S(1)} %slice.67), channel_id=1, source_target_pairs={{0,16},{16,0},{1,17},{17,1},{2,18},{18,2},{3,19},{19,3},{4,20},{20... | collective-permute-start | bytes 1572872 | tf_op jit(solution)/shard_map/ppermute | solution.py:23
  124.2 17.1 %collective-permute-start.9 = (f32[1024,128]{1,0:T(8,128)S(1)}, f32[1024,128]{1,0:T(8,128)S(1)}, u32[]{:S(2)}, u32[]{:S(2)}) collective-permute-start(f32[1024,128]{1,0:T(8,128)S(1)} %slice.73), channel_id=1, source_target_pairs={{0,384},{128,256},{256,128},{384,0},{1,385},{129,257},{257,129},{3... | collective-permute-start | bytes 1572872 | tf_op jit(solution)/shard_map/ppermute | solution.py:23
  136.3 11.0 %collective-permute-start.6 = (f32[512,128]{1,0:T(8,128)S(1)}, f32[512,128]{1,0:T(8,128)S(1)}, u32[]{:S(2)}, u32[]{:S(2)}) collective-permute-start(f32[512,128]{1,0:T(8,128)S(1)} %slice.69), channel_id=1, source_target_pairs={{0,384},{128,256},{256,128},{384,0},{1,385},{129,257},{257,129},{3... | collective-permute-start | bytes 786440 | tf_op jit(solution)/shard_map/ppermute | solution.py:23
  141.4 9.5 %collective-permute-start.10 = (f32[512,128]{1,0:T(8,128)S(1)}, f32[512,128]{1,0:T(8,128)S(1)}, u32[]{:S(2)}, u32[]{:S(2)}) collective-permute-start(f32[512,128]{1,0:T(8,128)S(1)} %slice.75), channel_id=1, source_target_pairs={{0,128},{128,0},{256,384},{384,256},{1,129},{129,1},{257,385},{385... | collective-permute-start | bytes 786440 | tf_op jit(solution)/shard_map/ppermute | solution.py:23
  147.4 7.2 %collective-permute-start.7 = (f32[256,128]{1,0:T(8,128)S(1)}, f32[256,128]{1,0:T(8,128)S(1)}, u32[]{:S(2)}, u32[]{:S(2)}) collective-permute-start(f32[256,128]{1,0:T(8,128)S(1)} %slice.71), channel_id=1, source_target_pairs={{0,128},{128,0},{256,384},{384,256},{1,129},{129,1},{257,385},{385... | collective-permute-start | bytes 393224 | tf_op jit(solution)/shard_map/ppermute | solution.py:23
  150.9 6.9 %collective-permute-start.11 = (f32[256,128]{1,0:T(8,128)S(1)}, f32[256,128]{1,0:T(8,128)S(1)}, u32[]{:S(2)}, u32[]{:S(2)}) collective-permute-start(f32[256,128]{1,0:T(8,128)S(1)} %slice.77), channel_id=1, source_target_pairs={{0,16},{16,0},{1,17},{17,1},{2,18},{18,2},{3,19},{19,3},{4,20},{20... | collective-permute-start | bytes 393224 | tf_op jit(solution)/shard_map/ppermute | solution.py:23

commit v7 on v6

--- a/solution.py
+++ b/solution.py
@@ -71,7 +71,7 @@
     group = e ^ (e >> 1)
     for half in range(2):
         side = half ^ zi
-        starts = (side * 4 + group, group * 2 + side)
+        starts = (group * 2 + side, side * 4 + k // 4)
         for cut in range(CUTS):
             at = ((starts[cut] * NP + lax.rem(k, 4)) * NX + n // 16) * 16
             at = pl.ds(pl.multiple_of(at, 16), 16)
@@ -237,15 +237,16 @@
     *halves, cols, lists = early(meta, half, NX * blocks, tokens, slots)
     halves = late(meta, lists, cols, low, halves, slots)
     scale = 2.0 / (tokens * NY * NZ * NC)
-    orders = ((("zi", 1), ("y", 3), ("y", 1)), (("y", 3), ("y", 1), ("zi", 1)))
-    cuts = [total(*cut) for cut in zip(halves[:CUTS], halves[CUTS:], orders)]
-    parts = jnp.concatenate(cuts, axis=1).reshape(NP * NX, -1, width)
+    left, right = (keep + swap(send, "core", 1) for keep, send in zip(halves[:CUTS], halves[CUTS:]))
+    left = total(left, (("y", 3), ("y", 1), ("zi", 1)))
+    right = total(right, (("zi", 1),)).reshape(NY, -1, right.shape[1])
+    right = jnp.sum(lax.all_to_all(right, "y", 0, 0, tiled=True), axis=0)
+    parts = jnp.concatenate([left, right], axis=1).reshape(NP * NX, -1, width)
     parts = lax.all_to_all(parts, ("zp", "x"), 0, 0, tiled=True).reshape(NP, -1, width)
     return jnp.sum(parts, axis=0)[None] * scale
 
 
-def total(keep, send, order):
-    kept = keep + swap(send, "core", 1)
+def total(kept, order):
     for axis, e in order:
         half = kept.shape[0] // 2
         kept = kept[:half] + swap(kept[half:], axis, e)

time: 180 us -> 178 us (0.989)
  starting transfers between devices: 53.9 us -> 51.6 us
  waiting for transfers between devices: 15.7 us -> 13.7 us
    ppermute x8 -> x6, starting transfers between devices: 48.7 us -> 42.9 us  [swap(): return lax.ppermute(v, axis, [(i, i ^ e) for i in range(SIZES[axis])])]
    all_to_all x0 -> x1, starting transfers between devices: none -> 3.47 us  [body(): right = jnp.sum(lax.all_to_all(right, 'y', 0, 0, tiled=True), axis=0)]
    ppermute x8 -> x6, waiting for transfers between devices: 15.7 us -> 12.9 us  [swap(): return lax.ppermute(v, axis, [(i, i ^ e) for i in range(SIZES[axis])])]
  transfers between devices with their start and end apart: 12 -> 11, of which waited for: 5 -> 4; matrix products, arithmetic and copies ran while one was open for 1% -> 2% of each run, Pallas kernels for 7% -> 7%
where the time goes in v7:
time: 178 us
  blocking collectives  89.4 us (50%)
  starting transfers between devices  51.6 us (29%)
  Pallas kernels  17 us (10%)
  waiting for transfers between devices  13.7 us (8%)
  other arithmetic  2.69 us (2%)
  local copies, waits for them, and re-layouts  2.53 us (1%)
    all_to_all x1, blocking collectives, exchange(): lax.all_to_all(jnp.broadcast_to(load, (NX, *load.shape)), 'x', 0, 0, tile...  67 us
    ppermute x6, starting transfers between devices, swap(): return lax.ppermute(v, axis, [(i, i ^ e) for i in range(SIZES[axis])])  42.9 us
    all_to_all x1, blocking collectives, body(): lax.all_to_all(parts, ('zp', 'x'), 0, 0, tiled=True).reshape(NP, -1, width)  22.4 us
    ppermute x6, waiting for transfers between devices, swap(): return lax.ppermute(v, axis, [(i, i ^ e) for i in range(SIZES[axis])])  12.9 us
    pallas_call x1, Pallas kernels, early(): pl.pallas_call(functools.partial(early_kernel, slots), out_shape=[half] *...  12.1 us
    ppermute x4, starting transfers between devices, body(): lax.ppermute(piece, ('zh', 'x'), [(i, NX + (i ^ e)) for i in range(NX)])  5.17 us
  transfers between devices with their start and end apart: 11, of which 4 were waited for; matrix products, arithmetic and copies ran while one was open for 2% of the time, Pallas kernels for 7%

profile of v7, /device:TPU:256, one launch (start us, length us, event | category | flops | bytes accessed | tf_op | source)
XLA Modules:
  0.0 177.9 jit_solution(7822855458046285202)
XLA Ops:
  0.0 0.0 copy-start
  0.0 1.4 copy.18
  1.4 1.4 shard_map.29
  2.8 1.3 collective-permute-start
  4.1 1.3 collective-permute-start.1
  5.4 1.3 collective-permute-start.2
  6.7 1.3 collective-permute-start.3
  8.0 0.0 copy-done
  8.0 0.5 slice.37
  9.1 67.5 %conditional.1 = (bf16[4,2064,256]{2,1,0:T(8,128)(2,1)}) conditional(s32[]{:T(128)} %bitcast.7, () %tuple.11, (bf16[4,512,256]{2,1,0:T(8,128)(2,1)S(1)}, s32[1,16,2]{1,2,0:T(2,128)S(1)}) %tuple.18), branch_computations={%region_0.0_spmd, %region_1.2_spmd} | conditional | flops 3170336 | bytes 15843720 | solution.py:220
  9.2 0.1 copy.13
  9.3 0.1 fusion.1
  9.3 0.3 broadcast_in_dim.7
  9.6 67.0 %all_to_all.14 = bf16[4,2064,256]{2,1,0:T(8,128)(2,1)} all-to-all(bf16[4,2064,256]{2,1,0:T(8,128)(2,1)S(1)} %broadcast_in_dim.7), channel_id=1, replica_groups=mesh['y'=4,'zp'=4,'zi'=2,'core'=2,'zh'=2,'x'=4] {'x'}, dimensions={0} | all-to-all | bytes 8454144 | tf_op jit(solution)/shard_map/cond/branch_1_fun/all_to_all | solution.py:61
  76.6 0.7 slice_convert_fusion
  77.3 0.1 copy.17
  77.5 0.1 concatenate.9.meta
  77.6 12.1 %shard_map.28 = (f32[2048,128]{1,0:T(8,128)S(1)}, f32[2048,128]{1,0:T(8,128)S(1)}, f32[2048,128]{1,0:T(8,128)S(1)}, f32[2048,128]{1,0:T(8,128)S(1)}, bf16[16,512,256]{2,1,0:T(8,128)(2,1)S(1)}, /*index=5*/s32[272]{0:T(512)S(1)}) custom-call(s32[200]{0:T(256)S(1)} %concatenate.9.meta, bf16[4,2064,256]{2,1,0:T(8,128)(2,1)} %get-tuple-element.47.source), custom_call_target="tpu_custom_call" | custom-call | tf_op jit(solution)/shard_map/pallas_call | solution.py:174
  89.7 0.0 collective-permute-done.refs_0_
  89.7 0.0 collective-permute-done.1.refs_1_
  89.7 0.0 collective-permute-done.2.refs_2_
  89.7 0.0 collective-permute-done.3.refs_3_
  89.7 3.5 %shard_map.30 = (f32[2048,128]{1,0:T(8,128)S(1)}, f32[2048,128]{1,0:T(8,128)S(1)}, f32[2048,128]{1,0:T(8,128)S(1)}, f32[2048,128]{1,0:T(8,128)S(1)}) custom-call(s32[200]{0:T(256)S(1)} %concatenate.9.meta, s32[272]{0:T(512)S(1)} %get-tuple-element.29.lists, ...), custom_call_target="tpu_custom_call", output_to_operand_aliasing={{0}: (7, {}), {1}: (8, {}), {2}: (9, {}), {3}: (10, {})} | custom-call | tf_op jit(solution)/shard_map/pallas_call | solution.py:194
  93.3 1.9 %collective-permute-start.4 = (f32[2048,128]{1,0:T(8,128)S(1)}, f32[2048,128]{1,0:T(8,128)S(1)}, u32[]{:S(2)}, u32[]{:S(2)}) collective-permute-start(f32[2048,128]{1,0:T(8,128)S(1)} %get-tuple-element.40), channel_id=1, source_target_pairs={{0,8},{8,0},{1,9},{9,1},{2,10},{10,2},{3,11},{11,3},{4,12},{12,4},... | collective-permute-start | bytes 3145736 | tf_op jit(solution)/shard_map/ppermute | solution.py:23
  95.2 2.4 %collective-permute-start.8 = (f32[2048,128]{1,0:T(8,128)S(1)}, f32[2048,128]{1,0:T(8,128)S(1)}, u32[]{:S(2)}, u32[]{:S(2)}) collective-permute-start(f32[2048,128]{1,0:T(8,128)S(1)} %get-tuple-element.42), channel_id=1, source_target_pairs={{0,8},{8,0},{1,9},{9,1},{2,10},{10,2},{3,11},{11,3},{4,12},{12,4},... | collective-permute-start | bytes 3145736 | tf_op jit(solution)/shard_map/ppermute | solution.py:23
  97.6 0.2 collective-permute-done.4
  97.8 0.1 add.45
  98.0 4.9 %collective-permute-start.5 = (f32[1024,128]{1,0:T(8,128)S(1)}, f32[1024,128]{1,0:T(8,128)S(1)}, u32[]{:S(2)}, u32[]{:S(2)}) collective-permute-start(f32[1024,128]{1,0:T(8,128)S(1)} %slice.51), channel_id=1, source_target_pairs={{0,384},{128,256},{256,128},{384,0},{1,385},{129,257},{257,129},{3... | collective-permute-start | bytes 1572872 | tf_op jit(solution)/shard_map/ppermute | solution.py:23
  102.9 0.0 collective-permute-done.8
  102.9 0.1 add.49
  103.1 26.3 %collective-permute-start.9 = (f32[1024,128]{1,0:T(8,128)S(1)}, f32[1024,128]{1,0:T(8,128)S(1)}, u32[]{:S(2)}, u32[]{:S(2)}) collective-permute-start(f32[1024,128]{1,0:T(8,128)S(1)} %slice.57), channel_id=1, source_target_pairs={{0,16},{16,0},{1,17},{17,1},{2,18},{18,2},{3,19},{19,3},{4,20},{20... | collective-permute-start | bytes 1572872 | tf_op jit(solution)/shard_map/ppermute | solution.py:23
  129.4 0.0 collective-permute-done.5
  129.4 0.1 slice_add_fusion.1
  129.5 2.0 %collective-permute-start.6 = (f32[512,128]{1,0:T(8,128)S(1)}, f32[512,128]{1,0:T(8,128)S(1)}, u32[]{:S(2)}, u32[]{:S(2)}) collective-permute-start(f32[512,128]{1,0:T(8,128)S(1)} %slice.53), channel_id=1, source_target_pairs={{0,128},{128,0},{256,384},{384,256},{1,129},{129,1},{257,385},{385... | collective-permute-start | bytes 786440 | tf_op jit(solution)/shard_map/ppermute | solution.py:23
  131.5 9.8 %collective-permute-done.9 = f32[1024,128]{1,0:T(8,128)S(1)} collective-permute-done((f32[1024,128]{1,0:T(8,128)S(1)}, f32[1024,128]{1,0:T(8,128)S(1)}, u32[]{:S(2)}, u32[]{:S(2)}) %collective-permute-start.9) | collective-permute-done | bytes 524320 | tf_op jit(solution)/shard_map/ppermute | solution.py:23
  141.3 0.8 slice_add_fusion
  142.1 3.5 %all-to-all-start.1 = ((f32[4,256,128]{2,1,0:T(8,128)}), f32[4,256,128]{2,1,0:T(8,128)S(1)}, u32[]{:S(2)}, u32[]{:S(2)}) async-start(f32[4,256,128]{2,1,0:T(8,128)} %bitcast.14), calls=%async_computation.1 | async-start | bytes 1048576 | tf_op jit(solution)/shard_map/all_to_all | solution.py:243
  145.6 0.0 collective-permute-done.6
  145.7 5.4 %collective-permute-start.7 = (f32[256,128]{1,0:T(8,128)S(1)}, f32[256,128]{1,0:T(8,128)S(1)}, u32[]{:S(2)}, u32[]{:S(2)}) collective-permute-start(f32[256,128]{1,0:T(8,128)S(1)} %slice.55), channel_id=1, source_target_pairs={{0,16},{16,0},{1,17},{17,1},{2,18},{18,2},{3,19},{19,3},{4,20},{20... | collective-permute-start | bytes 393224 | tf_op jit(solution)/shard_map/ppermute | solution.py:23
  151.0 2.9 %collective-permute-done.7 = f32[256,128]{1,0:T(8,128)S(1)} collective-permute-done((f32[256,128]{1,0:T(8,128)S(1)}, f32[256,128]{1,0:T(8,128)S(1)}, u32[]{:S(2)}, u32[]{:S(2)}) %collective-permute-start.7) | collective-permute-done | bytes 131104 | tf_op jit(solution)/shard_map/ppermute | solution.py:23
  154.0 0.8 all-to-all-done.1
  154.9 22.4 %all_to_all.15 = f32[16,16,256]{2,1,0:T(8,128)S(1)} all-to-all(f32[16,16,256]{2,1,0:T(8,128)S(1)} %bitcast.38), channel_id=1, replica_groups=mesh['y'=4,'zp'=4,'zi'=2,'core'=2,'zh'=2,'x'=4] {'zp','x'}, dimensions={0} | all-to-all | bytes 524288 | tf_op jit(solution)/shard_map/all_to_all | solution.py:245
  177.3 0.6 multiply_bitcast_fusion
  (13 shorter events, 0.2 us)
Async XLA Ops:
  0.0 8.0 %copy-start = (s32[1,16,2]{1,2,0:T(2,128)S(1)}, s32[1,16,2]{1,2,0:T(2,128)}, u32[]{:S(2)}) copy-start(s32[1,16,2]{1,2,0:T(2,128)} %param.5) | copy-start | bytes 388
  2.8 86.9 %collective-permute-start = (bf16[4,64,512]{2,1,0:T(8,128)(2,1)S(1)}, bf16[4,64,512]{2,1,0:T(8,128)(2,1)S(1)}, u32[]{:S(2)}, u32[]{:S(2)}) collective-permute-start(bf16[4,64,512]{2,1,0:T(8,128)(2,1)S(1)} %get-tuple-element.31), channel_id=1, source_target_pairs={{0,4},{1,5},{2,6},{3,7},{8,12},{9,13},{10,14},{11,15},{16,20},{17,... | collective-permute-start | bytes 786440 | tf_op jit(solution)/shard_map/ppermute | solution.py:216
  4.1 85.6 %collective-permute-start.1 = (bf16[4,64,512]{2,1,0:T(8,128)(2,1)S(1)}, bf16[4,64,512]{2,1,0:T(8,128)(2,1)S(1)}, u32[]{:S(2)}, u32[]{:S(2)}) collective-permute-start(bf16[4,64,512]{2,1,0:T(8,128)(2,1)S(1)} %get-tuple-element.32), channel_id=1, source_target_pairs={{0,5},{1,4},{2,7},{3,6},{8,13},{9,12},{10,15},{11,14},{16,21},{17,... | collective-permute-start | bytes 786440 | tf_op jit(solution)/shard_map/ppermute | solution.py:216
  5.4 84.4 %collective-permute-start.2 = (bf16[4,64,512]{2,1,0:T(8,128)(2,1)S(1)}, bf16[4,64,512]{2,1,0:T(8,128)(2,1)S(1)}, u32[]{:S(2)}, u32[]{:S(2)}) collective-permute-start(bf16[4,64,512]{2,1,0:T(8,128)(2,1)S(1)} %get-tuple-element.33), channel_id=1, source_target_pairs={{0,6},{1,7},{2,4},{3,5},{8,14},{9,15},{10,12},{11,13},{16,22},{17,... | collective-permute-start | bytes 786440 | tf_op jit(solution)/shard_map/ppermute | solution.py:216
  6.7 83.1 %collective-permute-start.3 = (bf16[4,64,512]{2,1,0:T(8,128)(2,1)S(1)}, bf16[4,64,512]{2,1,0:T(8,128)(2,1)S(1)}, u32[]{:S(2)}, u32[]{:S(2)}) collective-permute-start(bf16[4,64,512]{2,1,0:T(8,128)(2,1)S(1)} %get-tuple-element.34), channel_id=1, source_target_pairs={{0,7},{1,6},{2,5},{3,4},{8,15},{9,14},{10,13},{11,12},{16,23},{17,... | collective-permute-start | bytes 786440 | tf_op jit(solution)/shard_map/ppermute | solution.py:216
  93.3 4.6 %collective-permute-start.4 = (f32[2048,128]{1,0:T(8,128)S(1)}, f32[2048,128]{1,0:T(8,128)S(1)}, u32[]{:S(2)}, u32[]{:S(2)}) collective-permute-start(f32[2048,128]{1,0:T(8,128)S(1)} %get-tuple-element.40), channel_id=1, source_target_pairs={{0,8},{8,0},{1,9},{9,1},{2,10},{10,2},{3,11},{11,3},{4,12},{12,4},... | collective-permute-start | bytes 3145736 | tf_op jit(solution)/shard_map/ppermute | solution.py:23
  95.2 7.7 %collective-permute-start.8 = (f32[2048,128]{1,0:T(8,128)S(1)}, f32[2048,128]{1,0:T(8,128)S(1)}, u32[]{:S(2)}, u32[]{:S(2)}) collective-permute-start(f32[2048,128]{1,0:T(8,128)S(1)} %get-tuple-element.42), channel_id=1, source_target_pairs={{0,8},{8,0},{1,9},{9,1},{2,10},{10,2},{3,11},{11,3},{4,12},{12,4},... | collective-permute-start | bytes 3145736 | tf_op jit(solution)/shard_map/ppermute | solution.py:23
  98.0 31.4 %collective-permute-start.5 = (f32[1024,128]{1,0:T(8,128)S(1)}, f32[1024,128]{1,0:T(8,128)S(1)}, u32[]{:S(2)}, u32[]{:S(2)}) collective-permute-start(f32[1024,128]{1,0:T(8,128)S(1)} %slice.51), channel_id=1, source_target_pairs={{0,384},{128,256},{256,128},{384,0},{1,385},{129,257},{257,129},{3... | collective-permute-start | bytes 1572872 | tf_op jit(solution)/shard_map/ppermute | solution.py:23
  103.1 38.2 %collective-permute-start.9 = (f32[1024,128]{1,0:T(8,128)S(1)}, f32[1024,128]{1,0:T(8,128)S(1)}, u32[]{:S(2)}, u32[]{:S(2)}) collective-permute-start(f32[1024,128]{1,0:T(8,128)S(1)} %slice.57), channel_id=1, source_target_pairs={{0,16},{16,0},{1,17},{17,1},{2,18},{18,2},{3,19},{19,3},{4,20},{20... | collective-permute-start | bytes 1572872 | tf_op jit(solution)/shard_map/ppermute | solution.py:23
  129.5 16.2 %collective-permute-start.6 = (f32[512,128]{1,0:T(8,128)S(1)}, f32[512,128]{1,0:T(8,128)S(1)}, u32[]{:S(2)}, u32[]{:S(2)}) collective-permute-start(f32[512,128]{1,0:T(8,128)S(1)} %slice.53), channel_id=1, source_target_pairs={{0,128},{128,0},{256,384},{384,256},{1,129},{129,1},{257,385},{385... | collective-permute-start | bytes 786440 | tf_op jit(solution)/shard_map/ppermute | solution.py:23
  142.1 12.7 %all-to-all-start.1 = ((f32[4,256,128]{2,1,0:T(8,128)}), f32[4,256,128]{2,1,0:T(8,128)S(1)}, u32[]{:S(2)}, u32[]{:S(2)}) async-start(f32[4,256,128]{2,1,0:T(8,128)} %bitcast.14), calls=%async_computation.1 | async-start | bytes 1048576 | tf_op jit(solution)/shard_map/all_to_all | solution.py:243
  145.7 8.3 %collective-permute-start.7 = (f32[256,128]{1,0:T(8,128)S(1)}, f32[256,128]{1,0:T(8,128)S(1)}, u32[]{:S(2)}, u32[]{:S(2)}) collective-permute-start(f32[256,128]{1,0:T(8,128)S(1)} %slice.55), channel_id=1, source_target_pairs={{0,16},{16,0},{1,17},{17,1},{2,18},{18,2},{3,19},{19,3},{4,20},{20... | collective-permute-start | bytes 393224 | tf_op jit(solution)/shard_map/ppermute | solution.py:23

commit v8 on v7

--- a/solution.py
+++ b/solution.py
@@ -71,7 +71,7 @@
     group = e ^ (e >> 1)
     for half in range(2):
         side = half ^ zi
-        starts = (group * 2 + side, side * 4 + k // 4)
+        starts = ((group >> 1) * 4 + side * 2 + (group & 1), side * 4 + k // 4)
         for cut in range(CUTS):
             at = ((starts[cut] * NP + lax.rem(k, 4)) * NX + n // 16) * 16
             at = pl.ds(pl.multiple_of(at, 16), 16)
@@ -238,7 +238,7 @@
     halves = late(meta, lists, cols, low, halves, slots)
     scale = 2.0 / (tokens * NY * NZ * NC)
     left, right = (keep + swap(send, "core", 1) for keep, send in zip(halves[:CUTS], halves[CUTS:]))
-    left = total(left, (("y", 3), ("y", 1), ("zi", 1)))
+    left = total(left, (("y", 3), ("zi", 1), ("y", 1)))
     right = total(right, (("zi", 1),)).reshape(NY, -1, right.shape[1])
     right = jnp.sum(lax.all_to_all(right, "y", 0, 0, tiled=True), axis=0)
     parts = jnp.concatenate([left, right], axis=1).reshape(NP * NX, -1, width)

time: 178 us -> 179 us (level)
  starting transfers between devices: 51.6 us -> 59.6 us
  waiting for transfers between devices: 13.7 us -> 7.1 us
    ppermute x6, starting transfers between devices: 42.9 us -> 50.3 us  [swap(): return lax.ppermute(v, axis, [(i, i ^ e) for i in range(SIZES[axis])])]
    ppermute x6, waiting for transfers between devices: 12.9 us -> 7.01 us  [swap(): return lax.ppermute(v, axis, [(i, i ^ e) for i in range(SIZES[axis])])]
where the time goes in v8:
time: 179 us; the launch traced here: 178 us
  blocking collectives  88.6 us (49%)
  starting transfers between devices  59.6 us (33%)
  Pallas kernels  16.8 us (9%)
  waiting for transfers between devices  7.1 us (4%)
  other arithmetic  2.69 us (2%)
  local copies, waits for them, and re-layouts  2.53 us (1%)
    all_to_all x1, blocking collectives, exchange(): lax.all_to_all(jnp.broadcast_to(load, (NX, *load.shape)), 'x', 0, 0, tile...  67 us
    ppermute x6, starting transfers between devices, swap(): return lax.ppermute(v, axis, [(i, i ^ e) for i in range(SIZES[axis])])  50.3 us
    all_to_all x1, blocking collectives, body(): lax.all_to_all(parts, ('zp', 'x'), 0, 0, tiled=True).reshape(NP, -1, width)  21.6 us
    pallas_call x1, Pallas kernels, early(): pl.pallas_call(functools.partial(early_kernel, slots), out_shape=[half] *...  12.6 us
    ppermute x6, waiting for transfers between devices, swap(): return lax.ppermute(v, axis, [(i, i ^ e) for i in range(SIZES[axis])])  7.01 us
    ppermute x4, starting transfers between devices, body(): lax.ppermute(piece, ('zh', 'x'), [(i, NX + (i ^ e)) for i in range(NX)])  5.17 us
    all_to_all x1, starting transfers between devices, body(): right = jnp.sum(lax.all_to_all(right, 'y', 0, 0, tiled=True), axis=0)  4.21 us
  transfers between devices with their start and end apart: 11, of which 4 were waited for; matrix products, arithmetic and copies ran while one was open for 2% of the time, Pallas kernels for 7%

profile of v8, /device:TPU:256, one launch (start us, length us, event | category | flops | bytes accessed | tf_op | source)
XLA Modules:
  0.0 178.4 jit_solution(12563976173565957046)
XLA Ops:
  0.0 0.0 copy-start
  0.0 1.4 copy.18
  1.4 1.4 shard_map.29
  2.8 1.3 collective-permute-start
  4.1 1.3 collective-permute-start.1
  5.4 1.3 collective-permute-start.2
  6.7 1.3 collective-permute-start.3
  8.0 0.0 copy-done
  8.0 0.5 slice.37
  9.1 67.5 %conditional.1 = (bf16[4,2064,256]{2,1,0:T(8,128)(2,1)}) conditional(s32[]{:T(128)} %bitcast.7, () %tuple.11, (bf16[4,512,256]{2,1,0:T(8,128)(2,1)S(1)}, s32[1,16,2]{1,2,0:T(2,128)S(1)}) %tuple.18), branch_computations={%region_0.0_spmd, %region_1.2_spmd} | conditional | flops 3170336 | bytes 15843720 | solution.py:220
  9.2 0.1 copy.13
  9.3 0.1 fusion.1
  9.3 0.3 broadcast_in_dim.7
  9.6 67.0 %all_to_all.14 = bf16[4,2064,256]{2,1,0:T(8,128)(2,1)} all-to-all(bf16[4,2064,256]{2,1,0:T(8,128)(2,1)S(1)} %broadcast_in_dim.7), channel_id=1, replica_groups=mesh['y'=4,'zp'=4,'zi'=2,'core'=2,'zh'=2,'x'=4] {'x'}, dimensions={0} | all-to-all | bytes 8454144 | tf_op jit(solution)/shard_map/cond/branch_1_fun/all_to_all | solution.py:61
  76.6 0.7 slice_convert_fusion
  77.3 0.1 copy.17
  77.5 0.1 concatenate.9.meta
  77.6 12.6 %shard_map.28 = (f32[2048,128]{1,0:T(8,128)S(1)}, f32[2048,128]{1,0:T(8,128)S(1)}, f32[2048,128]{1,0:T(8,128)S(1)}, f32[2048,128]{1,0:T(8,128)S(1)}, bf16[16,512,256]{2,1,0:T(8,128)(2,1)S(1)}, /*index=5*/s32[272]{0:T(512)S(1)}) custom-call(s32[200]{0:T(256)S(1)} %concatenate.9.meta, bf16[4,2064,256]{2,1,0:T(8,128)(2,1)} %get-tuple-element.47.source), custom_call_target="tpu_custom_call" | custom-call | tf_op jit(solution)/shard_map/pallas_call | solution.py:174
  90.1 0.0 collective-permute-done.refs_0_
  90.1 0.0 collective-permute-done.1.refs_1_
  90.1 0.0 collective-permute-done.2.refs_2_
  90.2 0.0 collective-permute-done.3.refs_3_
  90.2 2.9 %shard_map.30 = (f32[2048,128]{1,0:T(8,128)S(1)}, f32[2048,128]{1,0:T(8,128)S(1)}, f32[2048,128]{1,0:T(8,128)S(1)}, f32[2048,128]{1,0:T(8,128)S(1)}) custom-call(s32[200]{0:T(256)S(1)} %concatenate.9.meta, s32[272]{0:T(512)S(1)} %get-tuple-element.29.lists, ...), custom_call_target="tpu_custom_call", output_to_operand_aliasing={{0}: (7, {}), {1}: (8, {}), {2}: (9, {}), {3}: (10, {})} | custom-call | tf_op jit(solution)/shard_map/pallas_call | solution.py:194
  93.1 1.9 %collective-permute-start.4 = (f32[2048,128]{1,0:T(8,128)S(1)}, f32[2048,128]{1,0:T(8,128)S(1)}, u32[]{:S(2)}, u32[]{:S(2)}) collective-permute-start(f32[2048,128]{1,0:T(8,128)S(1)} %get-tuple-element.40), channel_id=1, source_target_pairs={{0,8},{8,0},{1,9},{9,1},{2,10},{10,2},{3,11},{11,3},{4,12},{12,4},... | collective-permute-start | bytes 3145736 | tf_op jit(solution)/shard_map/ppermute | solution.py:23
  95.0 2.4 %collective-permute-start.8 = (f32[2048,128]{1,0:T(8,128)S(1)}, f32[2048,128]{1,0:T(8,128)S(1)}, u32[]{:S(2)}, u32[]{:S(2)}) collective-permute-start(f32[2048,128]{1,0:T(8,128)S(1)} %get-tuple-element.42), channel_id=1, source_target_pairs={{0,8},{8,0},{1,9},{9,1},{2,10},{10,2},{3,11},{11,3},{4,12},{12,4},... | collective-permute-start | bytes 3145736 | tf_op jit(solution)/shard_map/ppermute | solution.py:23
  97.4 0.2 collective-permute-done.4
  97.6 0.1 add.45
  97.8 4.9 %collective-permute-start.5 = (f32[1024,128]{1,0:T(8,128)S(1)}, f32[1024,128]{1,0:T(8,128)S(1)}, u32[]{:S(2)}, u32[]{:S(2)}) collective-permute-start(f32[1024,128]{1,0:T(8,128)S(1)} %slice.51), channel_id=1, source_target_pairs={{0,384},{128,256},{256,128},{384,0},{1,385},{129,257},{257,129},{3... | collective-permute-start | bytes 1572872 | tf_op jit(solution)/shard_map/ppermute | solution.py:23
  102.7 0.0 collective-permute-done.8
  102.7 0.1 add.49
  102.9 25.9 %collective-permute-start.9 = (f32[1024,128]{1,0:T(8,128)S(1)}, f32[1024,128]{1,0:T(8,128)S(1)}, u32[]{:S(2)}, u32[]{:S(2)}) collective-permute-start(f32[1024,128]{1,0:T(8,128)S(1)} %slice.57), channel_id=1, source_target_pairs={{0,16},{16,0},{1,17},{17,1},{2,18},{18,2},{3,19},{19,3},{4,20},{20... | collective-permute-start | bytes 1572872 | tf_op jit(solution)/shard_map/ppermute | solution.py:23
  128.8 0.0 collective-permute-done.5
  128.8 0.1 slice_add_fusion.1
  128.9 12.0 %collective-permute-start.6 = (f32[512,128]{1,0:T(8,128)S(1)}, f32[512,128]{1,0:T(8,128)S(1)}, u32[]{:S(2)}, u32[]{:S(2)}) collective-permute-start(f32[512,128]{1,0:T(8,128)S(1)} %slice.53), channel_id=1, source_target_pairs={{0,16},{16,0},{1,17},{17,1},{2,18},{18,2},{3,19},{19,3},{4,20},{20... | collective-permute-start | bytes 786440 | tf_op jit(solution)/shard_map/ppermute | solution.py:23
  140.9 0.0 collective-permute-done.9
  140.9 0.8 slice_add_fusion
  141.7 4.2 %all-to-all-start.1 = ((f32[4,256,128]{2,1,0:T(8,128)}), f32[4,256,128]{2,1,0:T(8,128)S(1)}, u32[]{:S(2)}, u32[]{:S(2)}) async-start(f32[4,256,128]{2,1,0:T(8,128)} %bitcast.14), calls=%async_computation.1 | async-start | bytes 1048576 | tf_op jit(solution)/shard_map/all_to_all | solution.py:243
  146.0 0.8 collective-permute-done.6
  146.8 3.1 %collective-permute-start.7 = (f32[256,128]{1,0:T(8,128)S(1)}, f32[256,128]{1,0:T(8,128)S(1)}, u32[]{:S(2)}, u32[]{:S(2)}) collective-permute-start(f32[256,128]{1,0:T(8,128)S(1)} %slice.55), channel_id=1, source_target_pairs={{0,128},{128,0},{256,384},{384,256},{1,129},{129,1},{257,385},{385... | collective-permute-start | bytes 393224 | tf_op jit(solution)/shard_map/ppermute | solution.py:23
  150.0 6.0 %collective-permute-done.7 = f32[256,128]{1,0:T(8,128)S(1)} collective-permute-done((f32[256,128]{1,0:T(8,128)S(1)}, f32[256,128]{1,0:T(8,128)S(1)}, u32[]{:S(2)}, u32[]{:S(2)}) %collective-permute-start.7) | collective-permute-done | bytes 131104 | tf_op jit(solution)/shard_map/ppermute | solution.py:23
  156.0 0.1 all-to-all-done.1
  156.1 21.6 %all_to_all.15 = f32[16,16,256]{2,1,0:T(8,128)S(1)} all-to-all(f32[16,16,256]{2,1,0:T(8,128)S(1)} %bitcast.38), channel_id=1, replica_groups=mesh['y'=4,'zp'=4,'zi'=2,'core'=2,'zh'=2,'x'=4] {'zp','x'}, dimensions={0} | all-to-all | bytes 524288 | tf_op jit(solution)/shard_map/all_to_all | solution.py:245
  177.7 0.6 multiply_bitcast_fusion
  (13 shorter events, 0.2 us)
Async XLA Ops:
  0.0 8.0 %copy-start = (s32[1,16,2]{1,2,0:T(2,128)S(1)}, s32[1,16,2]{1,2,0:T(2,128)}, u32[]{:S(2)}) copy-start(s32[1,16,2]{1,2,0:T(2,128)} %param.5) | copy-start | bytes 388
  2.8 87.4 %collective-permute-start = (bf16[4,64,512]{2,1,0:T(8,128)(2,1)S(1)}, bf16[4,64,512]{2,1,0:T(8,128)(2,1)S(1)}, u32[]{:S(2)}, u32[]{:S(2)}) collective-permute-start(bf16[4,64,512]{2,1,0:T(8,128)(2,1)S(1)} %get-tuple-element.31), channel_id=1, source_target_pairs={{0,4},{1,5},{2,6},{3,7},{8,12},{9,13},{10,14},{11,15},{16,20},{17,... | collective-permute-start | bytes 786440 | tf_op jit(solution)/shard_map/ppermute | solution.py:216
  4.1 86.1 %collective-permute-start.1 = (bf16[4,64,512]{2,1,0:T(8,128)(2,1)S(1)}, bf16[4,64,512]{2,1,0:T(8,128)(2,1)S(1)}, u32[]{:S(2)}, u32[]{:S(2)}) collective-permute-start(bf16[4,64,512]{2,1,0:T(8,128)(2,1)S(1)} %get-tuple-element.32), channel_id=1, source_target_pairs={{0,5},{1,4},{2,7},{3,6},{8,13},{9,12},{10,15},{11,14},{16,21},{17,... | collective-permute-start | bytes 786440 | tf_op jit(solution)/shard_map/ppermute | solution.py:216
  5.4 84.8 %collective-permute-start.2 = (bf16[4,64,512]{2,1,0:T(8,128)(2,1)S(1)}, bf16[4,64,512]{2,1,0:T(8,128)(2,1)S(1)}, u32[]{:S(2)}, u32[]{:S(2)}) collective-permute-start(bf16[4,64,512]{2,1,0:T(8,128)(2,1)S(1)} %get-tuple-element.33), channel_id=1, source_target_pairs={{0,6},{1,7},{2,4},{3,5},{8,14},{9,15},{10,12},{11,13},{16,22},{17,... | collective-permute-start | bytes 786440 | tf_op jit(solution)/shard_map/ppermute | solution.py:216
  6.7 83.5 %collective-permute-start.3 = (bf16[4,64,512]{2,1,0:T(8,128)(2,1)S(1)}, bf16[4,64,512]{2,1,0:T(8,128)(2,1)S(1)}, u32[]{:S(2)}, u32[]{:S(2)}) collective-permute-start(bf16[4,64,512]{2,1,0:T(8,128)(2,1)S(1)} %get-tuple-element.34), channel_id=1, source_target_pairs={{0,7},{1,6},{2,5},{3,4},{8,15},{9,14},{10,13},{11,12},{16,23},{17,... | collective-permute-start | bytes 786440 | tf_op jit(solution)/shard_map/ppermute | solution.py:216
  93.1 4.6 %collective-permute-start.4 = (f32[2048,128]{1,0:T(8,128)S(1)}, f32[2048,128]{1,0:T(8,128)S(1)}, u32[]{:S(2)}, u32[]{:S(2)}) collective-permute-start(f32[2048,128]{1,0:T(8,128)S(1)} %get-tuple-element.40), channel_id=1, source_target_pairs={{0,8},{8,0},{1,9},{9,1},{2,10},{10,2},{3,11},{11,3},{4,12},{12,4},... | collective-permute-start | bytes 3145736 | tf_op jit(solution)/shard_map/ppermute | solution.py:23
  95.0 7.7 %collective-permute-start.8 = (f32[2048,128]{1,0:T(8,128)S(1)}, f32[2048,128]{1,0:T(8,128)S(1)}, u32[]{:S(2)}, u32[]{:S(2)}) collective-permute-start(f32[2048,128]{1,0:T(8,128)S(1)} %get-tuple-element.42), channel_id=1, source_target_pairs={{0,8},{8,0},{1,9},{9,1},{2,10},{10,2},{3,11},{11,3},{4,12},{12,4},... | collective-permute-start | bytes 3145736 | tf_op jit(solution)/shard_map/ppermute | solution.py:23
  97.8 31.0 %collective-permute-start.5 = (f32[1024,128]{1,0:T(8,128)S(1)}, f32[1024,128]{1,0:T(8,128)S(1)}, u32[]{:S(2)}, u32[]{:S(2)}) collective-permute-start(f32[1024,128]{1,0:T(8,128)S(1)} %slice.51), channel_id=1, source_target_pairs={{0,384},{128,256},{256,128},{384,0},{1,385},{129,257},{257,129},{3... | collective-permute-start | bytes 1572872 | tf_op jit(solution)/shard_map/ppermute | solution.py:23
  102.9 38.0 %collective-permute-start.9 = (f32[1024,128]{1,0:T(8,128)S(1)}, f32[1024,128]{1,0:T(8,128)S(1)}, u32[]{:S(2)}, u32[]{:S(2)}) collective-permute-start(f32[1024,128]{1,0:T(8,128)S(1)} %slice.57), channel_id=1, source_target_pairs={{0,16},{16,0},{1,17},{17,1},{2,18},{18,2},{3,19},{19,3},{4,20},{20... | collective-permute-start | bytes 1572872 | tf_op jit(solution)/shard_map/ppermute | solution.py:23
  128.9 17.9 %collective-permute-start.6 = (f32[512,128]{1,0:T(8,128)S(1)}, f32[512,128]{1,0:T(8,128)S(1)}, u32[]{:S(2)}, u32[]{:S(2)}) collective-permute-start(f32[512,128]{1,0:T(8,128)S(1)} %slice.53), channel_id=1, source_target_pairs={{0,16},{16,0},{1,17},{17,1},{2,18},{18,2},{3,19},{19,3},{4,20},{20... | collective-permute-start | bytes 786440 | tf_op jit(solution)/shard_map/ppermute | solution.py:23
  141.7 14.3 %all-to-all-start.1 = ((f32[4,256,128]{2,1,0:T(8,128)}), f32[4,256,128]{2,1,0:T(8,128)S(1)}, u32[]{:S(2)}, u32[]{:S(2)}) async-start(f32[4,256,128]{2,1,0:T(8,128)} %bitcast.14), calls=%async_computation.1 | async-start | bytes 1048576 | tf_op jit(solution)/shard_map/all_to_all | solution.py:243
  146.8 9.1 %collective-permute-start.7 = (f32[256,128]{1,0:T(8,128)S(1)}, f32[256,128]{1,0:T(8,128)S(1)}, u32[]{:S(2)}, u32[]{:S(2)}) collective-permute-start(f32[256,128]{1,0:T(8,128)S(1)} %slice.55), channel_id=1, source_target_pairs={{0,128},{128,0},{256,384},{384,256},{1,129},{129,1},{257,385},{385... | collective-permute-start | bytes 393224 | tf_op jit(solution)/shard_map/ppermute | solution.py:23

commit v9 on v7

--- a/solution.py
+++ b/solution.py
@@ -36,20 +36,20 @@
     ).astype(jnp.bfloat16)
 
 
-def quarters_kernel(meta, own, *outs):
-    for d in range(NX):
+def quarters_kernel(places, meta, own, *outs):
+    for d, out in zip(places, outs):
         picker = quarter_picker(meta[0] ^ d, own.shape[2])
         for b in range(own.shape[0]):
-            outs[d][b] = pick(picker, own[b])
-
-
-def quarters(x, own):
+            out[b] = pick(picker, own[b])
+
+
+def quarters(x, own, places):
     blocks, tokens, width = own.shape
     return pl.pallas_call(
-        quarters_kernel,
-        out_shape=[jax.ShapeDtypeStruct((blocks, QUARTER, tokens), jnp.bfloat16)] * NX,
+        functools.partial(quarters_kernel, places),
+        out_shape=[jax.ShapeDtypeStruct((blocks, QUARTER, tokens), jnp.bfloat16)] * len(places),
         in_specs=[SMEM, VMEM],
-        out_specs=[VMEM] * NX,
+        out_specs=[VMEM] * len(places),
         compiler_params=pltpu.CompilerParams(vmem_limit_bytes=16 << 20),
     )(x[None].astype(jnp.int32), own)
 
@@ -211,7 +211,7 @@
     zh, x = lax.axis_index("zh"), lax.axis_index("x")
 
     own = jnp.transpose(activations, (1, 0, 2))
-    pieces = quarters(x, own)
+    pieces = [*quarters(x, own, (0,)), *quarters(x, own, (1, 2, 3))]
     low = [
         lax.ppermute(piece, ("zh", "x"), [(i, NX + (i ^ e)) for i in range(NX)])
         for e, piece in enumerate(pieces)

time: 178 us -> 177 us (level)
  no operation moved by 1% of the time
where the time goes in v9:
time: 177 us
  blocking collectives  89.4 us (51%)
  starting transfers between devices  51.2 us (29%)
  Pallas kernels  16.4 us (9%)
  waiting for transfers between devices  13.8 us (8%)
  other arithmetic  2.69 us (2%)
  local copies, waits for them, and re-layouts  2.53 us (1%)
    all_to_all x1, blocking collectives, exchange(): lax.all_to_all(jnp.broadcast_to(load, (NX, *load.shape)), 'x', 0, 0, tile...  66.8 us
    ppermute x6, starting transfers between devices, swap(): return lax.ppermute(v, axis, [(i, i ^ e) for i in range(SIZES[axis])])  42.6 us
    all_to_all x1, blocking collectives, body(): lax.all_to_all(parts, ('zp', 'x'), 0, 0, tiled=True).reshape(NP, -1, width)  22.6 us
    ppermute x6, waiting for transfers between devices, swap(): return lax.ppermute(v, axis, [(i, i ^ e) for i in range(SIZES[axis])])  12.9 us
    pallas_call x1, Pallas kernels, early(): pl.pallas_call(functools.partial(early_kernel, slots), out_shape=[half] *...  11.3 us
    ppermute x4, starting transfers between devices, body(): lax.ppermute(piece, ('zh', 'x'), [(i, NX + (i ^ e)) for i in range(NX)])  5.17 us
  transfers between devices with their start and end apart: 11, of which 4 were waited for; matrix products, arithmetic and copies ran while one was open for 2% of the time, Pallas kernels for 7%

profile of v9, /device:TPU:256, one launch (start us, length us, event | category | flops | bytes accessed | tf_op | source)
XLA Modules:
  0.0 176.9 jit_solution(3230355671621265620)
XLA Ops:
  0.0 0.0 copy-start
  0.0 1.4 copy.18
  1.4 0.4 shard_map.29
  1.8 1.3 collective-permute-start
  3.1 1.1 shard_map.30
  4.2 1.3 collective-permute-start.1
  5.5 1.3 collective-permute-start.2
  6.8 1.3 collective-permute-start.3
  8.1 0.0 copy-done
  8.1 0.5 slice.37
  9.3 67.3 %conditional.1 = (bf16[4,2064,256]{2,1,0:T(8,128)(2,1)}) conditional(s32[]{:T(128)} %bitcast.7, () %tuple.11, (bf16[4,512,256]{2,1,0:T(8,128)(2,1)S(1)}, s32[1,16,2]{1,2,0:T(2,128)S(1)}) %tuple.18), branch_computations={%region_0.0_spmd, %region_1.2_spmd} | conditional | flops 3170336 | bytes 15843720 | solution.py:220
  9.3 0.1 copy.13
  9.4 0.1 fusion.1
  9.5 0.3 broadcast_in_dim.5
  9.7 66.8 %all_to_all.14 = bf16[4,2064,256]{2,1,0:T(8,128)(2,1)} all-to-all(bf16[4,2064,256]{2,1,0:T(8,128)(2,1)S(1)} %broadcast_in_dim.5), channel_id=1, replica_groups=mesh['y'=4,'zp'=4,'zi'=2,'core'=2,'zh'=2,'x'=4] {'x'}, dimensions={0} | all-to-all | bytes 8454144 | tf_op jit(solution)/shard_map/cond/branch_1_fun/all_to_all | solution.py:61
  76.6 0.7 slice_convert_fusion
  77.3 0.1 copy.17
  77.4 0.1 concatenate.9.meta
  77.5 11.3 %shard_map.28 = (f32[2048,128]{1,0:T(8,128)S(1)}, f32[2048,128]{1,0:T(8,128)S(1)}, f32[2048,128]{1,0:T(8,128)S(1)}, f32[2048,128]{1,0:T(8,128)S(1)}, bf16[16,512,256]{2,1,0:T(8,128)(2,1)S(1)}, /*index=5*/s32[272]{0:T(512)S(1)}) custom-call(s32[200]{0:T(256)S(1)} %concatenate.9.meta, bf16[4,2064,256]{2,1,0:T(8,128)(2,1)} %get-tuple-element.45.source), custom_call_target="tpu_custom_call" | custom-call | tf_op jit(solution)/shard_map/pallas_call | solution.py:174
  88.9 0.0 collective-permute-done.refs_0_
  88.9 0.0 collective-permute-done.1.refs_1_
  88.9 0.0 collective-permute-done.2.refs_2_
  88.9 0.0 collective-permute-done.3.refs_3_
  88.9 3.5 %shard_map.31 = (f32[2048,128]{1,0:T(8,128)S(1)}, f32[2048,128]{1,0:T(8,128)S(1)}, f32[2048,128]{1,0:T(8,128)S(1)}, f32[2048,128]{1,0:T(8,128)S(1)}) custom-call(s32[200]{0:T(256)S(1)} %concatenate.9.meta, s32[272]{0:T(512)S(1)} %get-tuple-element.28.lists, ...), custom_call_target="tpu_custom_call", output_to_operand_aliasing={{0}: (7, {}), {1}: (8, {}), {2}: (9, {}), {3}: (10, {})} | custom-call | tf_op jit(solution)/shard_map/pallas_call | solution.py:194
  92.4 1.9 %collective-permute-start.4 = (f32[2048,128]{1,0:T(8,128)S(1)}, f32[2048,128]{1,0:T(8,128)S(1)}, u32[]{:S(2)}, u32[]{:S(2)}) collective-permute-start(f32[2048,128]{1,0:T(8,128)S(1)} %get-tuple-element.38), channel_id=1, source_target_pairs={{0,8},{8,0},{1,9},{9,1},{2,10},{10,2},{3,11},{11,3},{4,12},{12,4},... | collective-permute-start | bytes 3145736 | tf_op jit(solution)/shard_map/ppermute | solution.py:23
  94.4 2.4 %collective-permute-start.8 = (f32[2048,128]{1,0:T(8,128)S(1)}, f32[2048,128]{1,0:T(8,128)S(1)}, u32[]{:S(2)}, u32[]{:S(2)}) collective-permute-start(f32[2048,128]{1,0:T(8,128)S(1)} %get-tuple-element.40), channel_id=1, source_target_pairs={{0,8},{8,0},{1,9},{9,1},{2,10},{10,2},{3,11},{11,3},{4,12},{12,4},... | collective-permute-start | bytes 3145736 | tf_op jit(solution)/shard_map/ppermute | solution.py:23
  96.8 0.2 collective-permute-done.4
  97.0 0.1 add.45
  97.1 4.9 %collective-permute-start.5 = (f32[1024,128]{1,0:T(8,128)S(1)}, f32[1024,128]{1,0:T(8,128)S(1)}, u32[]{:S(2)}, u32[]{:S(2)}) collective-permute-start(f32[1024,128]{1,0:T(8,128)S(1)} %slice.51), channel_id=1, source_target_pairs={{0,384},{128,256},{256,128},{384,0},{1,385},{129,257},{257,129},{3... | collective-permute-start | bytes 1572872 | tf_op jit(solution)/shard_map/ppermute | solution.py:23
  102.1 0.0 collective-permute-done.8
  102.1 0.1 add.49
  102.2 26.0 %collective-permute-start.9 = (f32[1024,128]{1,0:T(8,128)S(1)}, f32[1024,128]{1,0:T(8,128)S(1)}, u32[]{:S(2)}, u32[]{:S(2)}) collective-permute-start(f32[1024,128]{1,0:T(8,128)S(1)} %slice.57), channel_id=1, source_target_pairs={{0,16},{16,0},{1,17},{17,1},{2,18},{18,2},{3,19},{19,3},{4,20},{20... | collective-permute-start | bytes 1572872 | tf_op jit(solution)/shard_map/ppermute | solution.py:23
  128.2 0.0 collective-permute-done.5
  128.2 0.1 slice_add_fusion.1
  128.3 2.0 %collective-permute-start.6 = (f32[512,128]{1,0:T(8,128)S(1)}, f32[512,128]{1,0:T(8,128)S(1)}, u32[]{:S(2)}, u32[]{:S(2)}) collective-permute-start(f32[512,128]{1,0:T(8,128)S(1)} %slice.53), channel_id=1, source_target_pairs={{0,128},{128,0},{256,384},{384,256},{1,129},{129,1},{257,385},{385... | collective-permute-start | bytes 786440 | tf_op jit(solution)/shard_map/ppermute | solution.py:23
  130.4 9.8 %collective-permute-done.9 = f32[1024,128]{1,0:T(8,128)S(1)} collective-permute-done((f32[1024,128]{1,0:T(8,128)S(1)}, f32[1024,128]{1,0:T(8,128)S(1)}, u32[]{:S(2)}, u32[]{:S(2)}) %collective-permute-start.9) | collective-permute-done | bytes 524320 | tf_op jit(solution)/shard_map/ppermute | solution.py:23
  140.1 0.8 slice_add_fusion
  141.0 3.5 %all-to-all-start.1 = ((f32[4,256,128]{2,1,0:T(8,128)}), f32[4,256,128]{2,1,0:T(8,128)S(1)}, u32[]{:S(2)}, u32[]{:S(2)}) async-start(f32[4,256,128]{2,1,0:T(8,128)} %bitcast.14), calls=%async_computation.1 | async-start | bytes 1048576 | tf_op jit(solution)/shard_map/all_to_all | solution.py:243
  144.5 0.0 collective-permute-done.6
  144.5 5.3 %collective-permute-start.7 = (f32[256,128]{1,0:T(8,128)S(1)}, f32[256,128]{1,0:T(8,128)S(1)}, u32[]{:S(2)}, u32[]{:S(2)}) collective-permute-start(f32[256,128]{1,0:T(8,128)S(1)} %slice.55), channel_id=1, source_target_pairs={{0,16},{16,0},{1,17},{17,1},{2,18},{18,2},{3,19},{19,3},{4,20},{20... | collective-permute-start | bytes 393224 | tf_op jit(solution)/shard_map/ppermute | solution.py:23
  149.9 2.9 %collective-permute-done.7 = f32[256,128]{1,0:T(8,128)S(1)} collective-permute-done((f32[256,128]{1,0:T(8,128)S(1)}, f32[256,128]{1,0:T(8,128)S(1)}, u32[]{:S(2)}, u32[]{:S(2)}) %collective-permute-start.7) | collective-permute-done | bytes 131104 | tf_op jit(solution)/shard_map/ppermute | solution.py:23
  152.8 0.8 all-to-all-done.1
  153.7 22.6 %all_to_all.15 = f32[16,16,256]{2,1,0:T(8,128)S(1)} all-to-all(f32[16,16,256]{2,1,0:T(8,128)S(1)} %bitcast.39), channel_id=1, replica_groups=mesh['y'=4,'zp'=4,'zi'=2,'core'=2,'zh'=2,'x'=4] {'zp','x'}, dimensions={0} | all-to-all | bytes 524288 | tf_op jit(solution)/shard_map/all_to_all | solution.py:245
  176.3 0.6 multiply_bitcast_fusion
  (13 shorter events, 0.2 us)
Async XLA Ops:
  0.0 8.1 %copy-start = (s32[1,16,2]{1,2,0:T(2,128)S(1)}, s32[1,16,2]{1,2,0:T(2,128)}, u32[]{:S(2)}) copy-start(s32[1,16,2]{1,2,0:T(2,128)} %param.5) | copy-start | bytes 388
  1.8 87.1 %collective-permute-start = (bf16[4,64,512]{2,1,0:T(8,128)(2,1)S(1)}, bf16[4,64,512]{2,1,0:T(8,128)(2,1)S(1)}, u32[]{:S(2)}, u32[]{:S(2)}) collective-permute-start(bf16[4,64,512]{2,1,0:T(8,128)(2,1)S(1)} %shard_map.29), channel_id=1, source_target_pairs={{0,4},{1,5},{2,6},{3,7},{8,12},{9,13},{10,14},{11,15},{16,20},{17,... | collective-permute-start | bytes 786440 | tf_op jit(solution)/shard_map/ppermute | solution.py:216
  4.2 84.7 %collective-permute-start.1 = (bf16[4,64,512]{2,1,0:T(8,128)(2,1)S(1)}, bf16[4,64,512]{2,1,0:T(8,128)(2,1)S(1)}, u32[]{:S(2)}, u32[]{:S(2)}) collective-permute-start(bf16[4,64,512]{2,1,0:T(8,128)(2,1)S(1)} %get-tuple-element.30), channel_id=1, source_target_pairs={{0,5},{1,4},{2,7},{3,6},{8,13},{9,12},{10,15},{11,14},{16,21},{17,... | collective-permute-start | bytes 786440 | tf_op jit(solution)/shard_map/ppermute | solution.py:216
  5.5 83.4 %collective-permute-start.2 = (bf16[4,64,512]{2,1,0:T(8,128)(2,1)S(1)}, bf16[4,64,512]{2,1,0:T(8,128)(2,1)S(1)}, u32[]{:S(2)}, u32[]{:S(2)}) collective-permute-start(bf16[4,64,512]{2,1,0:T(8,128)(2,1)S(1)} %get-tuple-element.31), channel_id=1, source_target_pairs={{0,6},{1,7},{2,4},{3,5},{8,14},{9,15},{10,12},{11,13},{16,22},{17,... | collective-permute-start | bytes 786440 | tf_op jit(solution)/shard_map/ppermute | solution.py:216
  6.8 82.1 %collective-permute-start.3 = (bf16[4,64,512]{2,1,0:T(8,128)(2,1)S(1)}, bf16[4,64,512]{2,1,0:T(8,128)(2,1)S(1)}, u32[]{:S(2)}, u32[]{:S(2)}) collective-permute-start(bf16[4,64,512]{2,1,0:T(8,128)(2,1)S(1)} %get-tuple-element.32), channel_id=1, source_target_pairs={{0,7},{1,6},{2,5},{3,4},{8,15},{9,14},{10,13},{11,12},{16,23},{17,... | collective-permute-start | bytes 786440 | tf_op jit(solution)/shard_map/ppermute | solution.py:216
  92.4 4.6 %collective-permute-start.4 = (f32[2048,128]{1,0:T(8,128)S(1)}, f32[2048,128]{1,0:T(8,128)S(1)}, u32[]{:S(2)}, u32[]{:S(2)}) collective-permute-start(f32[2048,128]{1,0:T(8,128)S(1)} %get-tuple-element.38), channel_id=1, source_target_pairs={{0,8},{8,0},{1,9},{9,1},{2,10},{10,2},{3,11},{11,3},{4,12},{12,4},... | collective-permute-start | bytes 3145736 | tf_op jit(solution)/shard_map/ppermute | solution.py:23
  94.4 7.7 %collective-permute-start.8 = (f32[2048,128]{1,0:T(8,128)S(1)}, f32[2048,128]{1,0:T(8,128)S(1)}, u32[]{:S(2)}, u32[]{:S(2)}) collective-permute-start(f32[2048,128]{1,0:T(8,128)S(1)} %get-tuple-element.40), channel_id=1, source_target_pairs={{0,8},{8,0},{1,9},{9,1},{2,10},{10,2},{3,11},{11,3},{4,12},{12,4},... | collective-permute-start | bytes 3145736 | tf_op jit(solution)/shard_map/ppermute | solution.py:23
  97.1 31.1 %collective-permute-start.5 = (f32[1024,128]{1,0:T(8,128)S(1)}, f32[1024,128]{1,0:T(8,128)S(1)}, u32[]{:S(2)}, u32[]{:S(2)}) collective-permute-start(f32[1024,128]{1,0:T(8,128)S(1)} %slice.51), channel_id=1, source_target_pairs={{0,384},{128,256},{256,128},{384,0},{1,385},{129,257},{257,129},{3... | collective-permute-start | bytes 1572872 | tf_op jit(solution)/shard_map/ppermute | solution.py:23
  102.2 37.9 %collective-permute-start.9 = (f32[1024,128]{1,0:T(8,128)S(1)}, f32[1024,128]{1,0:T(8,128)S(1)}, u32[]{:S(2)}, u32[]{:S(2)}) collective-permute-start(f32[1024,128]{1,0:T(8,128)S(1)} %slice.57), channel_id=1, source_target_pairs={{0,16},{16,0},{1,17},{17,1},{2,18},{18,2},{3,19},{19,3},{4,20},{20... | collective-permute-start | bytes 1572872 | tf_op jit(solution)/shard_map/ppermute | solution.py:23
  128.3 16.2 %collective-permute-start.6 = (f32[512,128]{1,0:T(8,128)S(1)}, f32[512,128]{1,0:T(8,128)S(1)}, u32[]{:S(2)}, u32[]{:S(2)}) collective-permute-start(f32[512,128]{1,0:T(8,128)S(1)} %slice.53), channel_id=1, source_target_pairs={{0,128},{128,0},{256,384},{384,256},{1,129},{129,1},{257,385},{385... | collective-permute-start | bytes 786440 | tf_op jit(solution)/shard_map/ppermute | solution.py:23
  141.0 12.7 %all-to-all-start.1 = ((f32[4,256,128]{2,1,0:T(8,128)}), f32[4,256,128]{2,1,0:T(8,128)S(1)}, u32[]{:S(2)}, u32[]{:S(2)}) async-start(f32[4,256,128]{2,1,0:T(8,128)} %bitcast.14), calls=%async_computation.1 | async-start | bytes 1048576 | tf_op jit(solution)/shard_map/all_to_all | solution.py:243
  144.5 8.3 %collective-permute-start.7 = (f32[256,128]{1,0:T(8,128)S(1)}, f32[256,128]{1,0:T(8,128)S(1)}, u32[]{:S(2)}, u32[]{:S(2)}) collective-permute-start(f32[256,128]{1,0:T(8,128)S(1)} %slice.55), channel_id=1, source_target_pairs={{0,16},{16,0},{1,17},{17,1},{2,18},{18,2},{3,19},{19,3},{4,20},{20... | collective-permute-start | bytes 393224 | tf_op jit(solution)/shard_map/ppermute | solution.py:23
